TPU v7x, 128 devices: a whole 4x4x4 slice. The times are simulated.
128 devices in a mesh: row: 16 (over z, x), rep: 8 (over y, core).
Axes of the slice: x: 4, y: 4, z: 4, core: 2. Of those that a mesh axis runs over, the one named last changes fastest.
Arguments:
- features: bfloat16 [65536, 256], P(('row', 'rep')), may hold values from -6 to 6
- weight: bfloat16 [256, 256], replicated, may hold values from -0.375 to 0.375
- cotangent: bfloat16 [65536, 256], P(('row', 'rep')), may hold values from -6 to 6
- row_mask: int32 [65536], P(('row', 'rep')), may hold values 0 or 1
- block_rows: int32 [49152], P(('row', 'rep')), may hold values from 0 to 31
- block_cols: int32 [49152], P(('row', 'rep')), may hold values from 0 to 63
- block_values: bfloat16 [49152, 128, 128], P(('row', 'rep')), may hold values from -0.06982422 to 0.06982422
- block_count: int32 [128], P(('row', 'rep')), may hold values from 48 to 384, as said below
Outputs:
- output: bfloat16 [65536, 256], P(('row', 'rep'))
- grad_features: bfloat16 [65536, 256], P(('row', 'rep'))
- grad_weight: float32 [256, 256], replicated
Inputs may be any that keep to these rules, and one draw needn't show every extreme that they name: `block_count`: each device has at least one live slot; in every draw some device has all 384 slots live.
All inputs are finite; a program needn't handle non-finite values. No bound on the sum of `row_mask` on one device may be relied on, other than what follows from the above.
Results may differ from a plain program's by a relative error of at most 0.0061.
Values may be sent and summed in bfloat16 or wider, within the bound.
No kernel may reach another device: no remote copies, remote signals or barrier semaphores. Data moves between devices by JAX's collectives and lax.ppermute only.
A program may use at most 192 MiB of HBM per device.

v0:
```python
import math

import jax
import jax.numpy as jnp
from jax import lax
from jax.sharding import PartitionSpec as P


def select_rows(indices, count, dtype):
    return (indices[:, None] == jnp.arange(count, dtype=jnp.int32)[None, :]).astype(dtype)


def add_into(total, hot, product):
    flat = product.reshape(product.shape[0], -1)
    return total + lax.dot_general(
        hot,
        flat,
        (((0,), (0,)), ((), ())),
        precision=lax.Precision.HIGHEST,
        preferred_element_type=jnp.float32,
    )


def shards(
    features, weight, cotangent, row_mask, block_rows, block_cols, block_values, block_count
):
    rows_dev, width = features.shape
    slot_total = block_rows.shape[0]
    edge = block_values.shape[1]
    n_rep = lax.axis_size("rep")
    n_row = lax.axis_size("row")
    factor = 1.0 / math.sqrt(rows_dev * n_row * n_rep)
    per_turn = math.gcd(slot_total, 128)
    turns = slot_total // per_turn
    live = (jnp.arange(slot_total, dtype=jnp.int32) < block_count[0]).astype(jnp.float32)
    value_turns = block_values.reshape(turns, per_turn, edge, edge)
    target_turns = block_rows.reshape(turns, per_turn)
    source_turns = block_cols.reshape(turns, per_turn)
    live_turns = live.reshape(turns, per_turn)
    group_blocks = n_rep * rows_dev // edge
    line = lax.all_gather(features, "row", axis=0, tiled=True)
    line_count = line.shape[0] // edge
    line_flat = line.reshape(line_count, edge * width)

    def forward_turn(total, item):
        values, targets, sources, weights = item
        picked = jnp.dot(
            select_rows(sources, line_count, jnp.bfloat16),
            line_flat,
            preferred_element_type=jnp.float32,
        ).astype(jnp.bfloat16)
        product = jnp.einsum(
            "kab,kbf->kaf",
            values,
            picked.reshape(-1, edge, width),
            preferred_element_type=jnp.float32,
        )
        hot = select_rows(targets, group_blocks, jnp.float32) * weights[:, None]
        return (add_into(total, hot, product), None)

    partial_value, _ = lax.scan(
        forward_turn,
        jnp.zeros((group_blocks, edge * width), jnp.float32),
        (value_turns, target_turns, source_turns, live_turns),
    )
    partial_value = partial_value.reshape(group_blocks * edge, width)
    summed = lax.psum_scatter(partial_value, "rep", scatter_dimension=0, tiled=True)
    aggregated = summed.astype(jnp.bfloat16)
    pre = jnp.dot(aggregated, weight, preferred_element_type=jnp.float32)
    gate = jax.nn.sigmoid(pre)
    output = (pre * gate).astype(jnp.bfloat16)
    mask = row_mask.astype(jnp.float32)[:, None]
    slope = (cotangent.astype(jnp.float32) * mask * gate * (1.0 + pre * (1.0 - gate))).astype(
        jnp.bfloat16
    )
    weight_term = lax.dot_general(
        aggregated, slope, (((0,), (0,)), ((), ())), preferred_element_type=jnp.float32
    )
    grad_weight = lax.psum(weight_term, ("row", "rep")) * factor
    own_back = jnp.dot(slope, weight.T, preferred_element_type=jnp.float32).astype(jnp.bfloat16)
    group_back = lax.all_gather(own_back, "rep", axis=0, tiled=True)
    back_flat = group_back.reshape(group_blocks, edge * width)

    def backward_turn(total, item):
        values, targets, sources, weights = item
        picked = jnp.dot(
            select_rows(targets, group_blocks, jnp.bfloat16),
            back_flat,
            preferred_element_type=jnp.float32,
        ).astype(jnp.bfloat16)
        product = jnp.einsum(
            "kab,kaf->kbf",
            values,
            picked.reshape(-1, edge, width),
            preferred_element_type=jnp.float32,
        )
        hot = select_rows(sources, line_count, jnp.float32) * weights[:, None]
        return (add_into(total, hot, product), None)

    line_total, _ = lax.scan(
        backward_turn,
        jnp.zeros((line_count, edge * width), jnp.float32),
        (value_turns, target_turns, source_turns, live_turns),
    )
    line_total = line_total.reshape(-1, width)
    line_sum = lax.psum_scatter(line_total, "row", scatter_dimension=0, tiled=True)
    grad_features = line_sum.astype(jnp.bfloat16)
    return (output, grad_features, grad_weight)


def solution(mesh):
    in_specs = (
        P(("row", "rep"), None),
        P(),
        P(("row", "rep"), None),
        P(("row", "rep")),
        P(("row", "rep")),
        P(("row", "rep")),
        P(("row", "rep"), None, None),
        P(("row", "rep")),
    )
    out_specs = (P(("row", "rep"), None), P(("row", "rep"), None), P())
    return jax.shard_map(shards, mesh=mesh, in_specs=in_specs, out_specs=out_specs, check_vma=False)
```

profile of v0, /device:TPU:0, one launch (start us, length us, event | category | flops | bytes accessed | tf_op | source)
XLA Modules:
  0.0 616.4 jit_solution(5595457996585056109)
XLA Ops:
  8.7 55.7 %all-gather.3.cloned.1.call-done = bf16[8192,256]{1,0:T(8,128)(2,1)} async-done(((bf16[512,256]{1,0:T(8,128)(2,1)}), bf16[8192,256]{1,0:T(8,128)(2,1)}) %all-gather.3.cloned.1.call-update) | async-done | bytes 4194320 | tf_op jit(solution)/shard_map/all_gather | solution.py:41
  71.8 181.8 %while.22 = (s32[]{:T(128)}, f32[32,32768]{1,0:T(8,128)}, s32[3,128]{1,0:T(4,128)S(1)}, f32[3,128]{1,0:T(4,128)S(1)}, bf16[3,128,128,128]{3,2,1,0:T(8,128)(2,1)}...) while((s32[]{:T(128)}, f32[32,32768]{1,0:T(8,128)}, ...), condition=%wide.region_1.2_spmd.clone, body=%wide.region_0.1_spmd.clone.sunk | while | flops 3227533312 | bytes 117445744 | solution.py:61
  88.7 12.7 %fusion.63 = f32[128,128,256]{2,1,0:T(8,128)} fusion(bf16[128,128,256]{2,1,0:T(8,128)(2,1)} %bitcast.84, bf16[3,128,128,128]{3,2,1,0:T(8,128)(2,1)} %get-tuple-element.284, s32[]{:T(128)} %get-tuple-element.271), kind=kOutput, calls=%fused_computation.2.clone.1 | convolution fusion | flops 1073741824 | bytes 29360640 | tf_op jit(solution)/shard_map/while/body/eval_jaxpr/kab,kbf->kaf/dot_general | solution.py:52
  101.4 17.7 %copy.23 = f32[16,8,128,256]{3,1,2,0:T(8,128)} copy(f32[16,8,128,256]{3,2,1,0:T(8,128)} %bitcast.82) | data formatting | bytes 33554432 | tf_op jit(solution)/shard_map/while
  119.1 12.8 %convolution_add_fusion.4 = f32[32,32768]{1,0:T(8,128)} fusion(f32[128,32768]{1,0:T(8,128)} %bitcast.86, f32[32,32768]{1,0:T(8,128)} %get-tuple-element.272, pred[]{:T(512)S(6)} %compare.6, f32[128]{0:T(128)S(1)} %fusion.64, s32[128]{0:T(128)S(1)} %get-tuple-element.252), kind=kOutput, calls=%fused_computation.1.clone.1 | convolution fusion | flops 1612718080 | bytes 25166848 | tf_op jit(solution)/shard_map/while/body/eval_jaxpr/dot_general | solution.py:15
  148.7 12.7 %fusion.63 = f32[128,128,256]{2,1,0:T(8,128)} fusion(bf16[128,128,256]{2,1,0:T(8,128)(2,1)} %bitcast.84, bf16[3,128,128,128]{3,2,1,0:T(8,128)(2,1)} %get-tuple-element.284, s32[]{:T(128)} %get-tuple-element.271), kind=kOutput, calls=%fused_computation.2.clone.1 | convolution fusion | flops 1073741824 | bytes 29360640 | tf_op jit(solution)/shard_map/while/body/eval_jaxpr/kab,kbf->kaf/dot_general | solution.py:52
  161.5 17.7 %copy.23 = f32[16,8,128,256]{3,1,2,0:T(8,128)} copy(f32[16,8,128,256]{3,2,1,0:T(8,128)} %bitcast.82) | data formatting | bytes 33554432 | tf_op jit(solution)/shard_map/while
  179.1 13.6 %convolution_add_fusion.4 = f32[32,32768]{1,0:T(8,128)} fusion(f32[128,32768]{1,0:T(8,128)} %bitcast.86, f32[32,32768]{1,0:T(8,128)} %get-tuple-element.272, pred[]{:T(512)S(6)} %compare.6, f32[128]{0:T(128)S(1)} %fusion.64, s32[128]{0:T(128)S(1)} %get-tuple-element.252), kind=kOutput, calls=%fused_computation.1.clone.1 | convolution fusion | flops 1612718080 | bytes 25166848 | tf_op jit(solution)/shard_map/while/body/eval_jaxpr/dot_general | solution.py:15
  209.6 12.7 %fusion.63 = f32[128,128,256]{2,1,0:T(8,128)} fusion(bf16[128,128,256]{2,1,0:T(8,128)(2,1)} %bitcast.84, bf16[3,128,128,128]{3,2,1,0:T(8,128)(2,1)} %get-tuple-element.284, s32[]{:T(128)} %get-tuple-element.271), kind=kOutput, calls=%fused_computation.2.clone.1 | convolution fusion | flops 1073741824 | bytes 29360640 | tf_op jit(solution)/shard_map/while/body/eval_jaxpr/kab,kbf->kaf/dot_general | solution.py:52
  222.3 17.7 %copy.23 = f32[16,8,128,256]{3,1,2,0:T(8,128)} copy(f32[16,8,128,256]{3,2,1,0:T(8,128)} %bitcast.82) | data formatting | bytes 33554432 | tf_op jit(solution)/shard_map/while
  240.0 13.6 %convolution_add_fusion.4 = f32[32,32768]{1,0:T(8,128)} fusion(f32[128,32768]{1,0:T(8,128)} %bitcast.86, f32[32,32768]{1,0:T(8,128)} %get-tuple-element.272, pred[]{:T(512)S(6)} %compare.6, f32[128]{0:T(128)S(1)} %fusion.64, s32[128]{0:T(128)S(1)} %get-tuple-element.252), kind=kOutput, calls=%fused_computation.1.clone.1 | convolution fusion | flops 1612718080 | bytes 25166848 | tf_op jit(solution)/shard_map/while/body/eval_jaxpr/dot_general | solution.py:15
  258.6 37.5 %reduce-scatter.3.cloned.1.call-done = f32[512,256]{1,0:T(8,128)} async-done(((f32[4096,256]{1,0:T(8,128)}), f32[512,256]{1,0:T(8,128)}) %reduce-scatter.3.cloned.1.call-update) | async-done | bytes 524304 | tf_op jit(solution)/shard_map/reduce_scatter | solution.py:67
  299.3 16.8 %copy.11 = bf16[384,128,128]{1,2,0:T(8,128)(2,1)} copy(bf16[384,128,128]{2,1,0:T(8,128)(2,1)} %bitcast.91) | data formatting | bytes 25165824 | tf_op args[6]
  326.3 187.0 %while.23 = (s32[]{:T(128)}, f32[64,32768]{1,0:T(8,128)}, s32[3,128]{1,0:T(4,128)S(1)}, f32[3,128]{1,0:T(4,128)}, bf16[3,128,128,128]{2,3,1,0:T(8,128)(2,1)}, /*...) while((s32[]{:T(128)}, f32[64,32768]{1,0:T(8,128)}, ...), condition=%wide.region_4.5_spmd.clone, body=%wide.region_3.4_spmd.clone.sunk | while | flops 4571811840 | bytes 123737200 | solution.py:100
  341.2 12.8 %fusion.71 = f32[128,128,256]{2,1,0:T(8,128)} fusion(bf16[128,128,256]{2,1,0:T(8,128)(2,1)} %bitcast.85, bf16[3,128,128,128]{2,3,1,0:T(8,128)(2,1)} %get-tuple-element.311, s32[]{:T(128)} %get-tuple-element.298), kind=kOutput, calls=%fused_computation.22.clone.1 | convolution fusion | flops 1073741824 | bytes 29360640 | tf_op jit(solution)/shard_map/while/body/eval_jaxpr/kab,kaf->kbf/dot_general | solution.py:91
  354.0 17.7 %copy.25 = f32[16,8,128,256]{3,1,2,0:T(8,128)} copy(f32[16,8,128,256]{3,2,1,0:T(8,128)} %bitcast.83) | data formatting | bytes 33554432 | tf_op jit(solution)/shard_map/while
  372.3 15.6 %convolution_add_fusion.5 = f32[64,32768]{1,0:T(8,128)} fusion(f32[128,32768]{1,0:T(8,128)} %bitcast.87, f32[64,32768]{1,0:T(8,128)} %get-tuple-element.299, pred[]{:T(512)S(6)} %compare.7, f32[128]{0:T(128)S(1)} %fusion.72, s32[128]{0:T(128)S(1)} %get-tuple-element.261), kind=kOutput, calls=%fused_computation.21.clone.1 | convolution fusion | flops 3225436160 | bytes 33555456 | tf_op jit(solution)/shard_map/while/body/eval_jaxpr/dot_general | solution.py:15
  402.7 12.8 %fusion.71 = f32[128,128,256]{2,1,0:T(8,128)} fusion(bf16[128,128,256]{2,1,0:T(8,128)(2,1)} %bitcast.85, bf16[3,128,128,128]{2,3,1,0:T(8,128)(2,1)} %get-tuple-element.311, s32[]{:T(128)} %get-tuple-element.298), kind=kOutput, calls=%fused_computation.22.clone.1 | convolution fusion | flops 1073741824 | bytes 29360640 | tf_op jit(solution)/shard_map/while/body/eval_jaxpr/kab,kaf->kbf/dot_general | solution.py:91
  415.4 17.7 %copy.25 = f32[16,8,128,256]{3,1,2,0:T(8,128)} copy(f32[16,8,128,256]{3,2,1,0:T(8,128)} %bitcast.83) | data formatting | bytes 33554432 | tf_op jit(solution)/shard_map/while
  433.8 16.9 %convolution_add_fusion.5 = f32[64,32768]{1,0:T(8,128)} fusion(f32[128,32768]{1,0:T(8,128)} %bitcast.87, f32[64,32768]{1,0:T(8,128)} %get-tuple-element.299, pred[]{:T(512)S(6)} %compare.7, f32[128]{0:T(128)S(1)} %fusion.72, s32[128]{0:T(128)S(1)} %get-tuple-element.261), kind=kOutput, calls=%fused_computation.21.clone.1 | convolution fusion | flops 3225436160 | bytes 33555456 | tf_op jit(solution)/shard_map/while/body/eval_jaxpr/dot_general | solution.py:15
  465.4 12.7 %fusion.71 = f32[128,128,256]{2,1,0:T(8,128)} fusion(bf16[128,128,256]{2,1,0:T(8,128)(2,1)} %bitcast.85, bf16[3,128,128,128]{2,3,1,0:T(8,128)(2,1)} %get-tuple-element.311, s32[]{:T(128)} %get-tuple-element.298), kind=kOutput, calls=%fused_computation.22.clone.1 | convolution fusion | flops 1073741824 | bytes 29360640 | tf_op jit(solution)/shard_map/while/body/eval_jaxpr/kab,kaf->kbf/dot_general | solution.py:91
  478.1 17.7 %copy.25 = f32[16,8,128,256]{3,1,2,0:T(8,128)} copy(f32[16,8,128,256]{3,2,1,0:T(8,128)} %bitcast.83) | data formatting | bytes 33554432 | tf_op jit(solution)/shard_map/while
  496.4 16.9 %convolution_add_fusion.5 = f32[64,32768]{1,0:T(8,128)} fusion(f32[128,32768]{1,0:T(8,128)} %bitcast.87, f32[64,32768]{1,0:T(8,128)} %get-tuple-element.299, pred[]{:T(512)S(6)} %compare.7, f32[128]{0:T(128)S(1)} %fusion.72, s32[128]{0:T(128)S(1)} %get-tuple-element.261), kind=kOutput, calls=%fused_computation.21.clone.1 | convolution fusion | flops 3225436160 | bytes 33555456 | tf_op jit(solution)/shard_map/while/body/eval_jaxpr/dot_general | solution.py:15
  524.4 83.8 %reduce-scatter.5.cloned.1.call-done = f32[512,256]{1,0:T(8,128)} async-done(((f32[8192,256]{1,0:T(8,128)}), f32[512,256]{1,0:T(8,128)}) %reduce-scatter.5.cloned.1.call-update) | async-done | bytes 524304 | tf_op jit(solution)/shard_map/reduce_scatter | solution.py:106
  (65 shorter events, 136.1 us)
Async XLA Ops:
  7.2 289.0 %copy-start = (bf16[256,256]{1,0:T(8,128)(2,1)S(1)}, bf16[256,256]{1,0:T(8,128)(2,1)}, u32[]{:S(2)}) copy-start(bf16[256,256]{1,0:T(8,128)(2,1)} %param.13) | copy-start | bytes 393220
  7.2 64.6 %copy-start.3 = (s32[384]{0:T(512)S(1)}, s32[384]{0:T(512)}, u32[]{:S(2)}) copy-start(s32[384]{0:T(512)} %param.16) | copy-start | bytes 4612
  7.2 64.6 %copy-start.4 = (s32[384]{0:T(512)S(1)}, s32[384]{0:T(512)}, u32[]{:S(2)}) copy-start(s32[384]{0:T(512)} %param.17) | copy-start | bytes 4612
  7.2 57.1 %all-gather.3.cloned.1.call-start = ((), (), s32[]{:S(2)}) async-start(), calls=%async_computation.2 | async-start | bytes 4456448 | tf_op jit(solution)/shard_map/all_gather | solution.py:41
  7.9 288.2 %reduce-scatter.3.cloned.1.call-start = ((), (), s32[]{:S(2)}) async-start(), calls=%async_computation.3 | async-start | bytes 4718592 | tf_op jit(solution)/shard_map/reduce_scatter | solution.py:67
  253.6 5.0 copy-start.5
  253.6 5.0 copy-start.6
  253.6 42.6 %copy-start.7 = (bf16[512,256]{1,0:T(8,128)(2,1)S(1)}, bf16[512,256]{1,0:T(8,128)(2,1)}, u32[]{:S(2)}) copy-start(bf16[512,256]{1,0:T(8,128)(2,1)} %param.14) | copy-start | bytes 786436
  258.5 64.9 %all-gather.5.cloned.1.call-start = ((), (), s32[]{:S(2)}) async-start(), calls=%async_computation.4 | async-start | bytes 2359296 | tf_op jit(solution)/shard_map/all_gather | solution.py:81
  299.3 16.8 %copy-start.2 = (f32[512,256]{1,0:T(8,128)S(1)}, f32[512,256]{1,0:T(8,128)}, u32[]{:S(2)}) copy-start(f32[512,256]{1,0:T(8,128)} %reduce-scatter.3.cloned.1.call-done) | copy-start | bytes 1572868
  299.3 223.4 %all-reduce.2.cloned.1.call-start = ((), (), s32[]{:S(2)}) async-start(), calls=%async_computation.6 | async-start | bytes 524288 | tf_op jit(solution)/shard_map/psum | solution.py:79
  317.1 291.0 %reduce-scatter.5.cloned.1.call-start = ((), (), s32[]{:S(2)}) async-start(), calls=%async_computation.5 | async-start | bytes 8912896 | tf_op jit(solution)/shard_map/reduce_scatter | solution.py:106
  513.3 96.6 %copy-start.1 = (bf16[256,256]{1,0:T(8,128)(2,1)S(1)}, bf16[256,256]{1,0:T(8,128)(2,1)}, u32[]{:S(2)}) copy-start(bf16[256,256]{1,0:T(8,128)(2,1)} %param.13) | copy-start | bytes 393220
Sparse Core Ops, SparseCore 0:
  10.2 54.1 all-gather.2
  258.6 37.4 reduce-scatter.2
  299.4 23.9 all-gather.4
  328.6 142.2 all-reduce.1
  522.8 85.2 reduce-scatter.4
where the time goes:
time: 619 us; the launch traced here: 616 us
  matrix products  210 us (34%)
  local copies, waits for them, and re-layouts  204 us (33%)
  waiting for transfers between devices  184 us (30%)
  between operations  14.5 us (2%)
    while x12, local copies, waits for them, and re-layouts  161 us
    dot_general x6, matrix products, add_into(): lax.dot_general(hot, flat, (((0,), (0,)), ((), ())), precision=lax.Precis...  89.3 us
    reduce_scatter x1, waiting for transfers between devices, shards(): lax.psum_scatter(line_total, 'row', scatter_dimension=0, tiled=True)  83.8 us
    all_gather x1, waiting for transfers between devices, shards(): line = lax.all_gather(features, 'row', axis=0, tiled=True)  55.7 us
    dot_general x3, matrix products, backward_turn(): jnp.einsum('kab,kaf->kbf', values, picked.reshape(-1, edge, width), prefe...  38.3 us
    dot_general x3, matrix products, forward_turn(): jnp.einsum('kab,kbf->kaf', values, picked.reshape(-1, edge, width), prefe...  38.2 us
    reduce_scatter x1, waiting for transfers between devices, shards(): lax.psum_scatter(partial_value, 'rep', scatter_dimension=0, tiled=True)  37.5 us
    dot_general x3, matrix products, forward_turn(): jnp.dot(select_rows(sources, line_count, jnp.bfloat16), line_flat, prefer...  23.4 us
  transfers between devices with their start and end apart: 5, of which 4 were waited for; matrix products, arithmetic and copies ran while one was open for 35% of the time, Pallas kernels for 0%

commit v1 on v0

v1 whole, which is shorter than its diff:
```python
import functools
import math

import jax
import jax.numpy as jnp
from jax import lax
from jax.experimental import pallas as pl
from jax.experimental.pallas import tpu as pltpu
from jax.sharding import PartitionSpec as P

EDGE = 128
MIB = 2**20


def spmm_body(per, unroll, n_dst, dims, count, src_idx, dst_idx, values, src, out, acc):
    i = pl.program_id(0)
    n = count[0]

    @pl.when(i == 0)
    def _():
        acc[...] = jnp.zeros_like(acc)

    @pl.when(i * per < n)
    def _():
        def one(k):
            g = i * per + k
            s = src_idx[g]
            d = jnp.where(g < n, dst_idx[g], n_dst)
            x = src[pl.ds(pl.multiple_of(s * EDGE, EDGE), EDGE), :]
            p = lax.dot_general(values[k], x, (dims, ((), ())), preferred_element_type=jnp.float32)
            acc[pl.ds(pl.multiple_of(d * EDGE, EDGE), EDGE), :] += p

        def step(t, carry):
            for u in range(unroll):
                one(t * unroll + u)
            return carry

        lax.fori_loop(0, per // unroll, step, 0)

    @pl.when(i == pl.num_programs(0) - 1)
    def _():
        out[...] = acc[: n_dst * EDGE, :].astype(out.dtype)


def spmm(count, src_idx, dst_idx, values, src, n_dst, transposed):
    slots = values.shape[0]
    width = src.shape[1]
    per = math.gcd(slots, 32)
    unroll = math.gcd(per, 8)
    dims = ((0,), (0,)) if transposed else ((1,), (0,))

    def chunk(i, count, s, d):
        return (jnp.minimum(i, jnp.maximum(count[0] - 1, 0) // per), 0, 0)

    whole = lambda i, *_: (0, 0)
    return pl.pallas_call(
        functools.partial(spmm_body, per, unroll, n_dst, dims),
        grid_spec=pltpu.PrefetchScalarGridSpec(
            num_scalar_prefetch=3,
            grid=(slots // per,),
            in_specs=[
                pl.BlockSpec((per, EDGE, EDGE), chunk),
                pl.BlockSpec(src.shape, whole),
            ],
            out_specs=pl.BlockSpec((n_dst * EDGE, width), whole),
            scratch_shapes=[pltpu.VMEM(((n_dst + 1) * EDGE, width), jnp.float32)],
        ),
        out_shape=jax.ShapeDtypeStruct((n_dst * EDGE, width), jnp.bfloat16),
        compiler_params=pltpu.CompilerParams(vmem_limit_bytes=48 * MIB),
    )(count, src_idx, dst_idx, values, src)


def shards(
    features, weight, cotangent, row_mask, block_rows, block_cols, block_values, block_count
):
    rows_dev, width = features.shape
    n_rep = lax.axis_size("rep")
    n_row = lax.axis_size("row")
    factor = 1.0 / math.sqrt(rows_dev * n_row * n_rep)
    group_blocks = n_rep * rows_dev // EDGE
    line_blocks = n_row * rows_dev // EDGE

    line = lax.all_gather(features, "row", axis=0, tiled=True)
    partial_value = spmm(
        block_count, block_cols, block_rows, block_values, line, group_blocks, False
    )
    parts = lax.all_to_all(partial_value, "rep", 0, 0, tiled=True)
    summed = jnp.sum(parts.reshape(n_rep, rows_dev, width).astype(jnp.float32), axis=0)
    aggregated = summed.astype(jnp.bfloat16)
    pre = jnp.dot(aggregated, weight, preferred_element_type=jnp.float32)
    gate = jax.nn.sigmoid(pre)
    output = (pre * gate).astype(jnp.bfloat16)
    mask = row_mask.astype(jnp.float32)[:, None]
    slope = (cotangent.astype(jnp.float32) * mask * gate * (1.0 + pre * (1.0 - gate))).astype(
        jnp.bfloat16
    )
    weight_term = lax.dot_general(
        aggregated, slope, (((0,), (0,)), ((), ())), preferred_element_type=jnp.float32
    )
    grad_weight = lax.psum(weight_term, ("row", "rep")) * factor
    own_back = jnp.dot(slope, weight.T, preferred_element_type=jnp.float32).astype(jnp.bfloat16)
    group_back = lax.all_gather(own_back, "rep", axis=0, tiled=True)
    line_total = spmm(
        block_count, block_rows, block_cols, block_values, group_back, line_blocks, True
    )
    line_parts = lax.all_to_all(line_total, "row", 0, 0, tiled=True)
    grad_features = jnp.sum(
        line_parts.reshape(n_row, rows_dev, width).astype(jnp.float32), axis=0
    ).astype(jnp.bfloat16)
    return (output, grad_features, grad_weight)


def solution(mesh):
    in_specs = (
        P(("row", "rep"), None),
        P(),
        P(("row", "rep"), None),
        P(("row", "rep")),
        P(("row", "rep")),
        P(("row", "rep")),
        P(("row", "rep"), None, None),
        P(("row", "rep")),
    )
    out_specs = (P(("row", "rep"), None), P(("row", "rep"), None), P())
    return jax.shard_map(shards, mesh=mesh, in_specs=in_specs, out_specs=out_specs, check_vma=False)
```

time: 619 us -> 360 us (0.58)
  matrix products: 210 us -> 3.03 us
  local copies, waits for them, and re-layouts: 204 us -> 2.98 us
  waiting for transfers between devices: 184 us -> 286 us
  starting transfers between devices: 0.2 us -> 26 us
  Pallas kernels: 0 us -> 18.1 us
    dot_general x18 -> x0, matrix products: 206 us -> none  [the longest x6 89.3 us: add_into(): lax.dot_general(hot, flat, (((0,), (0,)), ((), ())), precision=lax.Precis...]
    psum x1, waiting for transfers between devices: 0.02 us -> 173 us  [shards(): grad_weight = lax.psum(weight_term, ('row', 'rep')) * factor]
    while x12 -> x0, local copies, waits for them, and re-layouts: 161 us -> none
    reduce_scatter x2 -> x0, waiting for transfers between devices: 121 us -> none  [the longest x1 83.8 us: shards(): lax.psum_scatter(line_total, 'row', scatter_dimension=0, tiled=True)]
    all_to_all x0 -> x2, waiting for transfers between devices: none -> 27.1 us  [the longest x1 27.1 us: shards(): parts = lax.all_to_all(partial_value, 'rep', 0, 0, tiled=True)]
    all_to_all x0 -> x2, starting transfers between devices: none -> 25.9 us  [the longest x1 17.4 us: shards(): line_parts = lax.all_to_all(line_total, 'row', 0, 0, tiled=True)]
    reshape x4 -> x0, local copies, waits for them, and re-layouts: 24.5 us -> none  [the longest x1 9.33 us: shards(): line_total = line_total.reshape(-1, width)]
    all_gather x1, waiting for transfers between devices: 6.27 us -> 29.3 us  [shards(): group_back = lax.all_gather(own_back, 'rep', axis=0, tiled=True)]
  transfers between devices with their start and end apart: 5 -> 5, of which waited for: 4 -> 4; matrix products, arithmetic and copies ran while one was open for 35% -> 1% of each run, Pallas kernels for 0% -> 0%
where the time goes in v1:
time: 360 us; the launch traced here: 356 us
  waiting for transfers between devices  286 us (79%)
  starting transfers between devices  26 us (7%)
  Pallas kernels  18.1 us (5%)
  between operations  14.5 us (4%)
  other arithmetic  5.61 us (2%)
    psum x1, waiting for transfers between devices, shards(): grad_weight = lax.psum(weight_term, ('row', 'rep')) * factor  173 us
    all_gather x1, waiting for transfers between devices, shards(): line = lax.all_gather(features, 'row', axis=0, tiled=True)  55.8 us
    all_gather x1, waiting for transfers between devices, shards(): group_back = lax.all_gather(own_back, 'rep', axis=0, tiled=True)  29.3 us
    all_to_all x1, waiting for transfers between devices, shards(): parts = lax.all_to_all(partial_value, 'rep', 0, 0, tiled=True)  27.1 us
    pallas_call x2, Pallas kernels, spmm(): pl.pallas_call(functools.partial(spmm_body, per, unroll, n_dst, dims), gr...  18.1 us
    all_to_all x1, starting transfers between devices, shards(): line_parts = lax.all_to_all(line_total, 'row', 0, 0, tiled=True)  17.4 us
    all_to_all x1, starting transfers between devices, shards(): parts = lax.all_to_all(partial_value, 'rep', 0, 0, tiled=True)  8.44 us
  transfers between devices with their start and end apart: 5, of which 4 were waited for; matrix products, arithmetic and copies ran while one was open for 1% of the time, Pallas kernels for 0%

profile of v1, /device:TPU:0, one launch (start us, length us, event | category | flops | bytes accessed | tf_op | source)
XLA Modules:
  0.0 356.3 jit_solution(2933344137482639062)
XLA Ops:
  7.2 0.0 copy-start
  7.2 0.0 all-gather.3.cloned.1.call-start
  7.2 0.7 all-gather.3.cloned.1.call-update
  8.6 55.8 %all-gather.3.cloned.1.call-done.src = bf16[8192,256]{1,0:T(8,128)(2,1)} async-done(((bf16[512,256]{1,0:T(8,128)(2,1)}), bf16[8192,256]{1,0:T(8,128)(2,1)}) %all-gather.3.cloned.1.call-update) | async-done | bytes 4194320 | tf_op jit(solution)/shard_map/all_gather | solution.py:83
  64.3 0.7 copy-done.2
  65.0 0.7 copy-done.4
  65.7 9.0 %shard_map.103 = bf16[4096,256]{1,0:T(8,128)(2,1)} custom-call(s32[1]{0:T(128)S(6)} %copy.12.count, s32[384]{0:T(512)S(1)} %copy-done.2, s32[384]{0:T(512)S(1)} %copy-done.4, bf16[384,128,128]{2,1,0:T(8,128)(2,1)} %values.3, bf16[8192,256]{1,0:T(8,128)(2,1)} %all-gather.3.cloned.1.call-done.src), custom_call_target="tpu_custom_call" | custom-call | tf_op jit(solution)/shard_map/pallas_call | solution.py:56
  74.6 8.4 %all-to-all-start = ((bf16[8,512,256]{2,1,0:T(8,128)(2,1)}), bf16[8,512,256]{2,1,0:T(8,128)(2,1)S(1)}, u32[]{:S(2)}, u32[]{:S(2)}) async-start(bf16[8,512,256]{2,1,0:T(8,128)(2,1)} %bitcast), calls=%async_computation | async-start | bytes 4194304 | tf_op jit(solution)/shard_map/all_to_all | solution.py:87
  83.1 0.0 all-gather.5.cloned.1.call-start
  83.2 27.1 %all-to-all-done = bf16[8,512,256]{2,1,0:T(8,128)(2,1)S(1)} async-done(((bf16[8,512,256]{2,1,0:T(8,128)(2,1)}), bf16[8,512,256]{2,1,0:T(8,128)(2,1)S(1)}, u32[]{:S(2)}, u32[]{:S(2)}) %all-to-all-start) | async-done | bytes 2097184 | tf_op jit(solution)/shard_map/all_to_all | solution.py:87
  110.3 0.4 reduce_sum.24
  110.7 1.1 multiply_convert_fusion
  111.8 1.0 convolution_convert_fusion
  112.8 0.0 all-gather.5.cloned.1.call-update
  112.8 29.3 %all-gather.5.cloned.1.call-done.src = bf16[4096,256]{1,0:T(8,128)(2,1)} async-done(((bf16[512,256]{1,0:T(8,128)(2,1)}), bf16[4096,256]{1,0:T(8,128)(2,1)}) %all-gather.5.cloned.1.call-update) | async-done | bytes 2097168 | tf_op jit(solution)/shard_map/all_gather | solution.py:102
  142.1 1.6 copy-done.1
  143.6 9.2 %shard_map.104 = bf16[8192,256]{1,0:T(8,128)(2,1)} custom-call(s32[1]{0:T(128)S(6)} %copy.12.count, s32[384]{0:T(512)S(1)} %copy-done.5, s32[384]{0:T(512)S(1)} %copy-done.3, bf16[384,128,128]{2,1,0:T(8,128)(2,1)} %values.3, bf16[4096,256]{1,0:T(8,128)(2,1)S(1)} %copy-done.1), custom_call_target="tpu_custom_call" | custom-call | tf_op jit(solution)/shard_map/pallas_call | solution.py:56
  152.8 17.4 %all-to-all-start.1 = ((bf16[16,512,256]{2,1,0:T(8,128)(2,1)}), bf16[16,512,256]{2,1,0:T(8,128)(2,1)}, u32[]{:S(2)}, u32[]{:S(2)}) async-start(bf16[16,512,256]{2,1,0:T(8,128)(2,1)} %bitcast.8), calls=%async_computation.1 | async-start | bytes 8388608 | tf_op jit(solution)/shard_map/all_to_all | solution.py:106
  170.3 0.0 all-reduce.2.cloned.1.call-start
  170.3 1.0 fusion
  171.3 0.0 all-reduce.2.cloned.1.call-update
  171.3 173.3 %all-reduce.2.cloned.1.call-done = f32[256,256]{1,0:T(8,128)} async-done(((f32[256,256]{1,0:T(8,128)}), f32[256,256]{1,0:T(8,128)}) %all-reduce.2.cloned.1.call-update) | async-done | bytes 262160 | tf_op jit(solution)/shard_map/psum | solution.py:100
  344.6 1.7 broadcast_multiply_fusion
  346.3 3.5 reduce_sum.25
  (14 shorter events, 0.0 us)
Async XLA Ops:
  7.2 103.5 %copy-start = (bf16[256,256]{1,0:T(8,128)(2,1)S(1)}, bf16[256,256]{1,0:T(8,128)(2,1)}, u32[]{:S(2)}) copy-start(bf16[256,256]{1,0:T(8,128)(2,1)} %param.9) | copy-start | bytes 393220
  7.2 57.1 %all-gather.3.cloned.1.call-start = ((), (), s32[]{:S(2)}) async-start(), calls=%async_computation.2 | async-start | bytes 4456448 | tf_op jit(solution)/shard_map/all_gather | solution.py:83
  64.3 0.7 copy-start.2
  65.0 0.7 copy-start.4
  74.6 8.5 %copy-start.6 = (s32[512]{0:T(512)S(1)}, s32[512]{0:T(512)}, u32[]{:S(2)}) copy-start(s32[512]{0:T(512)} %param.11) | copy-start | bytes 6148
  74.6 36.1 %copy-start.7 = (bf16[512,256]{1,0:T(8,128)(2,1)S(1)}, bf16[512,256]{1,0:T(8,128)(2,1)}, u32[]{:S(2)}) copy-start(bf16[512,256]{1,0:T(8,128)(2,1)} %param.10) | copy-start | bytes 786436
  74.6 35.6 %all-to-all-start = ((bf16[8,512,256]{2,1,0:T(8,128)(2,1)}), bf16[8,512,256]{2,1,0:T(8,128)(2,1)S(1)}, u32[]{:S(2)}, u32[]{:S(2)}) async-start(bf16[8,512,256]{2,1,0:T(8,128)(2,1)} %bitcast), calls=%async_computation | async-start | bytes 4194304 | tf_op jit(solution)/shard_map/all_to_all | solution.py:87
  83.1 59.0 %copy-start.3 = (s32[384]{0:T(512)S(1)}, s32[384]{0:T(512)}, u32[]{:S(2)}) copy-start(s32[384]{0:T(512)} %dst_idx.3) | copy-start | bytes 4612
  83.1 59.0 %copy-start.5 = (s32[384]{0:T(512)S(1)}, s32[384]{0:T(512)}, u32[]{:S(2)}) copy-start(s32[384]{0:T(512)} %src_idx.3) | copy-start | bytes 4612
  83.1 58.9 %all-gather.5.cloned.1.call-start = ((), (), s32[]{:S(2)}) async-start(), calls=%async_computation.3 | async-start | bytes 2359296 | tf_op jit(solution)/shard_map/all_gather | solution.py:102
  142.1 1.6 copy-start.1
  152.8 193.4 %all-to-all-start.1 = ((bf16[16,512,256]{2,1,0:T(8,128)(2,1)}), bf16[16,512,256]{2,1,0:T(8,128)(2,1)}, u32[]{:S(2)}, u32[]{:S(2)}) async-start(bf16[16,512,256]{2,1,0:T(8,128)(2,1)} %bitcast.8), calls=%async_computation.1 | async-start | bytes 8388608 | tf_op jit(solution)/shard_map/all_to_all | solution.py:106
  170.3 174.3 %all-reduce.2.cloned.1.call-start = ((), (), s32[]{:S(2)}) async-start(), calls=%async_computation.4 | async-start | bytes 524288 | tf_op jit(solution)/shard_map/psum | solution.py:100
Sparse Core Ops, SparseCore 0:
  10.2 54.1 all-gather.2
  112.9 29.1 all-gather.4
  176.4 168.0 all-reduce.1

commit v2 on v1

v2 whole, which is shorter than its diff:
```python
import functools
import math

import jax
import jax.numpy as jnp
from jax import lax
from jax.experimental import pallas as pl
from jax.experimental.pallas import tpu as pltpu
from jax.sharding import PartitionSpec as P

EDGE = 128
MIB = 2**20
RING = 4
CORES = 2
UNROLL = 8
DEPTH = 4

f32 = jnp.float32
bf16 = jnp.bfloat16


def spmm_body(transposed, splits, n_src, steps, slots, srcs, dsts, values, *refs):
    pieces, rest = refs[:n_src], refs[n_src:]
    outs, (src, acc, ring, src_sem, sems) = rest[: len(splits)], rest[len(splits) :]
    n_steps = steps[0]

    def fetch(step, bank):
        for u in range(UNROLL):
            pair = step * UNROLL + u
            for half in range(2):
                place = pl.ds(half * EDGE, EDGE)
                at = ring.at[bank, u, place, :] if transposed else ring.at[bank, u, :, place]
                pltpu.make_async_copy(values.at[slots[2 * pair + half]], at, sems.at[bank]).start()

    for ahead in range(DEPTH - 1):

        @pl.when(ahead < n_steps)
        def _():
            fetch(ahead, ahead)

    base = 0
    for piece in pieces:
        rows = piece.shape[0]
        pltpu.make_async_copy(piece, src.at[pl.ds(base, rows), :], src_sem).start()
        base += rows
    src[pl.ds(base, EDGE), :] = jnp.zeros((EDGE, src.shape[1]), src.dtype)
    acc[...] = jnp.zeros_like(acc)
    loaded = src.at[pl.ds(0, base), :]
    pltpu.make_async_copy(loaded, loaded, src_sem).wait()
    dims = (((0,), (0,)), ((), ())) if transposed else (((1,), (0,)), ((), ()))

    def step(t, carry):
        bank = lax.rem(t, DEPTH)

        ahead = t + DEPTH - 1

        @pl.when(ahead < n_steps)
        def _():
            fetch(ahead, lax.rem(ahead, DEPTH))

        pltpu.make_async_copy(ring.at[bank], ring.at[bank], sems.at[bank]).wait()
        for u in range(UNROLL):
            pair = t * UNROLL + u
            x = jnp.concatenate(
                [
                    src[pl.ds(pl.multiple_of(srcs[2 * pair + half] * EDGE, EDGE), EDGE), :]
                    for half in range(2)
                ],
                axis=0,
            )
            product = lax.dot_general(ring[bank, u], x, dims, preferred_element_type=f32)
            acc[pl.ds(pl.multiple_of(dsts[pair] * EDGE, EDGE), EDGE), :] += product
        return carry

    lax.fori_loop(0, n_steps, step, 0)
    base = 0
    for out in outs:
        rows = out.shape[0]
        out[...] = acc[pl.ds(base, rows), :].astype(out.dtype)
        base += rows


def spmm(lists, values, pieces, splits, transposed):
    steps, slots, srcs, dsts = lists
    width = pieces[0].shape[1]
    n_src = sum(p.shape[0] for p in pieces)
    n_dst = sum(rows for rows, _ in splits)
    bank = (UNROLL, 2 * EDGE, EDGE) if transposed else (UNROLL, EDGE, 2 * EDGE)
    smem = pl.BlockSpec(memory_space=pltpu.SMEM)
    anywhere = pl.BlockSpec(memory_space=pl.ANY)
    vmem = pl.BlockSpec(memory_space=pltpu.VMEM)
    return pl.pallas_call(
        functools.partial(spmm_body, transposed, splits, len(pieces)),
        in_specs=[smem] * 4 + [anywhere] * (1 + len(pieces)),
        out_specs=[vmem] * len(splits),
        out_shape=[jax.ShapeDtypeStruct((rows, width), kind) for rows, kind in splits],
        scratch_shapes=[
            pltpu.VMEM((n_src + EDGE, width), bf16),
            pltpu.VMEM((n_dst, width), f32),
            pltpu.VMEM((DEPTH, *bank), bf16),
            pltpu.SemaphoreType.DMA,
            pltpu.SemaphoreType.DMA((DEPTH,)),
        ],
        compiler_params=pltpu.CompilerParams(vmem_limit_bytes=54 * MIB),
        cost_estimate=pl.CostEstimate(
            flops=values.shape[0] * EDGE * EDGE * width,
            bytes_accessed=values.shape[0] * EDGE * EDGE,
            transcendentals=0,
        ),
    )(steps, slots, srcs, dsts, values, *pieces)


def pair_lists(live, dst, src, n_dst, n_src):
    slots = dst.shape[0]
    room = -(-((slots + n_dst) // 2) // UNROLL) * UNROLL
    index = jnp.arange(slots, dtype=jnp.int32)
    same = (dst[:, None] == dst[None, :]) & live[None, :]
    rank = jnp.sum((same & (index[None, :] < index[:, None])).astype(jnp.int32), axis=1)
    bins = jnp.arange(n_dst, dtype=jnp.int32)
    counts = jnp.sum(((dst[:, None] == bins[None, :]) & live[:, None]).astype(jnp.int32), axis=0)
    pairs = (counts + 1) // 2
    start = jnp.sum(jnp.where(bins[None, :] < dst[:, None], pairs[None, :], 0), axis=1)
    place = jnp.where(live, 2 * start + rank, -1)
    places = jnp.arange(2 * room, dtype=jnp.int32)
    hit = place[None, :] == places[:, None]
    slot_at = jnp.sum(jnp.where(hit, index[None, :], 0), axis=1)
    src_at = n_src + jnp.sum(jnp.where(hit, src[None, :] - n_src, 0), axis=1)
    dst_at = jnp.sum(jnp.where(hit, dst[None, :], 0), axis=1)[::2]
    steps = (jnp.sum(pairs) + UNROLL - 1) // UNROLL
    return steps.reshape(1), slot_at, src_at, dst_at


def from_ring(value, axis, stride, size, shift):
    pairs = []
    for i in range(size):
        at = i // stride % RING
        pairs.append((i + ((at + shift) % RING - at) * stride, i))
    return lax.ppermute(value, axis, pairs)


def other_core(value):
    return lax.ppermute(value, "rep", [(i, i ^ 1) for i in range(RING * CORES)])


def shards(
    features, weight, cotangent, row_mask, block_rows, block_cols, block_values, block_count
):
    rows_dev, width = features.shape
    n_rep = lax.axis_size("rep")
    n_row = lax.axis_size("row")
    factor = 1.0 / math.sqrt(rows_dev * n_row * n_rep)
    group_blocks = n_rep * rows_dev // EDGE
    line_blocks = n_row * rows_dev // EDGE
    half_rows = rows_dev // 2
    per_half = half_rows // EDGE
    per_dev = rows_dev // EDGE
    i, j = lax.axis_index("row"), lax.axis_index("rep")
    z, x, y, core = i // RING, i % RING, j // CORES, j % CORES
    ring_x = functools.partial(from_ring, axis="row", stride=1, size=n_row)
    ring_z = functools.partial(from_ring, axis="row", stride=RING, size=n_row)
    ring_y = functools.partial(from_ring, axis="rep", stride=CORES, size=n_rep)
    shifts = (1, 3, 2)

    def gather(value, ring):
        got = {s: ring(value, shift=s) for s in shifts}
        return [value, got[1], got[2], got[3]]

    first, second = features[:half_rows], features[half_rows:]
    first_x, second_z = gather(first, ring_x), gather(second, ring_z)
    line = gather(jnp.concatenate(first_x), ring_z) + gather(jnp.concatenate(second_z), ring_x)

    live = jnp.arange(block_rows.shape[0], dtype=jnp.int32) < block_count[0]
    dev, q = block_rows // per_dev, block_rows % per_dev
    dy = (dev // CORES - y) % RING
    across = (dev % CORES) ^ core
    row_at = (across * RING + dy) * per_dev + q
    dev, q = block_cols // per_dev, block_cols % per_dev
    dz, dx = (dev // RING - z) % RING, (dev % RING - x) % RING
    h = q // per_half
    zx, xz = dz * RING + dx, dx * RING + dz
    gathered_at = (h * n_row + jnp.where(h == 0, zx, xz)) * per_half + q % per_half
    scattered_at = (h * n_row + jnp.where(h == 0, xz, zx)) * per_half + q % per_half
    forward = pair_lists(live, row_at, gathered_at, group_blocks, line_blocks)
    backward = pair_lists(live, scattered_at, row_at, line_blocks, group_blocks)
    line, forward, backward = lax.optimization_barrier((line, forward, backward))

    def scatter(parts, ring):
        got = {s: ring(parts[s], shift=RING - s) for s in shifts}
        return parts[0] + got[1].astype(f32) + got[2].astype(f32) + got[3].astype(f32)

    def cut(value, rows):
        return [value[k * rows : (k + 1) * rows] for k in range(RING)]

    side = RING * rows_dev
    mine, others = spmm(forward, block_values, line, ((side, f32), (side, bf16)), False)
    others = other_core(others)
    chip = [a + b.astype(f32) for a, b in zip(cut(mine, rows_dev), cut(others, rows_dev))]
    summed = scatter(chip[:1] + [c.astype(bf16) for c in chip[1:]], ring_y)
    aggregated = summed.astype(bf16)
    pre = jnp.dot(aggregated, weight, preferred_element_type=f32)
    gate = jax.nn.sigmoid(pre)
    output = (pre * gate).astype(bf16)
    mask = row_mask.astype(f32)[:, None]
    slope = (cotangent.astype(f32) * mask * gate * (1.0 + pre * (1.0 - gate))).astype(bf16)
    back = jnp.dot(slope, weight.T, preferred_element_type=f32).astype(bf16)
    backs = gather(back, ring_y)

    weight_term = lax.dot_general(
        aggregated, slope, (((0,), (0,)), ((), ())), preferred_element_type=f32
    )
    weight_term, backs[1] = lax.optimization_barrier((weight_term, backs[1]))
    backs += [other_core(jnp.concatenate(backs))]
    strip = weight_term.shape[0] // n_rep
    strips = weight_term.reshape(RING, CORES, strip, width)

    def at_ring(s):
        return lax.dynamic_index_in_dim(strips, (y + s) % RING, 0, keepdims=False)

    pair = scatter([at_ring(s) for s in range(RING)], ring_y)
    kept = jnp.where(core == 0, pair[0], pair[1])
    own = kept + other_core(jnp.where(core == 0, pair[1], pair[0]))

    ring_rows = RING * half_rows
    splits = (((ring_rows, f32),) + ((ring_rows, bf16),) * (RING - 1)) * 2
    parts = spmm(backward, block_values, backs, splits, True)

    def send(parts, ring):
        return {s: ring(parts[s], shift=RING - s) for s in shifts}

    def add(own, got):
        return own + got[1].astype(f32) + got[2].astype(f32) + got[3].astype(f32)

    near_got = [send(parts[:RING], ring_x), send(parts[RING:], ring_z)]
    own, near_got[0][1] = lax.optimization_barrier((own, near_got[0][1]))
    strips = lax.all_to_all(
        jnp.broadcast_to(own[None], (n_row, strip, width)), "row", 0, 0, tiled=True
    )
    strips = jnp.broadcast_to(jnp.sum(strips, axis=0)[None] * factor, (n_rep, strip, width))
    grad_weight = lax.all_to_all(strips, "rep", 0, 0, tiled=True).reshape(-1, width)
    near_sums = [
        cut(add(own, got), half_rows) for own, got in zip((parts[0], parts[RING]), near_got)
    ]
    totals = [
        scatter(near[:1] + [c.astype(bf16) for c in near[1:]], far)
        for near, far in zip(near_sums, (ring_z, ring_x))
    ]
    grad_features = jnp.concatenate(totals).astype(bf16)
    return output, grad_features, grad_weight


def solution(mesh):
    in_specs = (
        P(("row", "rep"), None),
        P(),
        P(("row", "rep"), None),
        P(("row", "rep")),
        P(("row", "rep")),
        P(("row", "rep")),
        P(("row", "rep"), None, None),
        P(("row", "rep")),
    )
    out_specs = (P(("row", "rep"), None), P(("row", "rep"), None), P())
    return jax.shard_map(shards, mesh=mesh, in_specs=in_specs, out_specs=out_specs, check_vma=False)
```

time: 360 us -> 189 us (0.53)
  the two profiles are of different devices: /device:TPU:0 before, /device:TPU:36 now
where the time goes in v2:
time: 189 us; the launch traced here: 188 us
  starting transfers between devices  87.6 us (46%)
  waiting for transfers between devices  58 us (31%)
  Pallas kernels  17.5 us (9%)
  other arithmetic  14 us (7%)
  local copies, waits for them, and re-layouts  5.99 us (3%)
  between operations  3.16 us (2%)
    ppermute x33, starting transfers between devices, from_ring(): return lax.ppermute(value, axis, pairs)  67.3 us
    ppermute x33, waiting for transfers between devices, from_ring(): return lax.ppermute(value, axis, pairs)  47.7 us
    pallas_call x2, Pallas kernels, spmm(): pl.pallas_call(functools.partial(spmm_body, transposed, splits, len(piece...  17.5 us
    all_to_all x1, starting transfers between devices, shards(): lax.all_to_all(jnp.broadcast_to(own[None], (n_row, strip, width)), 'row',...  13.8 us
    all_to_all x1, waiting for transfers between devices, shards(): lax.all_to_all(strips, 'rep', 0, 0, tiled=True).reshape(-1, width)  6.63 us
  transfers between devices with their start and end apart: 38, of which 14 were waited for; matrix products, arithmetic and copies ran while one was open for 8% of the time, Pallas kernels for 5%

profile of v2, /device:TPU:36, one launch (start us, length us, event | category | flops | bytes accessed | tf_op | source)
XLA Modules:
  0.0 187.9 jit_solution(12147523638829233180)
XLA Ops:
  12.7 2.6 %collective-permute-start.6 = (bf16[256,256]{1,0:T(8,128)(2,1)S(1)}, bf16[256,256]{1,0:T(8,128)(2,1)S(1)}, u32[]{:S(2)}, u32[]{:S(2)}) collective-permute-start(bf16[256,256]{1,0:T(8,128)(2,1)S(1)} %get-tuple-element.98), channel_id=1, source_target_pairs={{32,0},{40,8},{48,16},{56,24},{64,32},{72,40},{80,48},{88,56},{96,... | collective-permute-start | bytes 393224 | tf_op jit(solution)/shard_map/ppermute | solution.py:138
  18.6 3.4 %collective-permute-start.4 = (bf16[1024,256]{1,0:T(8,128)(2,1)S(1)}, bf16[1024,256]{1,0:T(8,128)(2,1)S(1)}, u32[]{:S(2)}, u32[]{:S(2)}) collective-permute-start(bf16[1024,256]{1,0:T(8,128)(2,1)S(1)} %pad_maximum_fusion.1.refs_0_), channel_id=1, source_target_pairs={{64,0},{72,8},{80,16},{88,24},{96,32},{104,40},{112,48},{120,56},{... | collective-permute-start | bytes 1572872 | tf_op jit(solution)/shard_map/ppermute | solution.py:138
  25.4 4.9 %collective-permute-done.5.refs_3_ = bf16[1024,256]{1,0:T(8,128)(2,1)S(1)} collective-permute-done((bf16[1024,256]{1,0:T(8,128)(2,1)S(1)}, bf16[1024,256]{1,0:T(8,128)(2,1)S(1)}, u32[]{:S(2)}, u32[]{:S(2)}) %collective-permute-start.5) | collective-permute-done | bytes 524320 | tf_op jit(solution)/shard_map/ppermute | solution.py:138
  35.3 8.0 %collective-permute-done.3.refs_1_ = bf16[1024,256]{1,0:T(8,128)(2,1)S(1)} collective-permute-done((bf16[1024,256]{1,0:T(8,128)(2,1)S(1)}, bf16[1024,256]{1,0:T(8,128)(2,1)S(1)}, u32[]{:S(2)}, u32[]{:S(2)}) %collective-permute-start.3) | collective-permute-done | bytes 524320 | tf_op jit(solution)/shard_map/ppermute | solution.py:138
  43.4 2.8 %collective-permute-done.10.refs_6_ = bf16[1024,256]{1,0:T(8,128)(2,1)} collective-permute-done((bf16[1024,256]{1,0:T(8,128)(2,1)S(1)}, bf16[1024,256]{1,0:T(8,128)(2,1)}, u32[]{:S(2)}, u32[]{:S(2)}) %collective-permute-start.10) | collective-permute-done | bytes 524320 | tf_op jit(solution)/shard_map/ppermute | solution.py:138
  47.0 8.6 %shard_map.103 = (f32[2048,256]{1,0:T(8,128)}, bf16[2048,256]{1,0:T(8,128)(2,1)}) custom-call(s32[1]{0:T(128)} %bitcast.1.steps, s32[416]{0:T(512)} %get-tuple-element.34.slots, s32[416]{0:T(512)} %broadcast_add_fusion.2.srcs, s32[208]{0:T(256)} %slice.76.dsts, bf16[384,128,128]{2,1,0:T(8,128)(2,1)} %values.3, bf16[1024,256]{1,0:T(8,128)(2,1)} %copy-done.2, ...), custom_call_target="tpu_custom_call" | custom-call | flops 1610612736 | bytes 6291456 | tf_op jit(solution)/shard_map/pallas_call | solution.py:92
  55.6 2.9 %collective-permute-start.12 = (bf16[2048,256]{1,0:T(8,128)(2,1)}, bf16[2048,256]{1,0:T(8,128)(2,1)S(1)}, u32[]{:S(2)}, u32[]{:S(2)}) collective-permute-start(bf16[2048,256]{1,0:T(8,128)(2,1)} %get-tuple-element.46), channel_id=1, source_target_pairs={{0,1},{1,0},{2,3},{3,2},{4,5},{5,4},{6,7},{7,6},{8,9},{9,8},{10,11... | collective-permute-start | bytes 3145736 | tf_op jit(solution)/shard_map/ppermute | solution.py:142
  62.7 3.2 %collective-permute-start.15 = (bf16[512,256]{1,0:T(8,128)(2,1)S(1)}, bf16[512,256]{1,0:T(8,128)(2,1)S(1)}, u32[]{:S(2)}, u32[]{:S(2)}) collective-permute-start(bf16[512,256]{1,0:T(8,128)(2,1)S(1)} %get-tuple-element.85), channel_id=1, source_target_pairs={{2,0},{3,1},{4,2},{5,3},{6,4},{7,5},{0,6},{1,7},{10,8},{11,9},{12,... | collective-permute-start | bytes 786440 | tf_op jit(solution)/shard_map/ppermute | solution.py:138
  66.7 6.2 %collective-permute-done.13 = bf16[512,256]{1,0:T(8,128)(2,1)S(1)} collective-permute-done((bf16[512,256]{1,0:T(8,128)(2,1)S(1)}, bf16[512,256]{1,0:T(8,128)(2,1)S(1)}, u32[]{:S(2)}, u32[]{:S(2)}) %collective-permute-start.13) | collective-permute-done | bytes 262176 | tf_op jit(solution)/shard_map/ppermute | solution.py:138
  72.9 4.5 %collective-permute-done.15 = bf16[512,256]{1,0:T(8,128)(2,1)S(1)} collective-permute-done((bf16[512,256]{1,0:T(8,128)(2,1)S(1)}, bf16[512,256]{1,0:T(8,128)(2,1)S(1)}, u32[]{:S(2)}, u32[]{:S(2)}) %collective-permute-start.15) | collective-permute-done | bytes 262176 | tf_op jit(solution)/shard_map/ppermute | solution.py:138
  85.6 8.8 %collective-permute-done.16.refs_1_ = bf16[512,256]{1,0:T(8,128)(2,1)S(1)} collective-permute-done((bf16[512,256]{1,0:T(8,128)(2,1)S(1)}, bf16[512,256]{1,0:T(8,128)(2,1)S(1)}, u32[]{:S(2)}, u32[]{:S(2)}) %collective-permute-start.16) | collective-permute-done | bytes 262176 | tf_op jit(solution)/shard_map/ppermute | solution.py:138
  94.4 3.4 %collective-permute-done.18.refs_3_ = bf16[512,256]{1,0:T(8,128)(2,1)S(1)} collective-permute-done((bf16[512,256]{1,0:T(8,128)(2,1)S(1)}, bf16[512,256]{1,0:T(8,128)(2,1)S(1)}, u32[]{:S(2)}, u32[]{:S(2)}) %collective-permute-start.18) | collective-permute-done | bytes 262176 | tf_op jit(solution)/shard_map/ppermute | solution.py:138
  98.1 3.2 %collective-permute-start.22 = (f32[2,32,256]{2,1,0:T(8,128)S(1)}, f32[2,32,256]{2,1,0:T(8,128)S(1)}, u32[]{:S(2)}, u32[]{:S(2)}) collective-permute-start(f32[2,32,256]{2,1,0:T(8,128)S(1)} %get-tuple-element.96), channel_id=1, source_target_pairs={{2,0},{3,1},{4,2},{5,3},{6,4},{7,5},{0,6},{1,7},{10,8},{11,9},{12,... | collective-permute-start | bytes 196616 | tf_op jit(solution)/shard_map/ppermute | solution.py:138
  102.4 8.9 %shard_map.104 = (f32[1024,256]{1,0:T(8,128)}, bf16[1024,256]{1,0:T(8,128)(2,1)}, bf16[1024,256]{1,0:T(8,128)(2,1)}, bf16[1024,256]{1,0:T(8,128)(2,1)}, f32[1024...) custom-call(s32[1]{0:T(128)} %bitcast.2.steps, ...), custom_call_target="tpu_custom_call" | custom-call | flops 1610612736 | bytes 6291456 | tf_op jit(solution)/shard_map/pallas_call | solution.py:92
  111.3 10.9 %collective-permute-start.24 = (bf16[1024,256]{1,0:T(8,128)(2,1)}, bf16[1024,256]{1,0:T(8,128)(2,1)S(1)}, u32[]{:S(2)}, u32[]{:S(2)}) collective-permute-start(bf16[1024,256]{1,0:T(8,128)(2,1)} %get-tuple-element.54), channel_id=1, source_target_pairs={{24,0},{0,8},{8,16},{16,24},{56,32},{32,40},{40,48},{48,56},{88,64... | collective-permute-start | bytes 1572872 | tf_op jit(solution)/shard_map/ppermute | solution.py:138
  125.1 5.8 %collective-permute-start.31 = (bf16[1024,256]{1,0:T(8,128)(2,1)}, bf16[1024,256]{1,0:T(8,128)(2,1)}, u32[]{:S(2)}, u32[]{:S(2)}) collective-permute-start(bf16[1024,256]{1,0:T(8,128)(2,1)} %get-tuple-element.60), channel_id=1, source_target_pairs={{64,0},{72,8},{80,16},{88,24},{96,32},{104,40},{112,48},{120,56},{... | collective-permute-start | bytes 1572872 | tf_op jit(solution)/shard_map/ppermute | solution.py:138
  131.0 3.2 %collective-permute-done.24 = bf16[1024,256]{1,0:T(8,128)(2,1)S(1)} collective-permute-done((bf16[1024,256]{1,0:T(8,128)(2,1)}, bf16[1024,256]{1,0:T(8,128)(2,1)S(1)}, u32[]{:S(2)}, u32[]{:S(2)}) %collective-permute-start.24) | collective-permute-done | bytes 524320 | tf_op jit(solution)/shard_map/ppermute | solution.py:138
  134.2 4.5 %collective-permute-start.32 = (bf16[1024,256]{1,0:T(8,128)(2,1)}, bf16[1024,256]{1,0:T(8,128)(2,1)}, u32[]{:S(2)}, u32[]{:S(2)}) collective-permute-start(bf16[1024,256]{1,0:T(8,128)(2,1)} %get-tuple-element.61), channel_id=1, source_target_pairs={{32,0},{40,8},{48,16},{56,24},{64,32},{72,40},{80,48},{88,56},{96,... | collective-permute-start | bytes 1572872 | tf_op jit(solution)/shard_map/ppermute | solution.py:138
  139.6 13.8 %all-to-all-start = ((f32[16,32,256]{2,1,0:T(8,128)}), f32[16,32,256]{2,1,0:T(8,128)S(1)}, u32[]{:S(2)}, u32[]{:S(2)}) async-start(f32[16,32,256]{2,1,0:T(8,128)} %broadcast_in_dim.132), calls=%async_computation | async-start | bytes 1048576 | tf_op jit(solution)/shard_map/all_to_all | solution.py:235
  159.0 3.9 %collective-permute-done.32 = bf16[1024,256]{1,0:T(8,128)(2,1)} collective-permute-done((bf16[1024,256]{1,0:T(8,128)(2,1)}, bf16[1024,256]{1,0:T(8,128)(2,1)}, u32[]{:S(2)}, u32[]{:S(2)}) %collective-permute-start.32) | collective-permute-done | bytes 524320 | tf_op jit(solution)/shard_map/ppermute | solution.py:138
  164.4 5.4 %collective-permute-start.33 = (bf16[256,256]{1,0:T(8,128)(2,1)S(1)}, bf16[256,256]{1,0:T(8,128)(2,1)S(1)}, u32[]{:S(2)}, u32[]{:S(2)}) collective-permute-start(bf16[256,256]{1,0:T(8,128)(2,1)S(1)} %get-tuple-element.90), channel_id=1, source_target_pairs={{24,0},{0,8},{8,16},{16,24},{56,32},{32,40},{40,48},{48,56},{88,64... | collective-permute-start | bytes 393224 | tf_op jit(solution)/shard_map/ppermute | solution.py:138
  169.8 5.7 %collective-permute-start.34 = (bf16[256,256]{1,0:T(8,128)(2,1)S(1)}, bf16[256,256]{1,0:T(8,128)(2,1)S(1)}, u32[]{:S(2)}, u32[]{:S(2)}) collective-permute-start(bf16[256,256]{1,0:T(8,128)(2,1)S(1)} %get-tuple-element.92), channel_id=1, source_target_pairs={{16,0},{24,8},{0,16},{8,24},{48,32},{56,40},{32,48},{40,56},{80,64... | collective-permute-start | bytes 393224 | tf_op jit(solution)/shard_map/ppermute | solution.py:138
  176.3 3.4 %all-to-all-start.1 = ((f32[8,32,256]{2,1,0:T(8,128)}), f32[8,32,256]{2,1,0:T(8,128)S(1)}, u32[]{:S(2)}, u32[]{:S(2)}) async-start(f32[8,32,256]{2,1,0:T(8,128)} %broadcast_in_dim.133), calls=%async_computation.1 | async-start | bytes 524288 | tf_op jit(solution)/shard_map/all_to_all | solution.py:239
  180.5 6.6 %all-to-all-done.1 = f32[8,32,256]{2,1,0:T(8,128)S(1)} async-done(((f32[8,32,256]{2,1,0:T(8,128)}), f32[8,32,256]{2,1,0:T(8,128)S(1)}, u32[]{:S(2)}, u32[]{:S(2)}) %all-to-all-start.1) | async-done | bytes 262176 | tf_op jit(solution)/shard_map/all_to_all | solution.py:239
  (130 shorter events, 50.0 us)
Async XLA Ops:
  1.7 20.3 %collective-permute-start.8 = (bf16[256,256]{1,0:T(8,128)(2,1)S(1)}, bf16[256,256]{1,0:T(8,128)(2,1)S(1)}, u32[]{:S(2)}, u32[]{:S(2)}) collective-permute-start(bf16[256,256]{1,0:T(8,128)(2,1)S(1)} %get-tuple-element.98), channel_id=1, source_target_pairs={{96,0},{104,8},{112,16},{120,24},{0,32},{8,40},{16,48},{24,56},{32... | collective-permute-start | bytes 393224 | tf_op jit(solution)/shard_map/ppermute | solution.py:138
  3.7 18.8 %collective-permute-start.7 = (bf16[256,256]{1,0:T(8,128)(2,1)S(1)}, bf16[256,256]{1,0:T(8,128)(2,1)S(1)}, u32[]{:S(2)}, u32[]{:S(2)}) collective-permute-start(bf16[256,256]{1,0:T(8,128)(2,1)S(1)} %get-tuple-element.98), channel_id=1, source_target_pairs={{64,0},{72,8},{80,16},{88,24},{96,32},{104,40},{112,48},{120,56},{... | collective-permute-start | bytes 393224 | tf_op jit(solution)/shard_map/ppermute | solution.py:138
  15.4 14.9 %collective-permute-start.5 = (bf16[1024,256]{1,0:T(8,128)(2,1)S(1)}, bf16[1024,256]{1,0:T(8,128)(2,1)S(1)}, u32[]{:S(2)}, u32[]{:S(2)}) collective-permute-start(bf16[1024,256]{1,0:T(8,128)(2,1)S(1)} %pad_maximum_fusion.1.refs_0_), channel_id=1, source_target_pairs={{96,0},{104,8},{112,16},{120,24},{0,32},{8,40},{16,48},{24,56},{32... | collective-permute-start | bytes 1572872 | tf_op jit(solution)/shard_map/ppermute | solution.py:138
  18.6 16.7 %collective-permute-start.4 = (bf16[1024,256]{1,0:T(8,128)(2,1)S(1)}, bf16[1024,256]{1,0:T(8,128)(2,1)S(1)}, u32[]{:S(2)}, u32[]{:S(2)}) collective-permute-start(bf16[1024,256]{1,0:T(8,128)(2,1)S(1)} %pad_maximum_fusion.1.refs_0_), channel_id=1, source_target_pairs={{64,0},{72,8},{80,16},{88,24},{96,32},{104,40},{112,48},{120,56},{... | collective-permute-start | bytes 1572872 | tf_op jit(solution)/shard_map/ppermute | solution.py:138
  22.0 21.3 %collective-permute-start.3 = (bf16[1024,256]{1,0:T(8,128)(2,1)S(1)}, bf16[1024,256]{1,0:T(8,128)(2,1)S(1)}, u32[]{:S(2)}, u32[]{:S(2)}) collective-permute-start(bf16[1024,256]{1,0:T(8,128)(2,1)S(1)} %pad_maximum_fusion.1.refs_0_), channel_id=1, source_target_pairs={{32,0},{40,8},{48,16},{56,24},{64,32},{72,40},{80,48},{88,56},{96,... | collective-permute-start | bytes 1572872 | tf_op jit(solution)/shard_map/ppermute | solution.py:138
  22.5 20.9 %collective-permute-start.11 = (bf16[1024,256]{1,0:T(8,128)(2,1)S(1)}, bf16[1024,256]{1,0:T(8,128)(2,1)S(1)}, u32[]{:S(2)}, u32[]{:S(2)}) collective-permute-start(bf16[1024,256]{1,0:T(8,128)(2,1)S(1)} %pad_maximum_fusion.2.refs_4_), channel_id=1, source_target_pairs={{24,0},{0,8},{8,16},{16,24},{56,32},{32,40},{40,48},{48,56},{88,64... | collective-permute-start | bytes 1572872 | tf_op jit(solution)/shard_map/ppermute | solution.py:138
  24.0 22.1 %collective-permute-start.10 = (bf16[1024,256]{1,0:T(8,128)(2,1)S(1)}, bf16[1024,256]{1,0:T(8,128)(2,1)}, u32[]{:S(2)}, u32[]{:S(2)}) collective-permute-start(bf16[1024,256]{1,0:T(8,128)(2,1)S(1)} %pad_maximum_fusion.2.refs_4_), channel_id=1, source_target_pairs={{16,0},{24,8},{0,16},{8,24},{48,32},{56,40},{32,48},{40,56},{80,64... | collective-permute-start | bytes 1572872 | tf_op jit(solution)/shard_map/ppermute | solution.py:138
  30.3 16.6 %collective-permute-start.9 = (bf16[1024,256]{1,0:T(8,128)(2,1)S(1)}, bf16[1024,256]{1,0:T(8,128)(2,1)}, u32[]{:S(2)}, u32[]{:S(2)}) collective-permute-start(bf16[1024,256]{1,0:T(8,128)(2,1)S(1)} %pad_maximum_fusion.2.refs_4_), channel_id=1, source_target_pairs={{8,0},{16,8},{24,16},{0,24},{40,32},{48,40},{56,48},{32,56},{72,64... | collective-permute-start | bytes 1572872 | tf_op jit(solution)/shard_map/ppermute | solution.py:138
  62.7 14.7 %collective-permute-start.15 = (bf16[512,256]{1,0:T(8,128)(2,1)S(1)}, bf16[512,256]{1,0:T(8,128)(2,1)S(1)}, u32[]{:S(2)}, u32[]{:S(2)}) collective-permute-start(bf16[512,256]{1,0:T(8,128)(2,1)S(1)} %get-tuple-element.85), channel_id=1, source_target_pairs={{2,0},{3,1},{4,2},{5,3},{6,4},{7,5},{0,6},{1,7},{10,8},{11,9},{12,... | collective-permute-start | bytes 786440 | tf_op jit(solution)/shard_map/ppermute | solution.py:138
  83.8 14.0 %collective-permute-start.17 = (bf16[512,256]{1,0:T(8,128)(2,1)S(1)}, bf16[512,256]{1,0:T(8,128)(2,1)S(1)}, u32[]{:S(2)}, u32[]{:S(2)}) collective-permute-start(bf16[512,256]{1,0:T(8,128)(2,1)S(1)} %convolution_convert_fusion.refs_0_), channel_id=1, source_target_pairs={{4,0},{5,1},{6,2},{7,3},{0,4},{1,5},{2,6},{3,7},{12,8},{13,9},{14,... | collective-permute-start | bytes 786440 | tf_op jit(solution)/shard_map/ppermute | solution.py:138
  98.1 24.2 %collective-permute-start.20 = (f32[2,32,256]{2,1,0:T(8,128)S(1)}, f32[2,32,256]{2,1,0:T(8,128)S(1)}, u32[]{:S(2)}, u32[]{:S(2)}) collective-permute-start(f32[2,32,256]{2,1,0:T(8,128)S(1)} %get-tuple-element.95), channel_id=1, source_target_pairs={{6,0},{7,1},{0,2},{1,3},{2,4},{3,5},{4,6},{5,7},{14,8},{15,9},{8,1... | collective-permute-start | bytes 196616 | tf_op jit(solution)/shard_map/ppermute | solution.py:138
  98.1 25.7 %collective-permute-start.22 = (f32[2,32,256]{2,1,0:T(8,128)S(1)}, f32[2,32,256]{2,1,0:T(8,128)S(1)}, u32[]{:S(2)}, u32[]{:S(2)}) collective-permute-start(f32[2,32,256]{2,1,0:T(8,128)S(1)} %get-tuple-element.96), channel_id=1, source_target_pairs={{2,0},{3,1},{4,2},{5,3},{6,4},{7,5},{0,6},{1,7},{10,8},{11,9},{12,... | collective-permute-start | bytes 196616 | tf_op jit(solution)/shard_map/ppermute | solution.py:138
  101.4 22.4 %collective-permute-start.21 = (f32[2,32,256]{2,1,0:T(8,128)S(1)}, f32[2,32,256]{2,1,0:T(8,128)S(1)}, u32[]{:S(2)}, u32[]{:S(2)}) collective-permute-start(f32[2,32,256]{2,1,0:T(8,128)S(1)} %get-tuple-element.97), channel_id=1, source_target_pairs={{4,0},{5,1},{6,2},{7,3},{0,4},{1,5},{2,6},{3,7},{12,8},{13,9},{14,... | collective-permute-start | bytes 196616 | tf_op jit(solution)/shard_map/ppermute | solution.py:138
  111.3 22.8 %collective-permute-start.24 = (bf16[1024,256]{1,0:T(8,128)(2,1)}, bf16[1024,256]{1,0:T(8,128)(2,1)S(1)}, u32[]{:S(2)}, u32[]{:S(2)}) collective-permute-start(bf16[1024,256]{1,0:T(8,128)(2,1)} %get-tuple-element.54), channel_id=1, source_target_pairs={{24,0},{0,8},{8,16},{16,24},{56,32},{32,40},{40,48},{48,56},{88,64... | collective-permute-start | bytes 1572872 | tf_op jit(solution)/shard_map/ppermute | solution.py:138
  122.2 31.1 %collective-permute-start.25 = (bf16[1024,256]{1,0:T(8,128)(2,1)}, bf16[1024,256]{1,0:T(8,128)(2,1)S(1)}, u32[]{:S(2)}, u32[]{:S(2)}) collective-permute-start(bf16[1024,256]{1,0:T(8,128)(2,1)} %get-tuple-element.56), channel_id=1, source_target_pairs={{16,0},{24,8},{0,16},{8,24},{48,32},{56,40},{32,48},{40,56},{80,64... | collective-permute-start | bytes 1572872 | tf_op jit(solution)/shard_map/ppermute | solution.py:138
  122.2 31.1 %collective-permute-start.26 = (bf16[1024,256]{1,0:T(8,128)(2,1)}, bf16[1024,256]{1,0:T(8,128)(2,1)}, u32[]{:S(2)}, u32[]{:S(2)}) collective-permute-start(bf16[1024,256]{1,0:T(8,128)(2,1)} %get-tuple-element.57), channel_id=1, source_target_pairs={{8,0},{16,8},{24,16},{0,24},{40,32},{48,40},{56,48},{32,56},{72,64... | collective-permute-start | bytes 1572872 | tf_op jit(solution)/shard_map/ppermute | solution.py:138
  125.1 31.8 %collective-permute-start.30 = (bf16[1024,256]{1,0:T(8,128)(2,1)}, bf16[1024,256]{1,0:T(8,128)(2,1)S(1)}, u32[]{:S(2)}, u32[]{:S(2)}) collective-permute-start(bf16[1024,256]{1,0:T(8,128)(2,1)} %get-tuple-element.59), channel_id=1, source_target_pairs={{96,0},{104,8},{112,16},{120,24},{0,32},{8,40},{16,48},{24,56},{32... | collective-permute-start | bytes 1572872 | tf_op jit(solution)/shard_map/ppermute | solution.py:138
  125.1 33.9 %collective-permute-start.31 = (bf16[1024,256]{1,0:T(8,128)(2,1)}, bf16[1024,256]{1,0:T(8,128)(2,1)}, u32[]{:S(2)}, u32[]{:S(2)}) collective-permute-start(bf16[1024,256]{1,0:T(8,128)(2,1)} %get-tuple-element.60), channel_id=1, source_target_pairs={{64,0},{72,8},{80,16},{88,24},{96,32},{104,40},{112,48},{120,56},{... | collective-permute-start | bytes 1572872 | tf_op jit(solution)/shard_map/ppermute | solution.py:138
  134.2 28.7 %collective-permute-start.32 = (bf16[1024,256]{1,0:T(8,128)(2,1)}, bf16[1024,256]{1,0:T(8,128)(2,1)}, u32[]{:S(2)}, u32[]{:S(2)}) collective-permute-start(bf16[1024,256]{1,0:T(8,128)(2,1)} %get-tuple-element.61), channel_id=1, source_target_pairs={{32,0},{40,8},{48,16},{56,24},{64,32},{72,40},{80,48},{88,56},{96,... | collective-permute-start | bytes 1572872 | tf_op jit(solution)/shard_map/ppermute | solution.py:138
  139.6 36.0 %all-to-all-start = ((f32[16,32,256]{2,1,0:T(8,128)}), f32[16,32,256]{2,1,0:T(8,128)S(1)}, u32[]{:S(2)}, u32[]{:S(2)}) async-start(f32[16,32,256]{2,1,0:T(8,128)} %broadcast_in_dim.132), calls=%async_computation | async-start | bytes 1048576 | tf_op jit(solution)/shard_map/all_to_all | solution.py:235
  154.8 15.0 %collective-permute-start.27 = (bf16[256,256]{1,0:T(8,128)(2,1)S(1)}, bf16[256,256]{1,0:T(8,128)(2,1)S(1)}, u32[]{:S(2)}, u32[]{:S(2)}) collective-permute-start(bf16[256,256]{1,0:T(8,128)(2,1)S(1)} %get-tuple-element.87), channel_id=1, source_target_pairs={{96,0},{104,8},{112,16},{120,24},{0,32},{8,40},{16,48},{24,56},{32... | collective-permute-start | bytes 393224 | tf_op jit(solution)/shard_map/ppermute | solution.py:138
  156.4 19.1 %collective-permute-start.29 = (bf16[256,256]{1,0:T(8,128)(2,1)S(1)}, bf16[256,256]{1,0:T(8,128)(2,1)S(1)}, u32[]{:S(2)}, u32[]{:S(2)}) collective-permute-start(bf16[256,256]{1,0:T(8,128)(2,1)S(1)} %get-tuple-element.88), channel_id=1, source_target_pairs={{32,0},{40,8},{48,16},{56,24},{64,32},{72,40},{80,48},{88,56},{96,... | collective-permute-start | bytes 393224 | tf_op jit(solution)/shard_map/ppermute | solution.py:138
  156.9 18.5 %collective-permute-start.28 = (bf16[256,256]{1,0:T(8,128)(2,1)S(1)}, bf16[256,256]{1,0:T(8,128)(2,1)S(1)}, u32[]{:S(2)}, u32[]{:S(2)}) collective-permute-start(bf16[256,256]{1,0:T(8,128)(2,1)S(1)} %get-tuple-element.89), channel_id=1, source_target_pairs={{64,0},{72,8},{80,16},{88,24},{96,32},{104,40},{112,48},{120,56},{... | collective-permute-start | bytes 393224 | tf_op jit(solution)/shard_map/ppermute | solution.py:138
  164.4 15.3 %collective-permute-start.33 = (bf16[256,256]{1,0:T(8,128)(2,1)S(1)}, bf16[256,256]{1,0:T(8,128)(2,1)S(1)}, u32[]{:S(2)}, u32[]{:S(2)}) collective-permute-start(bf16[256,256]{1,0:T(8,128)(2,1)S(1)} %get-tuple-element.90), channel_id=1, source_target_pairs={{24,0},{0,8},{8,16},{16,24},{56,32},{32,40},{40,48},{48,56},{88,64... | collective-permute-start | bytes 393224 | tf_op jit(solution)/shard_map/ppermute | solution.py:138
  (30 other events, 413.9 us)

commit v3 on v2

--- a/solution.py
+++ b/solution.py
@@ -12,17 +12,17 @@
 MIB = 2**20
 RING = 4
 CORES = 2
-UNROLL = 8
+UNROLL = 16
 DEPTH = 4
 
 f32 = jnp.float32
 bf16 = jnp.bfloat16
 
 
-def spmm_body(transposed, splits, n_src, steps, slots, srcs, dsts, values, *refs):
+def spmm_body(transposed, splits, n_src, room, table, values, *refs):
     pieces, rest = refs[:n_src], refs[n_src:]
-    outs, (src, acc, ring, src_sem, sems) = rest[: len(splits)], rest[len(splits) :]
-    n_steps = steps[0]
+    outs, (src, acc, narrow, ring, src_sem, out_sem, sems) = rest[: len(splits)], rest[len(splits) :]
+    n_steps = table[5 * room]
 
     def fetch(step, bank):
         for u in range(UNROLL):
@@ -30,7 +30,7 @@
             for half in range(2):
                 place = pl.ds(half * EDGE, EDGE)
                 at = ring.at[bank, u, place, :] if transposed else ring.at[bank, u, :, place]
-                pltpu.make_async_copy(values.at[slots[2 * pair + half]], at, sems.at[bank]).start()
+                pltpu.make_async_copy(values.at[table[2 * pair + half]], at, sems.at[bank]).start()
 
     for ahead in range(DEPTH - 1):
 
@@ -51,7 +51,6 @@
 
     def step(t, carry):
         bank = lax.rem(t, DEPTH)
-
         ahead = t + DEPTH - 1
 
         @pl.when(ahead < n_steps)
@@ -63,51 +62,57 @@
             pair = t * UNROLL + u
             x = jnp.concatenate(
                 [
-                    src[pl.ds(pl.multiple_of(srcs[2 * pair + half] * EDGE, EDGE), EDGE), :]
+                    src[pl.ds(pl.multiple_of(table[2 * (room + pair) + half] * EDGE, EDGE), EDGE), :]
                     for half in range(2)
                 ],
                 axis=0,
             )
             product = lax.dot_general(ring[bank, u], x, dims, preferred_element_type=f32)
-            acc[pl.ds(pl.multiple_of(dsts[pair] * EDGE, EDGE), EDGE), :] += product
+            acc[pl.ds(pl.multiple_of(table[4 * room + pair] * EDGE, EDGE), EDGE), :] += product
         return carry
 
     lax.fori_loop(0, n_steps, step, 0)
     base = 0
     for out in outs:
         rows = out.shape[0]
-        out[...] = acc[pl.ds(base, rows), :].astype(out.dtype)
+        at = acc.at[pl.ds(base, rows), :]
+        if out.dtype != acc.dtype:
+            narrow[pl.ds(base, rows), :] = acc[pl.ds(base, rows), :].astype(out.dtype)
+            at = narrow.at[pl.ds(base, rows), :]
+        pltpu.make_async_copy(at, out, out_sem).start()
         base += rows
-
-
-def spmm(lists, values, pieces, splits, transposed):
-    steps, slots, srcs, dsts = lists
+    for out in outs:
+        pltpu.make_async_copy(out, out, out_sem).wait()
+
+
+def spmm(table, values, pieces, splits, transposed):
     width = pieces[0].shape[1]
     n_src = sum(p.shape[0] for p in pieces)
     n_dst = sum(rows for rows, _ in splits)
     bank = (UNROLL, 2 * EDGE, EDGE) if transposed else (UNROLL, EDGE, 2 * EDGE)
     smem = pl.BlockSpec(memory_space=pltpu.SMEM)
     anywhere = pl.BlockSpec(memory_space=pl.ANY)
-    vmem = pl.BlockSpec(memory_space=pltpu.VMEM)
     return pl.pallas_call(
-        functools.partial(spmm_body, transposed, splits, len(pieces)),
-        in_specs=[smem] * 4 + [anywhere] * (1 + len(pieces)),
-        out_specs=[vmem] * len(splits),
+        functools.partial(spmm_body, transposed, splits, len(pieces), table.shape[0] // 5),
+        in_specs=[smem] + [anywhere] * (1 + len(pieces)),
+        out_specs=[anywhere] * len(splits),
         out_shape=[jax.ShapeDtypeStruct((rows, width), kind) for rows, kind in splits],
         scratch_shapes=[
             pltpu.VMEM((n_src + EDGE, width), bf16),
             pltpu.VMEM((n_dst, width), f32),
+            pltpu.VMEM((n_dst, width), bf16),
             pltpu.VMEM((DEPTH, *bank), bf16),
+            pltpu.SemaphoreType.DMA,
             pltpu.SemaphoreType.DMA,
             pltpu.SemaphoreType.DMA((DEPTH,)),
         ],
         compiler_params=pltpu.CompilerParams(vmem_limit_bytes=54 * MIB),
         cost_estimate=pl.CostEstimate(
-            flops=values.shape[0] * EDGE * EDGE * width,
-            bytes_accessed=values.shape[0] * EDGE * EDGE,
+            flops=2 * values.shape[0] * EDGE * EDGE * width,
+            bytes_accessed=2 * values.shape[0] * EDGE * EDGE,
             transcendentals=0,
         ),
-    )(steps, slots, srcs, dsts, values, *pieces)
+    )(table, values, *pieces)
 
 
 def pair_lists(live, dst, src, n_dst, n_src):
@@ -127,7 +132,7 @@
     src_at = n_src + jnp.sum(jnp.where(hit, src[None, :] - n_src, 0), axis=1)
     dst_at = jnp.sum(jnp.where(hit, dst[None, :], 0), axis=1)[::2]
     steps = (jnp.sum(pairs) + UNROLL - 1) // UNROLL
-    return steps.reshape(1), slot_at, src_at, dst_at
+    return jnp.concatenate([slot_at, src_at, dst_at, steps.reshape(1)])
 
 
 def from_ring(value, axis, stride, size, shift):
@@ -167,7 +172,12 @@
 
     first, second = features[:half_rows], features[half_rows:]
     first_x, second_z = gather(first, ring_x), gather(second, ring_z)
-    line = gather(jnp.concatenate(first_x), ring_z) + gather(jnp.concatenate(second_z), ring_x)
+    second_z = jnp.concatenate(second_z)
+    middle = second_z.shape[0] // 2
+    up, down = ring_x(second_z, shift=1), ring_x(second_z, shift=3)
+    across_up, across_down = ring_x(up[:middle], shift=1), ring_x(down[middle:], shift=3)
+    line = gather(jnp.concatenate(first_x), ring_z)
+    line += [second_z, up, across_up, across_down, down]
 
     live = jnp.arange(block_rows.shape[0], dtype=jnp.int32) < block_count[0]
     dev, q = block_rows // per_dev, block_rows % per_dev
@@ -205,24 +215,24 @@
     back = jnp.dot(slope, weight.T, preferred_element_type=f32).astype(bf16)
     backs = gather(back, ring_y)
 
+    backs += [other_core(jnp.concatenate(backs))]
+
     weight_term = lax.dot_general(
         aggregated, slope, (((0,), (0,)), ((), ())), preferred_element_type=f32
     )
-    weight_term, backs[1] = lax.optimization_barrier((weight_term, backs[1]))
-    backs += [other_core(jnp.concatenate(backs))]
-    strip = weight_term.shape[0] // n_rep
-    strips = weight_term.reshape(RING, CORES, strip, width)
-
-    def at_ring(s):
-        return lax.dynamic_index_in_dim(strips, (y + s) % RING, 0, keepdims=False)
-
-    pair = scatter([at_ring(s) for s in range(RING)], ring_y)
-    kept = jnp.where(core == 0, pair[0], pair[1])
-    own = kept + other_core(jnp.where(core == 0, pair[1], pair[0]))
+    devices = n_row * n_rep
+    strips = lax.all_to_all(
+        weight_term.reshape(devices, -1, width), ("row", "rep"), 0, 0, tiled=True
+    )
 
     ring_rows = RING * half_rows
-    splits = (((ring_rows, f32),) + ((ring_rows, bf16),) * (RING - 1)) * 2
+    part_rows = ring_rows // 2
+    splits = ((ring_rows, f32),) + ((ring_rows, bf16),) * (RING - 1)
+    splits += ((ring_rows, f32), (part_rows, f32), (part_rows, bf16), (part_rows, bf16))
+    splits += ((part_rows, bf16), (part_rows, bf16), (part_rows, f32))
     parts = spmm(backward, block_values, backs, splits, True)
+    parts, strips = lax.optimization_barrier((parts, strips))
+    strip = jnp.sum(strips, axis=0) * factor
 
     def send(parts, ring):
         return {s: ring(parts[s], shift=RING - s) for s in shifts}
@@ -230,20 +240,25 @@
     def add(own, got):
         return own + got[1].astype(f32) + got[2].astype(f32) + got[3].astype(f32)
 
-    near_got = [send(parts[:RING], ring_x), send(parts[RING:], ring_z)]
-    own, near_got[0][1] = lax.optimization_barrier((own, near_got[0][1]))
-    strips = lax.all_to_all(
-        jnp.broadcast_to(own[None], (n_row, strip, width)), "row", 0, 0, tiled=True
-    )
-    strips = jnp.broadcast_to(jnp.sum(strips, axis=0)[None] * factor, (n_rep, strip, width))
-    grad_weight = lax.all_to_all(strips, "rep", 0, 0, tiled=True).reshape(-1, width)
-    near_sums = [
-        cut(add(own, got), half_rows) for own, got in zip((parts[0], parts[RING]), near_got)
-    ]
-    totals = [
-        scatter(near[:1] + [c.astype(bf16) for c in near[1:]], far)
-        for near, far in zip(near_sums, (ring_z, ring_x))
-    ]
+    near_first = send(parts[:RING], ring_x)
+    own_z, up_a, up_b, across_a, across_b, down_a, down_b = parts[RING:]
+    through_a, through_b = ring_z(across_a, shift=3), ring_z(across_b, shift=1)
+    up = jnp.concatenate([(up_a + through_a.astype(f32)).astype(bf16), up_b])
+    down = jnp.concatenate([down_a, (down_b + through_b.astype(f32)).astype(bf16)])
+
+    up, down, strip = lax.optimization_barrier((up, down, strip))
+    from_up, from_down = ring_z(up, shift=3), ring_z(down, shift=1)
+    grad_weight = lax.all_to_all(
+        jnp.broadcast_to(strip[None], strips.shape), ("row", "rep"), 0, 0, tiled=True
+    ).reshape(-1, width)
+
+    near_sum = cut(add(parts[0], near_first), half_rows)
+    far_first = near_sum[:1] + [c.astype(bf16) for c in near_sum[1:]]
+    far_first_got = send(far_first, ring_z)
+    near_sum = cut(own_z + from_up.astype(f32) + from_down.astype(f32), half_rows)
+    far_second = near_sum[:1] + [c.astype(bf16) for c in near_sum[1:]]
+    far_second_got = send(far_second, ring_x)
+    totals = [add(far_first[0], far_first_got), add(far_second[0], far_second_got)]
     grad_features = jnp.concatenate(totals).astype(bf16)
     return output, grad_features, grad_weight
 

time: 189 us -> 178 us (0.942)
  the two profiles are of different devices: /device:TPU:36 before, /device:TPU:0 now
where the time goes in v3:
time: 178 us
  starting transfers between devices  79.2 us (44%)
  waiting for transfers between devices  51.5 us (29%)
  Pallas kernels  17.6 us (10%)
  other arithmetic  14.8 us (8%)
  local copies, waits for them, and re-layouts  10 us (6%)
  between operations  3.02 us (2%)
    ppermute x32, starting transfers between devices, from_ring(): return lax.ppermute(value, axis, pairs)  59.9 us
    ppermute x32, waiting for transfers between devices, from_ring(): return lax.ppermute(value, axis, pairs)  35.4 us
    pallas_call x2, Pallas kernels, spmm(): pl.pallas_call(functools.partial(spmm_body, transposed, splits, len(piece...  17.6 us
    all_to_all x1, waiting for transfers between devices, shards(): lax.all_to_all(jnp.broadcast_to(strip[None], strips.shape), ('row', 'rep'...  12.9 us
    all_to_all x1, starting transfers between devices, shards(): lax.all_to_all(jnp.broadcast_to(strip[None], strips.shape), ('row', 'rep'...  10.3 us
    all_to_all x1, starting transfers between devices, shards(): lax.all_to_all(weight_term.reshape(devices, -1, width), ('row', 'rep'), 0...  8.91 us
  transfers between devices with their start and end apart: 36, of which 18 were waited for; matrix products, arithmetic and copies ran while one was open for 11% of the time, Pallas kernels for 5%

profile of v3, /device:TPU:0, one launch (start us, length us, event | category | flops | bytes accessed | tf_op | source)
XLA Modules:
  0.0 177.8 jit_solution(3419917649112518410)
XLA Ops:
  3.7 3.6 %collective-permute-start.7 = (bf16[256,256]{1,0:T(8,128)(2,1)S(1)}, bf16[256,256]{1,0:T(8,128)(2,1)S(1)}, u32[]{:S(2)}, u32[]{:S(2)}) collective-permute-start(bf16[256,256]{1,0:T(8,128)(2,1)S(1)} %get-tuple-element.113), channel_id=1, source_target_pairs={{64,0},{72,8},{80,16},{88,24},{96,32},{104,40},{112,48},{120,56},{... | collective-permute-start | bytes 393224 | tf_op jit(solution)/shard_map/ppermute | solution.py:143
  9.8 2.7 %collective-permute-start.1 = (bf16[256,256]{1,0:T(8,128)(2,1)S(1)}, bf16[256,256]{1,0:T(8,128)(2,1)S(1)}, u32[]{:S(2)}, u32[]{:S(2)}) collective-permute-start(bf16[256,256]{1,0:T(8,128)(2,1)S(1)} %get-tuple-element.114), channel_id=1, source_target_pairs={{16,0},{24,8},{0,16},{8,24},{48,32},{56,40},{32,48},{40,56},{80,64... | collective-permute-start | bytes 393224 | tf_op jit(solution)/shard_map/ppermute | solution.py:143
  19.7 2.6 %collective-permute-start.9 = (bf16[1024,256]{1,0:T(8,128)(2,1)S(1)}, bf16[1024,256]{1,0:T(8,128)(2,1)S(1)}, u32[]{:S(2)}, u32[]{:S(2)}) collective-permute-start(bf16[1024,256]{1,0:T(8,128)(2,1)S(1)} %pad_maximum_fusion.2.refs_4_), channel_id=1, source_target_pairs={{8,0},{16,8},{24,16},{0,24},{40,32},{48,40},{56,48},{32,56},{72,64... | collective-permute-start | bytes 1572872 | tf_op jit(solution)/shard_map/ppermute | solution.py:143
  25.5 2.4 %collective-permute-start.3 = (bf16[1024,256]{1,0:T(8,128)(2,1)S(1)}, bf16[1024,256]{1,0:T(8,128)(2,1)}, u32[]{:S(2)}, u32[]{:S(2)}) collective-permute-start(bf16[1024,256]{1,0:T(8,128)(2,1)S(1)} %pad_maximum_fusion.1.refs_0_), channel_id=1, source_target_pairs={{32,0},{40,8},{48,16},{56,24},{64,32},{72,40},{80,48},{88,56},{96,... | collective-permute-start | bytes 1572872 | tf_op jit(solution)/shard_map/ppermute | solution.py:143
  27.8 4.5 %collective-permute-done.11.refs_8_ = bf16[1024,256]{1,0:T(8,128)(2,1)S(1)} collective-permute-done((bf16[1024,256]{1,0:T(8,128)(2,1)S(1)}, bf16[1024,256]{1,0:T(8,128)(2,1)S(1)}, u32[]{:S(2)}, u32[]{:S(2)}) %collective-permute-start.11) | collective-permute-done | bytes 524320 | tf_op jit(solution)/shard_map/ppermute | solution.py:143
  33.6 3.6 %collective-permute-start.10 = (bf16[512,256]{1,0:T(8,128)(2,1)}, bf16[512,256]{1,0:T(8,128)(2,1)}, u32[]{:S(2)}, u32[]{:S(2)}) collective-permute-start(bf16[512,256]{1,0:T(8,128)(2,1)} %slice.94), channel_id=1, source_target_pairs={{8,0},{16,8},{24,16},{0,24},{40,32},{48,40},{56,48},{32,56},{72,64... | collective-permute-start | bytes 786440 | tf_op jit(solution)/shard_map/ppermute | solution.py:143
  44.4 2.8 %collective-permute-done.5.refs_3_ = bf16[1024,256]{1,0:T(8,128)(2,1)S(1)} collective-permute-done((bf16[1024,256]{1,0:T(8,128)(2,1)S(1)}, bf16[1024,256]{1,0:T(8,128)(2,1)S(1)}, u32[]{:S(2)}, u32[]{:S(2)}) %collective-permute-start.5) | collective-permute-done | bytes 524320 | tf_op jit(solution)/shard_map/ppermute | solution.py:143
  48.1 8.3 %shard_map.103 = (f32[2048,256]{1,0:T(8,128)}, bf16[2048,256]{1,0:T(8,128)(2,1)}) custom-call(s32[1041]{0:T(1024)} %concatenate.27.table, bf16[384,128,128]{2,1,0:T(8,128)(2,1)} %values.3, bf16[1024,256]{1,0:T(8,128)(2,1)} %copy-done.3, bf16[1024,256]{1,0:T(8,128)(2,1)} %collective-permute-done.3.refs_1_, bf16[1024,256]{1,0:T(8,128)(2,1)} %copy-done.13, ...), custom_call_target="tpu_custom_call" | custom-call | flops 3221225472 | bytes 12582912 | tf_op jit(solution)/shard_map/pallas_call | solution.py:95
  56.5 2.9 %collective-permute-done.13 = bf16[2048,256]{1,0:T(8,128)(2,1)S(1)} collective-permute-done((bf16[2048,256]{1,0:T(8,128)(2,1)}, bf16[2048,256]{1,0:T(8,128)(2,1)S(1)}, u32[]{:S(2)}, u32[]{:S(2)}) %collective-permute-start.13) | collective-permute-done | bytes 1048608 | tf_op jit(solution)/shard_map/ppermute | solution.py:147
  61.0 6.5 %collective-permute-start.14 = (bf16[512,256]{1,0:T(8,128)(2,1)S(1)}, bf16[512,256]{1,0:T(8,128)(2,1)S(1)}, u32[]{:S(2)}, u32[]{:S(2)}) collective-permute-start(bf16[512,256]{1,0:T(8,128)(2,1)S(1)} %get-tuple-element.102), channel_id=1, source_target_pairs={{6,0},{7,1},{0,2},{1,3},{2,4},{3,5},{4,6},{5,7},{14,8},{15,9},{8,1... | collective-permute-start | bytes 786440 | tf_op jit(solution)/shard_map/ppermute | solution.py:143
  69.6 4.5 %collective-permute-done.14 = bf16[512,256]{1,0:T(8,128)(2,1)S(1)} collective-permute-done((bf16[512,256]{1,0:T(8,128)(2,1)S(1)}, bf16[512,256]{1,0:T(8,128)(2,1)S(1)}, u32[]{:S(2)}, u32[]{:S(2)}) %collective-permute-start.14) | collective-permute-done | bytes 262176 | tf_op jit(solution)/shard_map/ppermute | solution.py:143
  74.1 2.5 %collective-permute-done.16 = bf16[512,256]{1,0:T(8,128)(2,1)S(1)} collective-permute-done((bf16[512,256]{1,0:T(8,128)(2,1)S(1)}, bf16[512,256]{1,0:T(8,128)(2,1)S(1)}, u32[]{:S(2)}, u32[]{:S(2)}) %collective-permute-start.16) | collective-permute-done | bytes 262176 | tf_op jit(solution)/shard_map/ppermute | solution.py:143
  81.6 2.6 %collective-permute-start.19 = (bf16[512,256]{1,0:T(8,128)(2,1)S(1)}, bf16[512,256]{1,0:T(8,128)(2,1)S(1)}, u32[]{:S(2)}, u32[]{:S(2)}) collective-permute-start(bf16[512,256]{1,0:T(8,128)(2,1)S(1)} %convolution_convert_fusion.refs_0_), channel_id=1, source_target_pairs={{6,0},{7,1},{0,2},{1,3},{2,4},{3,5},{4,6},{5,7},{14,8},{15,9},{8,1... | collective-permute-start | bytes 786440 | tf_op jit(solution)/shard_map/ppermute | solution.py:143
  84.2 3.8 %collective-permute-start.18 = (bf16[512,256]{1,0:T(8,128)(2,1)S(1)}, bf16[512,256]{1,0:T(8,128)(2,1)S(1)}, u32[]{:S(2)}, u32[]{:S(2)}) collective-permute-start(bf16[512,256]{1,0:T(8,128)(2,1)S(1)} %convolution_convert_fusion.refs_0_), channel_id=1, source_target_pairs={{4,0},{5,1},{6,2},{7,3},{0,4},{1,5},{2,6},{3,7},{12,8},{13,9},{14,... | collective-permute-start | bytes 786440 | tf_op jit(solution)/shard_map/ppermute | solution.py:143
  88.3 4.6 %collective-permute-done.19.refs_3_ = bf16[512,256]{1,0:T(8,128)(2,1)S(1)} collective-permute-done((bf16[512,256]{1,0:T(8,128)(2,1)S(1)}, bf16[512,256]{1,0:T(8,128)(2,1)S(1)}, u32[]{:S(2)}, u32[]{:S(2)}) %collective-permute-start.19) | collective-permute-done | bytes 262176 | tf_op jit(solution)/shard_map/ppermute | solution.py:143
  92.8 5.9 %collective-permute-done.18.refs_2_ = bf16[512,256]{1,0:T(8,128)(2,1)S(1)} collective-permute-done((bf16[512,256]{1,0:T(8,128)(2,1)S(1)}, bf16[512,256]{1,0:T(8,128)(2,1)S(1)}, u32[]{:S(2)}, u32[]{:S(2)}) %collective-permute-start.18) | collective-permute-done | bytes 262176 | tf_op jit(solution)/shard_map/ppermute | solution.py:143
  100.1 8.9 %all-to-all-start = ((f32[128,2,256]{2,1,0:T(2,128)}), f32[128,2,256]{2,1,0:T(2,128)S(1)}, u32[]{:S(2)}, u32[]{:S(2)}) async-start(f32[128,2,256]{2,1,0:T(2,128)} %reshape.92), calls=%async_computation | async-start | bytes 524288 | tf_op jit(solution)/shard_map/all_to_all | solution.py:224
  110.0 9.3 %shard_map.104 = (f32[1024,256]{1,0:T(8,128)}, bf16[1024,256]{1,0:T(8,128)(2,1)}, bf16[1024,256]{1,0:T(8,128)(2,1)}, bf16[1024,256]{1,0:T(8,128)(2,1)}, f32[1024...) custom-call(s32[1121]{0:T(1024)} %concatenate.28.table, ...), custom_call_target="tpu_custom_call" | custom-call | flops 3221225472 | bytes 12582912 | tf_op jit(solution)/shard_map/pallas_call | solution.py:95
  119.7 3.2 %collective-permute-start.27 = (bf16[512,256]{1,0:T(8,128)(2,1)}, bf16[512,256]{1,0:T(8,128)(2,1)S(1)}, u32[]{:S(2)}, u32[]{:S(2)}) collective-permute-start(bf16[512,256]{1,0:T(8,128)(2,1)} %get-tuple-element.72), channel_id=1, source_target_pairs={{96,0},{104,8},{112,16},{120,24},{0,32},{8,40},{16,48},{24,56},{32... | collective-permute-start | bytes 786440 | tf_op jit(solution)/shard_map/ppermute | solution.py:143
  123.1 4.4 %collective-permute-start.21 = (bf16[1024,256]{1,0:T(8,128)(2,1)}, bf16[1024,256]{1,0:T(8,128)(2,1)}, u32[]{:S(2)}, u32[]{:S(2)}) collective-permute-start(bf16[1024,256]{1,0:T(8,128)(2,1)} %get-tuple-element.67), channel_id=1, source_target_pairs={{24,0},{0,8},{8,16},{16,24},{56,32},{32,40},{40,48},{48,56},{88,64... | collective-permute-start | bytes 1572872 | tf_op jit(solution)/shard_map/ppermute | solution.py:143
  127.9 2.5 %collective-permute-start.23 = (bf16[1024,256]{1,0:T(8,128)(2,1)}, bf16[1024,256]{1,0:T(8,128)(2,1)}, u32[]{:S(2)}, u32[]{:S(2)}) collective-permute-start(bf16[1024,256]{1,0:T(8,128)(2,1)} %get-tuple-element.69), channel_id=1, source_target_pairs={{8,0},{16,8},{24,16},{0,24},{40,32},{48,40},{56,48},{32,56},{72,64... | collective-permute-start | bytes 1572872 | tf_op jit(solution)/shard_map/ppermute | solution.py:143
  133.6 10.3 %all-to-all-start.1 = ((f32[128,2,256]{2,1,0:T(2,128)}), f32[128,2,256]{2,1,0:T(2,128)S(1)}, u32[]{:S(2)}, u32[]{:S(2)}) async-start(f32[128,2,256]{2,1,0:T(2,128)} %broadcast_in_dim.126), calls=%async_computation.1 | async-start | bytes 524288 | tf_op jit(solution)/shard_map/all_to_all | solution.py:251
  147.1 12.9 %all-to-all-done.1 = f32[128,2,256]{2,1,0:T(2,128)S(1)} async-done(((f32[128,2,256]{2,1,0:T(2,128)}), f32[128,2,256]{2,1,0:T(2,128)S(1)}, u32[]{:S(2)}, u32[]{:S(2)}) %all-to-all-start.1) | async-done | bytes 262176 | tf_op jit(solution)/shard_map/all_to_all | solution.py:251
  167.3 3.2 %collective-permute-start.33 = (bf16[256,256]{1,0:T(8,128)(2,1)S(1)}, bf16[256,256]{1,0:T(8,128)(2,1)S(1)}, u32[]{:S(2)}, u32[]{:S(2)}) collective-permute-start(bf16[256,256]{1,0:T(8,128)(2,1)S(1)} %get-tuple-element.109), channel_id=1, source_target_pairs={{8,0},{16,8},{24,16},{0,24},{40,32},{48,40},{56,48},{32,56},{72,64... | collective-permute-start | bytes 393224 | tf_op jit(solution)/shard_map/ppermute | solution.py:143
  (134 shorter events, 56.3 us)
Async XLA Ops:
  1.7 15.8 %collective-permute-start.8 = (bf16[256,256]{1,0:T(8,128)(2,1)S(1)}, bf16[256,256]{1,0:T(8,128)(2,1)S(1)}, u32[]{:S(2)}, u32[]{:S(2)}) collective-permute-start(bf16[256,256]{1,0:T(8,128)(2,1)S(1)} %get-tuple-element.113), channel_id=1, source_target_pairs={{96,0},{104,8},{112,16},{120,24},{0,32},{8,40},{16,48},{24,56},{32... | collective-permute-start | bytes 393224 | tf_op jit(solution)/shard_map/ppermute | solution.py:143
  3.7 15.3 %collective-permute-start.7 = (bf16[256,256]{1,0:T(8,128)(2,1)S(1)}, bf16[256,256]{1,0:T(8,128)(2,1)S(1)}, u32[]{:S(2)}, u32[]{:S(2)}) collective-permute-start(bf16[256,256]{1,0:T(8,128)(2,1)S(1)} %get-tuple-element.113), channel_id=1, source_target_pairs={{64,0},{72,8},{80,16},{88,24},{96,32},{104,40},{112,48},{120,56},{... | collective-permute-start | bytes 393224 | tf_op jit(solution)/shard_map/ppermute | solution.py:143
  7.3 11.7 %collective-permute-start.6 = (bf16[256,256]{1,0:T(8,128)(2,1)S(1)}, bf16[256,256]{1,0:T(8,128)(2,1)S(1)}, u32[]{:S(2)}, u32[]{:S(2)}) collective-permute-start(bf16[256,256]{1,0:T(8,128)(2,1)S(1)} %get-tuple-element.113), channel_id=1, source_target_pairs={{32,0},{40,8},{48,16},{56,24},{64,32},{72,40},{80,48},{88,56},{96,... | collective-permute-start | bytes 393224 | tf_op jit(solution)/shard_map/ppermute | solution.py:143
  8.3 14.8 %collective-permute-start.2 = (bf16[256,256]{1,0:T(8,128)(2,1)S(1)}, bf16[256,256]{1,0:T(8,128)(2,1)S(1)}, u32[]{:S(2)}, u32[]{:S(2)}) collective-permute-start(bf16[256,256]{1,0:T(8,128)(2,1)S(1)} %get-tuple-element.114), channel_id=1, source_target_pairs={{24,0},{0,8},{8,16},{16,24},{56,32},{32,40},{40,48},{48,56},{88,64... | collective-permute-start | bytes 393224 | tf_op jit(solution)/shard_map/ppermute | solution.py:143
  9.8 13.3 %collective-permute-start.1 = (bf16[256,256]{1,0:T(8,128)(2,1)S(1)}, bf16[256,256]{1,0:T(8,128)(2,1)S(1)}, u32[]{:S(2)}, u32[]{:S(2)}) collective-permute-start(bf16[256,256]{1,0:T(8,128)(2,1)S(1)} %get-tuple-element.114), channel_id=1, source_target_pairs={{16,0},{24,8},{0,16},{8,24},{48,32},{56,40},{32,48},{40,56},{80,64... | collective-permute-start | bytes 393224 | tf_op jit(solution)/shard_map/ppermute | solution.py:143
  19.1 13.3 %collective-permute-start.11 = (bf16[1024,256]{1,0:T(8,128)(2,1)S(1)}, bf16[1024,256]{1,0:T(8,128)(2,1)S(1)}, u32[]{:S(2)}, u32[]{:S(2)}) collective-permute-start(bf16[1024,256]{1,0:T(8,128)(2,1)S(1)} %pad_maximum_fusion.2.refs_4_), channel_id=1, source_target_pairs={{24,0},{0,8},{8,16},{16,24},{56,32},{32,40},{40,48},{48,56},{88,64... | collective-permute-start | bytes 1572872 | tf_op jit(solution)/shard_map/ppermute | solution.py:143
  19.7 13.1 %collective-permute-start.9 = (bf16[1024,256]{1,0:T(8,128)(2,1)S(1)}, bf16[1024,256]{1,0:T(8,128)(2,1)S(1)}, u32[]{:S(2)}, u32[]{:S(2)}) collective-permute-start(bf16[1024,256]{1,0:T(8,128)(2,1)S(1)} %pad_maximum_fusion.2.refs_4_), channel_id=1, source_target_pairs={{8,0},{16,8},{24,16},{0,24},{40,32},{48,40},{56,48},{32,56},{72,64... | collective-permute-start | bytes 1572872 | tf_op jit(solution)/shard_map/ppermute | solution.py:143
  24.0 23.2 %collective-permute-start.5 = (bf16[1024,256]{1,0:T(8,128)(2,1)S(1)}, bf16[1024,256]{1,0:T(8,128)(2,1)S(1)}, u32[]{:S(2)}, u32[]{:S(2)}) collective-permute-start(bf16[1024,256]{1,0:T(8,128)(2,1)S(1)} %pad_maximum_fusion.1.refs_0_), channel_id=1, source_target_pairs={{96,0},{104,8},{112,16},{120,24},{0,32},{8,40},{16,48},{24,56},{32... | collective-permute-start | bytes 1572872 | tf_op jit(solution)/shard_map/ppermute | solution.py:143
  25.1 22.1 %collective-permute-start.4 = (bf16[1024,256]{1,0:T(8,128)(2,1)S(1)}, bf16[1024,256]{1,0:T(8,128)(2,1)S(1)}, u32[]{:S(2)}, u32[]{:S(2)}) collective-permute-start(bf16[1024,256]{1,0:T(8,128)(2,1)S(1)} %pad_maximum_fusion.1.refs_0_), channel_id=1, source_target_pairs={{64,0},{72,8},{80,16},{88,24},{96,32},{104,40},{112,48},{120,56},{... | collective-permute-start | bytes 1572872 | tf_op jit(solution)/shard_map/ppermute | solution.py:143
  25.5 22.4 %collective-permute-start.3 = (bf16[1024,256]{1,0:T(8,128)(2,1)S(1)}, bf16[1024,256]{1,0:T(8,128)(2,1)}, u32[]{:S(2)}, u32[]{:S(2)}) collective-permute-start(bf16[1024,256]{1,0:T(8,128)(2,1)S(1)} %pad_maximum_fusion.1.refs_0_), channel_id=1, source_target_pairs={{32,0},{40,8},{48,16},{56,24},{64,32},{72,40},{80,48},{88,56},{96,... | collective-permute-start | bytes 1572872 | tf_op jit(solution)/shard_map/ppermute | solution.py:143
  32.3 15.6 %collective-permute-start.12 = (bf16[512,256]{1,0:T(8,128)(2,1)S(1)}, bf16[512,256]{1,0:T(8,128)(2,1)}, u32[]{:S(2)}, u32[]{:S(2)}) collective-permute-start(bf16[512,256]{1,0:T(8,128)(2,1)S(1)} %slice.95), channel_id=1, source_target_pairs={{24,0},{0,8},{8,16},{16,24},{56,32},{32,40},{40,48},{48,56},{88,64... | collective-permute-start | bytes 786440 | tf_op jit(solution)/shard_map/ppermute | solution.py:143
  33.6 14.3 %collective-permute-start.10 = (bf16[512,256]{1,0:T(8,128)(2,1)}, bf16[512,256]{1,0:T(8,128)(2,1)}, u32[]{:S(2)}, u32[]{:S(2)}) collective-permute-start(bf16[512,256]{1,0:T(8,128)(2,1)} %slice.94), channel_id=1, source_target_pairs={{8,0},{16,8},{24,16},{0,24},{40,32},{48,40},{56,48},{32,56},{72,64... | collective-permute-start | bytes 786440 | tf_op jit(solution)/shard_map/ppermute | solution.py:143
  61.0 13.1 %collective-permute-start.14 = (bf16[512,256]{1,0:T(8,128)(2,1)S(1)}, bf16[512,256]{1,0:T(8,128)(2,1)S(1)}, u32[]{:S(2)}, u32[]{:S(2)}) collective-permute-start(bf16[512,256]{1,0:T(8,128)(2,1)S(1)} %get-tuple-element.102), channel_id=1, source_target_pairs={{6,0},{7,1},{0,2},{1,3},{2,4},{3,5},{4,6},{5,7},{14,8},{15,9},{8,1... | collective-permute-start | bytes 786440 | tf_op jit(solution)/shard_map/ppermute | solution.py:143
  67.5 11.5 %collective-permute-start.15 = (bf16[512,256]{1,0:T(8,128)(2,1)S(1)}, bf16[512,256]{1,0:T(8,128)(2,1)S(1)}, u32[]{:S(2)}, u32[]{:S(2)}) collective-permute-start(bf16[512,256]{1,0:T(8,128)(2,1)S(1)} %get-tuple-element.104), channel_id=1, source_target_pairs={{4,0},{5,1},{6,2},{7,3},{0,4},{1,5},{2,6},{3,7},{12,8},{13,9},{14,... | collective-permute-start | bytes 786440 | tf_op jit(solution)/shard_map/ppermute | solution.py:143
  81.6 11.3 %collective-permute-start.19 = (bf16[512,256]{1,0:T(8,128)(2,1)S(1)}, bf16[512,256]{1,0:T(8,128)(2,1)S(1)}, u32[]{:S(2)}, u32[]{:S(2)}) collective-permute-start(bf16[512,256]{1,0:T(8,128)(2,1)S(1)} %convolution_convert_fusion.refs_0_), channel_id=1, source_target_pairs={{6,0},{7,1},{0,2},{1,3},{2,4},{3,5},{4,6},{5,7},{14,8},{15,9},{8,1... | collective-permute-start | bytes 786440 | tf_op jit(solution)/shard_map/ppermute | solution.py:143
  84.2 14.6 %collective-permute-start.18 = (bf16[512,256]{1,0:T(8,128)(2,1)S(1)}, bf16[512,256]{1,0:T(8,128)(2,1)S(1)}, u32[]{:S(2)}, u32[]{:S(2)}) collective-permute-start(bf16[512,256]{1,0:T(8,128)(2,1)S(1)} %convolution_convert_fusion.refs_0_), channel_id=1, source_target_pairs={{4,0},{5,1},{6,2},{7,3},{0,4},{1,5},{2,6},{3,7},{12,8},{13,9},{14,... | collective-permute-start | bytes 786440 | tf_op jit(solution)/shard_map/ppermute | solution.py:143
  88.0 10.8 %collective-permute-start.17 = (bf16[512,256]{1,0:T(8,128)(2,1)S(1)}, bf16[512,256]{1,0:T(8,128)(2,1)S(1)}, u32[]{:S(2)}, u32[]{:S(2)}) collective-permute-start(bf16[512,256]{1,0:T(8,128)(2,1)S(1)} %convolution_convert_fusion.refs_0_), channel_id=1, source_target_pairs={{2,0},{3,1},{4,2},{5,3},{6,4},{7,5},{0,6},{1,7},{10,8},{11,9},{12,... | collective-permute-start | bytes 786440 | tf_op jit(solution)/shard_map/ppermute | solution.py:143
  100.1 19.6 %all-to-all-start = ((f32[128,2,256]{2,1,0:T(2,128)}), f32[128,2,256]{2,1,0:T(2,128)S(1)}, u32[]{:S(2)}, u32[]{:S(2)}) async-start(f32[128,2,256]{2,1,0:T(2,128)} %reshape.92), calls=%async_computation | async-start | bytes 524288 | tf_op jit(solution)/shard_map/all_to_all | solution.py:224
  123.1 37.9 %collective-permute-start.21 = (bf16[1024,256]{1,0:T(8,128)(2,1)}, bf16[1024,256]{1,0:T(8,128)(2,1)}, u32[]{:S(2)}, u32[]{:S(2)}) collective-permute-start(bf16[1024,256]{1,0:T(8,128)(2,1)} %get-tuple-element.67), channel_id=1, source_target_pairs={{24,0},{0,8},{8,16},{16,24},{56,32},{32,40},{40,48},{48,56},{88,64... | collective-permute-start | bytes 1572872 | tf_op jit(solution)/shard_map/ppermute | solution.py:143
  127.5 33.5 %collective-permute-start.22 = (bf16[1024,256]{1,0:T(8,128)(2,1)}, bf16[1024,256]{1,0:T(8,128)(2,1)}, u32[]{:S(2)}, u32[]{:S(2)}) collective-permute-start(bf16[1024,256]{1,0:T(8,128)(2,1)} %get-tuple-element.68), channel_id=1, source_target_pairs={{16,0},{24,8},{0,16},{8,24},{48,32},{56,40},{32,48},{40,56},{80,64... | collective-permute-start | bytes 1572872 | tf_op jit(solution)/shard_map/ppermute | solution.py:143
  127.9 33.1 %collective-permute-start.23 = (bf16[1024,256]{1,0:T(8,128)(2,1)}, bf16[1024,256]{1,0:T(8,128)(2,1)}, u32[]{:S(2)}, u32[]{:S(2)}) collective-permute-start(bf16[1024,256]{1,0:T(8,128)(2,1)} %get-tuple-element.69), channel_id=1, source_target_pairs={{8,0},{16,8},{24,16},{0,24},{40,32},{48,40},{56,48},{32,56},{72,64... | collective-permute-start | bytes 1572872 | tf_op jit(solution)/shard_map/ppermute | solution.py:143
  133.6 26.5 %all-to-all-start.1 = ((f32[128,2,256]{2,1,0:T(2,128)}), f32[128,2,256]{2,1,0:T(2,128)S(1)}, u32[]{:S(2)}, u32[]{:S(2)}) async-start(f32[128,2,256]{2,1,0:T(2,128)} %broadcast_in_dim.126), calls=%async_computation.1 | async-start | bytes 524288 | tf_op jit(solution)/shard_map/all_to_all | solution.py:251
  143.8 23.1 %collective-permute-start.29 = (bf16[1024,256]{1,0:T(8,128)(2,1)S(1)}, bf16[1024,256]{1,0:T(8,128)(2,1)S(1)}, u32[]{:S(2)}, u32[]{:S(2)}) collective-permute-start(bf16[1024,256]{1,0:T(8,128)(2,1)S(1)} %pad_maximum_fusion.3), channel_id=1, source_target_pairs={{96,0},{104,8},{112,16},{120,24},{0,32},{8,40},{16,48},{24,56},{32... | collective-permute-start | bytes 1572872 | tf_op jit(solution)/shard_map/ppermute | solution.py:143
  145.0 22.0 %collective-permute-start.30 = (bf16[1024,256]{1,0:T(8,128)(2,1)S(1)}, bf16[1024,256]{1,0:T(8,128)(2,1)S(1)}, u32[]{:S(2)}, u32[]{:S(2)}) collective-permute-start(bf16[1024,256]{1,0:T(8,128)(2,1)S(1)} %pad_maximum_fusion.4), channel_id=1, source_target_pairs={{32,0},{40,8},{48,16},{56,24},{64,32},{72,40},{80,48},{88,56},{96,... | collective-permute-start | bytes 1572872 | tf_op jit(solution)/shard_map/ppermute | solution.py:143
  (30 other events, 417.4 us)

commit v4 on v3

--- a/solution.py
+++ b/solution.py
@@ -106,7 +106,7 @@
             pltpu.SemaphoreType.DMA,
             pltpu.SemaphoreType.DMA((DEPTH,)),
         ],
-        compiler_params=pltpu.CompilerParams(vmem_limit_bytes=54 * MIB),
+        compiler_params=pltpu.CompilerParams(vmem_limit_bytes=49 * MIB),
         cost_estimate=pl.CostEstimate(
             flops=2 * values.shape[0] * EDGE * EDGE * width,
             bytes_accessed=2 * values.shape[0] * EDGE * EDGE,
@@ -172,6 +172,7 @@
 
     first, second = features[:half_rows], features[half_rows:]
     first_x, second_z = gather(first, ring_x), gather(second, ring_z)
+    block_rows, block_cols, first_x = lax.optimization_barrier((block_rows, block_cols, first_x))
     second_z = jnp.concatenate(second_z)
     middle = second_z.shape[0] // 2
     up, down = ring_x(second_z, shift=1), ring_x(second_z, shift=3)
@@ -215,15 +216,17 @@
     back = jnp.dot(slope, weight.T, preferred_element_type=f32).astype(bf16)
     backs = gather(back, ring_y)
 
-    backs += [other_core(jnp.concatenate(backs))]
 
     weight_term = lax.dot_general(
         aggregated, slope, (((0,), (0,)), ((), ())), preferred_element_type=f32
     )
-    devices = n_row * n_rep
-    strips = lax.all_to_all(
-        weight_term.reshape(devices, -1, width), ("row", "rep"), 0, 0, tiled=True
-    )
+
+    def trade(value, axis):
+        return lax.all_to_all(value, axis, 0, 0, tiled=True)
+
+    strips = trade(weight_term.reshape(n_row, -1, width), "row")
+    backs, strips = lax.optimization_barrier((backs, strips))
+    backs += [other_core(jnp.concatenate(backs))]
 
     ring_rows = RING * half_rows
     part_rows = ring_rows // 2
@@ -231,8 +234,6 @@
     splits += ((ring_rows, f32), (part_rows, f32), (part_rows, bf16), (part_rows, bf16))
     splits += ((part_rows, bf16), (part_rows, bf16), (part_rows, f32))
     parts = spmm(backward, block_values, backs, splits, True)
-    parts, strips = lax.optimization_barrier((parts, strips))
-    strip = jnp.sum(strips, axis=0) * factor
 
     def send(parts, ring):
         return {s: ring(parts[s], shift=RING - s) for s in shifts}
@@ -246,11 +247,12 @@
     up = jnp.concatenate([(up_a + through_a.astype(f32)).astype(bf16), up_b])
     down = jnp.concatenate([down_a, (down_b + through_b.astype(f32)).astype(bf16)])
 
-    up, down, strip = lax.optimization_barrier((up, down, strip))
+    up, down, strips = lax.optimization_barrier((up, down, strips))
     from_up, from_down = ring_z(up, shift=3), ring_z(down, shift=1)
-    grad_weight = lax.all_to_all(
-        jnp.broadcast_to(strip[None], strips.shape), ("row", "rep"), 0, 0, tiled=True
-    ).reshape(-1, width)
+    strip = jnp.sum(strips, axis=0) * factor
+    strip = jnp.sum(trade(jnp.broadcast_to(strip[None], (n_rep, *strip.shape)), "rep"), axis=0)
+    strips = trade(jnp.broadcast_to(strip[None], (n_row, *strip.shape)), "row")
+    grad_weight = strips.reshape(-1, width)
 
     near_sum = cut(add(parts[0], near_first), half_rows)
     far_first = near_sum[:1] + [c.astype(bf16) for c in near_sum[1:]]

time: 178 us -> 160 us (0.90); the launches traced: 178 us -> 158 us
  waiting for transfers between devices: 51.5 us -> 36 us
  blocking collectives: 0 us -> 13.1 us
  starting transfers between devices: 79.2 us -> 66.6 us
  Pallas kernels: 17.6 us -> 14.1 us
    all_to_all x0 -> x1, blocking collectives: none -> 13.1 us  [trade(): return lax.all_to_all(value, axis, 0, 0, tiled=True)]
    ppermute x32, waiting for transfers between devices: 35.4 us -> 26.2 us  [from_ring(): return lax.ppermute(value, axis, pairs)]
    all_to_all x2, waiting for transfers between devices: 13.2 us -> 4.33 us  [trade(): return lax.all_to_all(value, axis, 0, 0, tiled=True)]
    all_to_all x2, starting transfers between devices: 19.2 us -> 10.3 us  [trade(): return lax.all_to_all(value, axis, 0, 0, tiled=True)]
    ppermute x32, starting transfers between devices: 59.9 us -> 56.1 us  [from_ring(): return lax.ppermute(value, axis, pairs)]
    pallas_call x2, Pallas kernels: 17.6 us -> 14.1 us  [spmm(): pl.pallas_call(functools.partial(spmm_body, transposed, splits, len(piece...]
    ppermute x2, waiting for transfers between devices: 2.86 us -> 5.5 us  [other_core(): return lax.ppermute(value, 'rep', [(i, i ^ 1) for i in range(RING * CORES)])]
  transfers between devices with their start and end apart: 36 -> 36, of which waited for: 18 -> 12; matrix products, arithmetic and copies ran while one was open for 11% -> 11% of each run, Pallas kernels for 5% -> 0%
where the time goes in v4:
time: 160 us; the launch traced here: 158 us
  starting transfers between devices  66.6 us (42%)
  waiting for transfers between devices  36 us (22%)
  other arithmetic  14.7 us (9%)
  Pallas kernels  14.1 us (9%)
  blocking collectives  13.1 us (8%)
  local copies, waits for them, and re-layouts  8.65 us (5%)
  between operations  2.84 us (2%)
  matrix products  1.62 us (1%)
    ppermute x32, starting transfers between devices, from_ring(): return lax.ppermute(value, axis, pairs)  56.1 us
    ppermute x32, waiting for transfers between devices, from_ring(): return lax.ppermute(value, axis, pairs)  26.2 us
    pallas_call x2, Pallas kernels, spmm(): pl.pallas_call(functools.partial(spmm_body, transposed, splits, len(piece...  14.1 us
    all_to_all x1, blocking collectives, trade(): return lax.all_to_all(value, axis, 0, 0, tiled=True)  13.1 us
    all_to_all x2, starting transfers between devices, trade(): return lax.all_to_all(value, axis, 0, 0, tiled=True)  10.3 us
    ppermute x2, waiting for transfers between devices, other_core(): return lax.ppermute(value, 'rep', [(i, i ^ 1) for i in range(RING * CORES)])  5.5 us
    all_to_all x2, waiting for transfers between devices, trade(): return lax.all_to_all(value, axis, 0, 0, tiled=True)  4.33 us
    another operation x4, other arithmetic  3.2 us
  transfers between devices with their start and end apart: 36, of which 12 were waited for; matrix products, arithmetic and copies ran while one was open for 11% of the time, Pallas kernels for 0%

profile of v4, /device:TPU:0, one launch (start us, length us, event | category | flops | bytes accessed | tf_op | source)
XLA Modules:
  0.0 157.7 jit_solution(14236783325027542824)
XLA Ops:
  3.3 2.7 %collective-permute-start.1 = (bf16[256,256]{1,0:T(8,128)(2,1)S(1)}, bf16[256,256]{1,0:T(8,128)(2,1)S(1)}, u32[]{:S(2)}, u32[]{:S(2)}) collective-permute-start(bf16[256,256]{1,0:T(8,128)(2,1)S(1)} %get-tuple-element.41), channel_id=1, source_target_pairs={{16,0},{24,8},{0,16},{8,24},{48,32},{56,40},{32,48},{40,56},{80,64... | collective-permute-start | bytes 393224 | tf_op jit(solution)/shard_map/ppermute | solution.py:143
  9.4 3.6 %collective-permute-start.7 = (bf16[256,256]{1,0:T(8,128)(2,1)S(1)}, bf16[256,256]{1,0:T(8,128)(2,1)S(1)}, u32[]{:S(2)}, u32[]{:S(2)}) collective-permute-start(bf16[256,256]{1,0:T(8,128)(2,1)S(1)} %get-tuple-element.111), channel_id=1, source_target_pairs={{64,0},{72,8},{80,16},{88,24},{96,32},{104,40},{112,48},{120,56},{... | collective-permute-start | bytes 393224 | tf_op jit(solution)/shard_map/ppermute | solution.py:143
  26.0 8.0 %collective-permute-done.11.refs_8_ = bf16[1024,256]{1,0:T(8,128)(2,1)S(1)} collective-permute-done((bf16[1024,256]{1,0:T(8,128)(2,1)S(1)}, bf16[1024,256]{1,0:T(8,128)(2,1)S(1)}, u32[]{:S(2)}, u32[]{:S(2)}) %collective-permute-start.11) | collective-permute-done | bytes 524320 | tf_op jit(solution)/shard_map/ppermute | solution.py:143
  35.8 3.0 %collective-permute-start.10 = (bf16[512,256]{1,0:T(8,128)(2,1)}, bf16[512,256]{1,0:T(8,128)(2,1)}, u32[]{:S(2)}, u32[]{:S(2)}) collective-permute-start(bf16[512,256]{1,0:T(8,128)(2,1)} %slice.94), channel_id=1, source_target_pairs={{8,0},{16,8},{24,16},{0,24},{40,32},{48,40},{56,48},{32,56},{72,64... | collective-permute-start | bytes 786440 | tf_op jit(solution)/shard_map/ppermute | solution.py:143
  45.2 6.6 %shard_map.103 = (f32[2048,256]{1,0:T(8,128)}, bf16[2048,256]{1,0:T(8,128)(2,1)}) custom-call(s32[1041]{0:T(1024)S(1)} %concatenate.27.table, bf16[384,128,128]{2,1,0:T(8,128)(2,1)} %values.3, bf16[1024,256]{1,0:T(8,128)(2,1)S(1)} %constant_dynamic-update-slice_fusion.refs_0_, bf16[1024,256]{1,0:T(8,128)(2,1)} %collective-permute-done.3.refs_1_, ...), custom_call_target="tpu_custom_call" | custom-call | flops 3221225472 | bytes 12582912 | tf_op jit(solution)/shard_map/pallas_call | solution.py:95
  51.9 2.9 %collective-permute-done.13 = bf16[2048,256]{1,0:T(8,128)(2,1)S(1)} collective-permute-done((bf16[2048,256]{1,0:T(8,128)(2,1)}, bf16[2048,256]{1,0:T(8,128)(2,1)S(1)}, u32[]{:S(2)}, u32[]{:S(2)}) %collective-permute-start.13) | collective-permute-done | bytes 1048608 | tf_op jit(solution)/shard_map/ppermute | solution.py:147
  56.3 4.8 %collective-permute-start.14 = (bf16[512,256]{1,0:T(8,128)(2,1)S(1)}, bf16[512,256]{1,0:T(8,128)(2,1)S(1)}, u32[]{:S(2)}, u32[]{:S(2)}) collective-permute-start(bf16[512,256]{1,0:T(8,128)(2,1)S(1)} %get-tuple-element.100), channel_id=1, source_target_pairs={{6,0},{7,1},{0,2},{1,3},{2,4},{3,5},{4,6},{5,7},{14,8},{15,9},{8,1... | collective-permute-start | bytes 786440 | tf_op jit(solution)/shard_map/ppermute | solution.py:143
  61.2 3.3 %collective-permute-start.15 = (bf16[512,256]{1,0:T(8,128)(2,1)S(1)}, bf16[512,256]{1,0:T(8,128)(2,1)S(1)}, u32[]{:S(2)}, u32[]{:S(2)}) collective-permute-start(bf16[512,256]{1,0:T(8,128)(2,1)S(1)} %get-tuple-element.102), channel_id=1, source_target_pairs={{4,0},{5,1},{6,2},{7,3},{0,4},{1,5},{2,6},{3,7},{12,8},{13,9},{14,... | collective-permute-start | bytes 786440 | tf_op jit(solution)/shard_map/ppermute | solution.py:143
  64.5 3.3 %collective-permute-done.14 = bf16[512,256]{1,0:T(8,128)(2,1)S(1)} collective-permute-done((bf16[512,256]{1,0:T(8,128)(2,1)S(1)}, bf16[512,256]{1,0:T(8,128)(2,1)S(1)}, u32[]{:S(2)}, u32[]{:S(2)}) %collective-permute-start.14) | collective-permute-done | bytes 262176 | tf_op jit(solution)/shard_map/ppermute | solution.py:143
  67.8 2.5 %collective-permute-done.16 = bf16[512,256]{1,0:T(8,128)(2,1)S(1)} collective-permute-done((bf16[512,256]{1,0:T(8,128)(2,1)S(1)}, bf16[512,256]{1,0:T(8,128)(2,1)S(1)}, u32[]{:S(2)}, u32[]{:S(2)}) %collective-permute-start.16) | collective-permute-done | bytes 262176 | tf_op jit(solution)/shard_map/ppermute | solution.py:143
  70.3 4.4 %collective-permute-done.15 = bf16[512,256]{1,0:T(8,128)(2,1)S(1)} collective-permute-done((bf16[512,256]{1,0:T(8,128)(2,1)S(1)}, bf16[512,256]{1,0:T(8,128)(2,1)S(1)}, u32[]{:S(2)}, u32[]{:S(2)}) %collective-permute-start.15) | collective-permute-done | bytes 262176 | tf_op jit(solution)/shard_map/ppermute | solution.py:143
  78.7 2.8 %collective-permute-start.18 = (bf16[512,256]{1,0:T(8,128)(2,1)S(1)}, bf16[512,256]{1,0:T(8,128)(2,1)S(1)}, u32[]{:S(2)}, u32[]{:S(2)}) collective-permute-start(bf16[512,256]{1,0:T(8,128)(2,1)S(1)} %convolution_convert_fusion.refs_0_), channel_id=1, source_target_pairs={{4,0},{5,1},{6,2},{7,3},{0,4},{1,5},{2,6},{3,7},{12,8},{13,9},{14,... | collective-permute-start | bytes 786440 | tf_op jit(solution)/shard_map/ppermute | solution.py:143
  82.1 13.1 %all_to_all.15 = f32[16,16,256]{2,1,0:T(8,128)S(1)} all-to-all(f32[16,16,256]{2,1,0:T(8,128)S(1)} %bitcast.14), channel_id=1, replica_groups=mesh['row'=16,'rep'=8] {'row'}, dimensions={0} | all-to-all | bytes 524288 | tf_op jit(solution)/shard_map/all_to_all | solution.py:225
  95.4 2.6 %collective-permute-done.20.refs_4_ = bf16[2048,256]{1,0:T(8,128)(2,1)S(1)} collective-permute-done((bf16[2048,256]{1,0:T(8,128)(2,1)S(1)}, bf16[2048,256]{1,0:T(8,128)(2,1)S(1)}, u32[]{:S(2)}, u32[]{:S(2)}) %collective-permute-start.20) | collective-permute-done | bytes 1048608 | tf_op jit(solution)/shard_map/ppermute | solution.py:147
  99.1 7.5 %shard_map.104 = (f32[1024,256]{1,0:T(8,128)}, bf16[1024,256]{1,0:T(8,128)(2,1)S(1)}, bf16[1024,256]{1,0:T(8,128)(2,1)S(1)}, bf16[1024,256]{1,0:T(8,128)(2,1)S(1...) custom-call(s32[1121]{0:T(1024)S(1)} %concatenate.28.table, ...), custom_call_target="tpu_custom_call" | custom-call | flops 3221225472 | bytes 12582912 | tf_op jit(solution)/shard_map/pallas_call | solution.py:95
  106.8 3.1 %collective-permute-start.28 = (bf16[512,256]{1,0:T(8,128)(2,1)S(1)}, bf16[512,256]{1,0:T(8,128)(2,1)S(1)}, u32[]{:S(2)}, u32[]{:S(2)}) collective-permute-start(bf16[512,256]{1,0:T(8,128)(2,1)S(1)} %get-tuple-element.74), channel_id=1, source_target_pairs={{32,0},{40,8},{48,16},{56,24},{64,32},{72,40},{80,48},{88,56},{96,... | collective-permute-start | bytes 786440 | tf_op jit(solution)/shard_map/ppermute | solution.py:143
  109.9 3.9 %collective-permute-start.21 = (bf16[1024,256]{1,0:T(8,128)(2,1)S(1)}, bf16[1024,256]{1,0:T(8,128)(2,1)}, u32[]{:S(2)}, u32[]{:S(2)}) collective-permute-start(bf16[1024,256]{1,0:T(8,128)(2,1)S(1)} %get-tuple-element.65), channel_id=1, source_target_pairs={{24,0},{0,8},{8,16},{16,24},{56,32},{32,40},{40,48},{48,56},{88,64... | collective-permute-start | bytes 1572872 | tf_op jit(solution)/shard_map/ppermute | solution.py:143
  113.9 2.3 %collective-permute-start.22 = (bf16[1024,256]{1,0:T(8,128)(2,1)S(1)}, bf16[1024,256]{1,0:T(8,128)(2,1)}, u32[]{:S(2)}, u32[]{:S(2)}) collective-permute-start(bf16[1024,256]{1,0:T(8,128)(2,1)S(1)} %get-tuple-element.66), channel_id=1, source_target_pairs={{16,0},{24,8},{0,16},{8,24},{48,32},{56,40},{32,48},{40,56},{80,64... | collective-permute-start | bytes 1572872 | tf_op jit(solution)/shard_map/ppermute | solution.py:143
  119.1 4.4 %all-to-all-start.1 = ((f32[8,16,256]{2,1,0:T(8,128)}), f32[8,16,256]{2,1,0:T(8,128)S(1)}, u32[]{:S(2)}, u32[]{:S(2)}) async-start(f32[8,16,256]{2,1,0:T(8,128)} %broadcast_in_dim.132), calls=%async_computation.1 | async-start | bytes 262144 | tf_op jit(solution)/shard_map/all_to_all | solution.py:225
  126.7 2.9 %all-to-all-done.1 = f32[8,16,256]{2,1,0:T(8,128)S(1)} async-done(((f32[8,16,256]{2,1,0:T(8,128)}), f32[8,16,256]{2,1,0:T(8,128)S(1)}, u32[]{:S(2)}, u32[]{:S(2)}) %all-to-all-start.1) | async-done | bytes 131104 | tf_op jit(solution)/shard_map/all_to_all | solution.py:225
  130.4 5.9 %all-to-all-start.2 = ((f32[16,16,256]{2,1,0:T(8,128)}), f32[16,16,256]{2,1,0:T(8,128)S(1)}, u32[]{:S(2)}, u32[]{:S(2)}) async-start(f32[16,16,256]{2,1,0:T(8,128)} %broadcast_in_dim.133), calls=%async_computation.2 | async-start | bytes 524288 | tf_op jit(solution)/shard_map/all_to_all | solution.py:225
  140.6 2.5 %collective-permute-start.26 = (bf16[256,256]{1,0:T(8,128)(2,1)S(1)}, bf16[256,256]{1,0:T(8,128)(2,1)S(1)}, u32[]{:S(2)}, u32[]{:S(2)}) collective-permute-start(bf16[256,256]{1,0:T(8,128)(2,1)S(1)} %get-tuple-element.104), channel_id=1, source_target_pairs={{32,0},{40,8},{48,16},{56,24},{64,32},{72,40},{80,48},{88,56},{96,... | collective-permute-start | bytes 393224 | tf_op jit(solution)/shard_map/ppermute | solution.py:143
  147.1 2.6 %collective-permute-start.33 = (bf16[256,256]{1,0:T(8,128)(2,1)S(1)}, bf16[256,256]{1,0:T(8,128)(2,1)S(1)}, u32[]{:S(2)}, u32[]{:S(2)}) collective-permute-start(bf16[256,256]{1,0:T(8,128)(2,1)S(1)} %get-tuple-element.107), channel_id=1, source_target_pairs={{8,0},{16,8},{24,16},{0,24},{40,32},{48,40},{56,48},{32,56},{72,64... | collective-permute-start | bytes 393224 | tf_op jit(solution)/shard_map/ppermute | solution.py:143
  150.1 3.9 %collective-permute-done.31 = bf16[256,256]{1,0:T(8,128)(2,1)S(1)} collective-permute-done((bf16[256,256]{1,0:T(8,128)(2,1)S(1)}, bf16[256,256]{1,0:T(8,128)(2,1)S(1)}, u32[]{:S(2)}, u32[]{:S(2)}) %collective-permute-start.31) | collective-permute-done | bytes 131104 | tf_op jit(solution)/shard_map/ppermute | solution.py:143
  (115 shorter events, 52.2 us)
Async XLA Ops:
  1.7 12.0 %collective-permute-start.2 = (bf16[256,256]{1,0:T(8,128)(2,1)S(1)}, bf16[256,256]{1,0:T(8,128)(2,1)S(1)}, u32[]{:S(2)}, u32[]{:S(2)}) collective-permute-start(bf16[256,256]{1,0:T(8,128)(2,1)S(1)} %get-tuple-element.41), channel_id=1, source_target_pairs={{24,0},{0,8},{8,16},{16,24},{56,32},{32,40},{40,48},{48,56},{88,64... | collective-permute-start | bytes 393224 | tf_op jit(solution)/shard_map/ppermute | solution.py:143
  3.3 11.4 %collective-permute-start.1 = (bf16[256,256]{1,0:T(8,128)(2,1)S(1)}, bf16[256,256]{1,0:T(8,128)(2,1)S(1)}, u32[]{:S(2)}, u32[]{:S(2)}) collective-permute-start(bf16[256,256]{1,0:T(8,128)(2,1)S(1)} %get-tuple-element.41), channel_id=1, source_target_pairs={{16,0},{24,8},{0,16},{8,24},{48,32},{56,40},{32,48},{40,56},{80,64... | collective-permute-start | bytes 393224 | tf_op jit(solution)/shard_map/ppermute | solution.py:143
  7.5 12.2 %collective-permute-start.8 = (bf16[256,256]{1,0:T(8,128)(2,1)S(1)}, bf16[256,256]{1,0:T(8,128)(2,1)S(1)}, u32[]{:S(2)}, u32[]{:S(2)}) collective-permute-start(bf16[256,256]{1,0:T(8,128)(2,1)S(1)} %get-tuple-element.111), channel_id=1, source_target_pairs={{96,0},{104,8},{112,16},{120,24},{0,32},{8,40},{16,48},{24,56},{32... | collective-permute-start | bytes 393224 | tf_op jit(solution)/shard_map/ppermute | solution.py:143
  9.4 11.4 %collective-permute-start.7 = (bf16[256,256]{1,0:T(8,128)(2,1)S(1)}, bf16[256,256]{1,0:T(8,128)(2,1)S(1)}, u32[]{:S(2)}, u32[]{:S(2)}) collective-permute-start(bf16[256,256]{1,0:T(8,128)(2,1)S(1)} %get-tuple-element.111), channel_id=1, source_target_pairs={{64,0},{72,8},{80,16},{88,24},{96,32},{104,40},{112,48},{120,56},{... | collective-permute-start | bytes 393224 | tf_op jit(solution)/shard_map/ppermute | solution.py:143
  14.8 30.4 %collective-permute-start.5 = (bf16[1024,256]{1,0:T(8,128)(2,1)S(1)}, bf16[1024,256]{1,0:T(8,128)(2,1)S(1)}, u32[]{:S(2)}, u32[]{:S(2)}) collective-permute-start(bf16[1024,256]{1,0:T(8,128)(2,1)S(1)} %constant_dynamic-update-slice_fusion.refs_0_), channel_id=1, source_target_pairs={{96,0},{104,8},{112,16},{120,24},{0,32},{8,40},{16,48},{24,56},{32... | collective-permute-start | bytes 1572872 | tf_op jit(solution)/shard_map/ppermute | solution.py:143
  15.9 29.3 %collective-permute-start.4 = (bf16[1024,256]{1,0:T(8,128)(2,1)S(1)}, bf16[1024,256]{1,0:T(8,128)(2,1)S(1)}, u32[]{:S(2)}, u32[]{:S(2)}) collective-permute-start(bf16[1024,256]{1,0:T(8,128)(2,1)S(1)} %constant_dynamic-update-slice_fusion.refs_0_), channel_id=1, source_target_pairs={{64,0},{72,8},{80,16},{88,24},{96,32},{104,40},{112,48},{120,56},{... | collective-permute-start | bytes 1572872 | tf_op jit(solution)/shard_map/ppermute | solution.py:143
  19.7 25.5 %collective-permute-start.3 = (bf16[1024,256]{1,0:T(8,128)(2,1)S(1)}, bf16[1024,256]{1,0:T(8,128)(2,1)}, u32[]{:S(2)}, u32[]{:S(2)}) collective-permute-start(bf16[1024,256]{1,0:T(8,128)(2,1)S(1)} %constant_dynamic-update-slice_fusion.refs_0_), channel_id=1, source_target_pairs={{32,0},{40,8},{48,16},{56,24},{64,32},{72,40},{80,48},{88,56},{96,... | collective-permute-start | bytes 1572872 | tf_op jit(solution)/shard_map/ppermute | solution.py:143
  20.8 13.2 %collective-permute-start.11 = (bf16[1024,256]{1,0:T(8,128)(2,1)S(1)}, bf16[1024,256]{1,0:T(8,128)(2,1)S(1)}, u32[]{:S(2)}, u32[]{:S(2)}) collective-permute-start(bf16[1024,256]{1,0:T(8,128)(2,1)S(1)} %pad_maximum_fusion.1.refs_4_), channel_id=1, source_target_pairs={{24,0},{0,8},{8,16},{16,24},{56,32},{32,40},{40,48},{48,56},{88,64... | collective-permute-start | bytes 1572872 | tf_op jit(solution)/shard_map/ppermute | solution.py:143
  22.2 12.8 %collective-permute-start.9 = (bf16[1024,256]{1,0:T(8,128)(2,1)S(1)}, bf16[1024,256]{1,0:T(8,128)(2,1)S(1)}, u32[]{:S(2)}, u32[]{:S(2)}) collective-permute-start(bf16[1024,256]{1,0:T(8,128)(2,1)S(1)} %pad_maximum_fusion.1.refs_4_), channel_id=1, source_target_pairs={{8,0},{16,8},{24,16},{0,24},{40,32},{48,40},{56,48},{32,56},{72,64... | collective-permute-start | bytes 1572872 | tf_op jit(solution)/shard_map/ppermute | solution.py:143
  34.8 10.4 %collective-permute-start.12 = (bf16[512,256]{1,0:T(8,128)(2,1)}, bf16[512,256]{1,0:T(8,128)(2,1)S(1)}, u32[]{:S(2)}, u32[]{:S(2)}) collective-permute-start(bf16[512,256]{1,0:T(8,128)(2,1)} %slice.95), channel_id=1, source_target_pairs={{24,0},{0,8},{8,16},{16,24},{56,32},{32,40},{40,48},{48,56},{88,64... | collective-permute-start | bytes 786440 | tf_op jit(solution)/shard_map/ppermute | solution.py:143
  56.3 11.4 %collective-permute-start.14 = (bf16[512,256]{1,0:T(8,128)(2,1)S(1)}, bf16[512,256]{1,0:T(8,128)(2,1)S(1)}, u32[]{:S(2)}, u32[]{:S(2)}) collective-permute-start(bf16[512,256]{1,0:T(8,128)(2,1)S(1)} %get-tuple-element.100), channel_id=1, source_target_pairs={{6,0},{7,1},{0,2},{1,3},{2,4},{3,5},{4,6},{5,7},{14,8},{15,9},{8,1... | collective-permute-start | bytes 786440 | tf_op jit(solution)/shard_map/ppermute | solution.py:143
  61.2 13.5 %collective-permute-start.15 = (bf16[512,256]{1,0:T(8,128)(2,1)S(1)}, bf16[512,256]{1,0:T(8,128)(2,1)S(1)}, u32[]{:S(2)}, u32[]{:S(2)}) collective-permute-start(bf16[512,256]{1,0:T(8,128)(2,1)S(1)} %get-tuple-element.102), channel_id=1, source_target_pairs={{4,0},{5,1},{6,2},{7,3},{0,4},{1,5},{2,6},{3,7},{12,8},{13,9},{14,... | collective-permute-start | bytes 786440 | tf_op jit(solution)/shard_map/ppermute | solution.py:143
  77.2 18.0 %collective-permute-start.19 = (bf16[512,256]{1,0:T(8,128)(2,1)S(1)}, bf16[512,256]{1,0:T(8,128)(2,1)S(1)}, u32[]{:S(2)}, u32[]{:S(2)}) collective-permute-start(bf16[512,256]{1,0:T(8,128)(2,1)S(1)} %convolution_convert_fusion.refs_0_), channel_id=1, source_target_pairs={{6,0},{7,1},{0,2},{1,3},{2,4},{3,5},{4,6},{5,7},{14,8},{15,9},{8,1... | collective-permute-start | bytes 786440 | tf_op jit(solution)/shard_map/ppermute | solution.py:143
  78.7 16.5 %collective-permute-start.18 = (bf16[512,256]{1,0:T(8,128)(2,1)S(1)}, bf16[512,256]{1,0:T(8,128)(2,1)S(1)}, u32[]{:S(2)}, u32[]{:S(2)}) collective-permute-start(bf16[512,256]{1,0:T(8,128)(2,1)S(1)} %convolution_convert_fusion.refs_0_), channel_id=1, source_target_pairs={{4,0},{5,1},{6,2},{7,3},{0,4},{1,5},{2,6},{3,7},{12,8},{13,9},{14,... | collective-permute-start | bytes 786440 | tf_op jit(solution)/shard_map/ppermute | solution.py:143
  81.6 13.7 %collective-permute-start.17 = (bf16[512,256]{1,0:T(8,128)(2,1)S(1)}, bf16[512,256]{1,0:T(8,128)(2,1)S(1)}, u32[]{:S(2)}, u32[]{:S(2)}) collective-permute-start(bf16[512,256]{1,0:T(8,128)(2,1)S(1)} %convolution_convert_fusion.refs_0_), channel_id=1, source_target_pairs={{2,0},{3,1},{4,2},{5,3},{6,4},{7,5},{0,6},{1,7},{10,8},{11,9},{12,... | collective-permute-start | bytes 786440 | tf_op jit(solution)/shard_map/ppermute | solution.py:143
  106.6 9.9 %collective-permute-start.27 = (bf16[512,256]{1,0:T(8,128)(2,1)S(1)}, bf16[512,256]{1,0:T(8,128)(2,1)S(1)}, u32[]{:S(2)}, u32[]{:S(2)}) collective-permute-start(bf16[512,256]{1,0:T(8,128)(2,1)S(1)} %get-tuple-element.70), channel_id=1, source_target_pairs={{96,0},{104,8},{112,16},{120,24},{0,32},{8,40},{16,48},{24,56},{32... | collective-permute-start | bytes 786440 | tf_op jit(solution)/shard_map/ppermute | solution.py:143
  109.9 27.5 %collective-permute-start.21 = (bf16[1024,256]{1,0:T(8,128)(2,1)S(1)}, bf16[1024,256]{1,0:T(8,128)(2,1)}, u32[]{:S(2)}, u32[]{:S(2)}) collective-permute-start(bf16[1024,256]{1,0:T(8,128)(2,1)S(1)} %get-tuple-element.65), channel_id=1, source_target_pairs={{24,0},{0,8},{8,16},{16,24},{56,32},{32,40},{40,48},{48,56},{88,64... | collective-permute-start | bytes 1572872 | tf_op jit(solution)/shard_map/ppermute | solution.py:143
  113.9 23.6 %collective-permute-start.22 = (bf16[1024,256]{1,0:T(8,128)(2,1)S(1)}, bf16[1024,256]{1,0:T(8,128)(2,1)}, u32[]{:S(2)}, u32[]{:S(2)}) collective-permute-start(bf16[1024,256]{1,0:T(8,128)(2,1)S(1)} %get-tuple-element.66), channel_id=1, source_target_pairs={{16,0},{24,8},{0,16},{8,24},{48,32},{56,40},{32,48},{40,56},{80,64... | collective-permute-start | bytes 1572872 | tf_op jit(solution)/shard_map/ppermute | solution.py:143
  116.1 21.9 %collective-permute-start.23 = (bf16[1024,256]{1,0:T(8,128)(2,1)S(1)}, bf16[1024,256]{1,0:T(8,128)(2,1)}, u32[]{:S(2)}, u32[]{:S(2)}) collective-permute-start(bf16[1024,256]{1,0:T(8,128)(2,1)S(1)} %get-tuple-element.67), channel_id=1, source_target_pairs={{8,0},{16,8},{24,16},{0,24},{40,32},{48,40},{56,48},{32,56},{72,64... | collective-permute-start | bytes 1572872 | tf_op jit(solution)/shard_map/ppermute | solution.py:143
  119.1 10.6 %all-to-all-start.1 = ((f32[8,16,256]{2,1,0:T(8,128)}), f32[8,16,256]{2,1,0:T(8,128)S(1)}, u32[]{:S(2)}, u32[]{:S(2)}) async-start(f32[8,16,256]{2,1,0:T(8,128)} %broadcast_in_dim.132), calls=%async_computation.1 | async-start | bytes 262144 | tf_op jit(solution)/shard_map/all_to_all | solution.py:225
  123.5 21.5 %collective-permute-start.29 = (bf16[1024,256]{1,0:T(8,128)(2,1)}, bf16[1024,256]{1,0:T(8,128)(2,1)}, u32[]{:S(2)}, u32[]{:S(2)}) collective-permute-start(bf16[1024,256]{1,0:T(8,128)(2,1)} %pad_maximum_fusion.2), channel_id=1, source_target_pairs={{96,0},{104,8},{112,16},{120,24},{0,32},{8,40},{16,48},{24,56},{32... | collective-permute-start | bytes 1572872 | tf_op jit(solution)/shard_map/ppermute | solution.py:143
  125.2 19.7 %collective-permute-start.30 = (bf16[1024,256]{1,0:T(8,128)(2,1)}, bf16[1024,256]{1,0:T(8,128)(2,1)}, u32[]{:S(2)}, u32[]{:S(2)}) collective-permute-start(bf16[1024,256]{1,0:T(8,128)(2,1)} %pad_maximum_fusion.3), channel_id=1, source_target_pairs={{32,0},{40,8},{48,16},{56,24},{64,32},{72,40},{80,48},{88,56},{96,... | collective-permute-start | bytes 1572872 | tf_op jit(solution)/shard_map/ppermute | solution.py:143
  130.4 14.6 %all-to-all-start.2 = ((f32[16,16,256]{2,1,0:T(8,128)}), f32[16,16,256]{2,1,0:T(8,128)S(1)}, u32[]{:S(2)}, u32[]{:S(2)}) async-start(f32[16,16,256]{2,1,0:T(8,128)} %broadcast_in_dim.133), calls=%async_computation.2 | async-start | bytes 524288 | tf_op jit(solution)/shard_map/all_to_all | solution.py:225
  139.8 9.9 %collective-permute-start.24 = (bf16[256,256]{1,0:T(8,128)(2,1)S(1)}, bf16[256,256]{1,0:T(8,128)(2,1)S(1)}, u32[]{:S(2)}, u32[]{:S(2)}) collective-permute-start(bf16[256,256]{1,0:T(8,128)(2,1)S(1)} %get-tuple-element.103), channel_id=1, source_target_pairs={{96,0},{104,8},{112,16},{120,24},{0,32},{8,40},{16,48},{24,56},{32... | collective-permute-start | bytes 393224 | tf_op jit(solution)/shard_map/ppermute | solution.py:143
  (18 other events, 225.6 us)

commit v5 on v4

--- a/solution.py
+++ b/solution.py
@@ -106,7 +106,7 @@
             pltpu.SemaphoreType.DMA,
             pltpu.SemaphoreType.DMA((DEPTH,)),
         ],
-        compiler_params=pltpu.CompilerParams(vmem_limit_bytes=49 * MIB),
+        compiler_params=pltpu.CompilerParams(vmem_limit_bytes=45 * MIB),
         cost_estimate=pl.CostEstimate(
             flops=2 * values.shape[0] * EDGE * EDGE * width,
             bytes_accessed=2 * values.shape[0] * EDGE * EDGE,
@@ -249,17 +249,17 @@
 
     up, down, strips = lax.optimization_barrier((up, down, strips))
     from_up, from_down = ring_z(up, shift=3), ring_z(down, shift=1)
-    strip = jnp.sum(strips, axis=0) * factor
+    strip = jnp.sum(strips, axis=0)
     strip = jnp.sum(trade(jnp.broadcast_to(strip[None], (n_rep, *strip.shape)), "rep"), axis=0)
-    strips = trade(jnp.broadcast_to(strip[None], (n_row, *strip.shape)), "row")
-    grad_weight = strips.reshape(-1, width)
-
-    near_sum = cut(add(parts[0], near_first), half_rows)
-    far_first = near_sum[:1] + [c.astype(bf16) for c in near_sum[1:]]
+    grad_weight = trade(jnp.broadcast_to(strip[None], (n_row, *strip.shape)), "row")
+
+    far_first = cut(add(parts[0], near_first).astype(bf16), half_rows)
     far_first_got = send(far_first, ring_z)
-    near_sum = cut(own_z + from_up.astype(f32) + from_down.astype(f32), half_rows)
-    far_second = near_sum[:1] + [c.astype(bf16) for c in near_sum[1:]]
+    far_second = own_z + from_up.astype(f32) + from_down.astype(f32)
+    far_second = cut(far_second.astype(bf16), half_rows)
     far_second_got = send(far_second, ring_x)
+    grad_weight, far_second_got = lax.optimization_barrier((grad_weight, far_second_got))
+    grad_weight = grad_weight.reshape(-1, width) * factor
     totals = [add(far_first[0], far_first_got), add(far_second[0], far_second_got)]
     grad_features = jnp.concatenate(totals).astype(bf16)
     return output, grad_features, grad_weight

time: 160 us -> 156 us (0.975); the launches traced: 158 us -> 156 us
  starting transfers between devices: 66.6 us -> 55.6 us
  waiting for transfers between devices: 36 us -> 42.8 us
  Pallas kernels: 14.1 us -> 17 us
  blocking collectives: 13.1 us -> 14.8 us
    ppermute x32, waiting for transfers between devices: 26.2 us -> 34.7 us  [from_ring(): return lax.ppermute(value, axis, pairs)]
    ppermute x32, starting transfers between devices: 56.1 us -> 47.9 us  [from_ring(): return lax.ppermute(value, axis, pairs)]
    another operation x4 -> x2, other arithmetic: 3.2 us -> 0.14 us
    convert_element_type x0 -> x2, other arithmetic: none -> 2.94 us  [the longest x1 1.58 us: shards(): far_first = cut(add(parts[0], near_first).astype(bf16), half_rows)]
    pallas_call x2, Pallas kernels: 14.1 us -> 17 us  [spmm(): pl.pallas_call(functools.partial(spmm_body, transposed, splits, len(piece...]
    all_to_all x2, starting transfers between devices: 10.3 us -> 7.51 us  [trade(): return lax.all_to_all(value, axis, 0, 0, tiled=True)]
    unnamed x16 -> x9, local copies, waits for them, and re-layouts: 1.74 us -> 0.05 us
    all_to_all x1, blocking collectives: 13.1 us -> 14.8 us  [trade(): return lax.all_to_all(value, axis, 0, 0, tiled=True)]
  transfers between devices with their start and end apart: 36 -> 36, of which waited for: 12 -> 15; matrix products, arithmetic and copies ran while one was open for 11% -> 12% of each run, Pallas kernels for 0% -> 0%
where the time goes in v5:
time: 156 us
  starting transfers between devices  55.6 us (36%)
  waiting for transfers between devices  42.8 us (27%)
  Pallas kernels  17 us (11%)
  blocking collectives  14.8 us (9%)
  other arithmetic  13.9 us (9%)
  local copies, waits for them, and re-layouts  7.09 us (5%)
  between operations  2.93 us (2%)
  matrix products  1.62 us (1%)
    ppermute x32, starting transfers between devices, from_ring(): return lax.ppermute(value, axis, pairs)  47.9 us
    ppermute x32, waiting for transfers between devices, from_ring(): return lax.ppermute(value, axis, pairs)  34.7 us
    pallas_call x2, Pallas kernels, spmm(): pl.pallas_call(functools.partial(spmm_body, transposed, splits, len(piece...  17 us
    all_to_all x1, blocking collectives, trade(): return lax.all_to_all(value, axis, 0, 0, tiled=True)  14.8 us
    all_to_all x2, starting transfers between devices, trade(): return lax.all_to_all(value, axis, 0, 0, tiled=True)  7.51 us
    ppermute x2, waiting for transfers between devices, other_core(): return lax.ppermute(value, 'rep', [(i, i ^ 1) for i in range(RING * CORES)])  5.29 us
  transfers between devices with their start and end apart: 36, of which 15 were waited for; matrix products, arithmetic and copies ran while one was open for 12% of the time, Pallas kernels for 0%

profile of v5, /device:TPU:0, one launch (start us, length us, event | category | flops | bytes accessed | tf_op | source)
XLA Modules:
  0.0 155.7 jit_solution(8124855806425159459)
XLA Ops:
  3.3 2.7 %collective-permute-start.1 = (bf16[256,256]{1,0:T(8,128)(2,1)S(1)}, bf16[256,256]{1,0:T(8,128)(2,1)S(1)}, u32[]{:S(2)}, u32[]{:S(2)}) collective-permute-start(bf16[256,256]{1,0:T(8,128)(2,1)S(1)} %get-tuple-element.45), channel_id=1, source_target_pairs={{16,0},{24,8},{0,16},{8,24},{48,32},{56,40},{32,48},{40,56},{80,64... | collective-permute-start | bytes 393224 | tf_op jit(solution)/shard_map/ppermute | solution.py:143
  9.4 3.6 %collective-permute-start.7 = (bf16[256,256]{1,0:T(8,128)(2,1)S(1)}, bf16[256,256]{1,0:T(8,128)(2,1)S(1)}, u32[]{:S(2)}, u32[]{:S(2)}) collective-permute-start(bf16[256,256]{1,0:T(8,128)(2,1)S(1)} %get-tuple-element.115), channel_id=1, source_target_pairs={{64,0},{72,8},{80,16},{88,24},{96,32},{104,40},{112,48},{120,56},{... | collective-permute-start | bytes 393224 | tf_op jit(solution)/shard_map/ppermute | solution.py:143
  26.1 8.0 %collective-permute-done.11.refs_8_ = bf16[1024,256]{1,0:T(8,128)(2,1)S(1)} collective-permute-done((bf16[1024,256]{1,0:T(8,128)(2,1)S(1)}, bf16[1024,256]{1,0:T(8,128)(2,1)S(1)}, u32[]{:S(2)}, u32[]{:S(2)}) %collective-permute-start.11) | collective-permute-done | bytes 524320 | tf_op jit(solution)/shard_map/ppermute | solution.py:143
  35.8 3.0 %collective-permute-start.10 = (bf16[512,256]{1,0:T(8,128)(2,1)}, bf16[512,256]{1,0:T(8,128)(2,1)}, u32[]{:S(2)}, u32[]{:S(2)}) collective-permute-start(bf16[512,256]{1,0:T(8,128)(2,1)} %slice.88), channel_id=1, source_target_pairs={{8,0},{16,8},{24,16},{0,24},{40,32},{48,40},{56,48},{32,56},{72,64... | collective-permute-start | bytes 786440 | tf_op jit(solution)/shard_map/ppermute | solution.py:143
  45.5 8.1 %shard_map.103 = (f32[2048,256]{1,0:T(8,128)S(1)}, bf16[2048,256]{1,0:T(8,128)(2,1)S(1)}) custom-call(s32[1041]{0:T(1024)S(1)} %concatenate.27.table, bf16[384,128,128]{2,1,0:T(8,128)(2,1)} %values.3, bf16[1024,256]{1,0:T(8,128)(2,1)S(1)} %constant_dynamic-update-slice_fusion.refs_0_, bf16[1024,256]{1,0:T(8,128)(2,1)} %collective-permute-done.3.refs_1_, ...), custom_call_target="tpu_custom_call" | custom-call | flops 3221225472 | bytes 12582912 | tf_op jit(solution)/shard_map/pallas_call | solution.py:95
  53.7 2.6 %collective-permute-done.13 = bf16[2048,256]{1,0:T(8,128)(2,1)S(1)} collective-permute-done((bf16[2048,256]{1,0:T(8,128)(2,1)S(1)}, bf16[2048,256]{1,0:T(8,128)(2,1)S(1)}, u32[]{:S(2)}, u32[]{:S(2)}) %collective-permute-start.13) | collective-permute-done | bytes 1048608 | tf_op jit(solution)/shard_map/ppermute | solution.py:147
  60.2 6.4 %collective-permute-done.14 = bf16[512,256]{1,0:T(8,128)(2,1)S(1)} collective-permute-done((bf16[512,256]{1,0:T(8,128)(2,1)S(1)}, bf16[512,256]{1,0:T(8,128)(2,1)S(1)}, u32[]{:S(2)}, u32[]{:S(2)}) %collective-permute-start.14) | collective-permute-done | bytes 262176 | tf_op jit(solution)/shard_map/ppermute | solution.py:143
  66.6 4.5 %collective-permute-done.16 = bf16[512,256]{1,0:T(8,128)(2,1)S(1)} collective-permute-done((bf16[512,256]{1,0:T(8,128)(2,1)S(1)}, bf16[512,256]{1,0:T(8,128)(2,1)S(1)}, u32[]{:S(2)}, u32[]{:S(2)}) %collective-permute-start.16) | collective-permute-done | bytes 262176 | tf_op jit(solution)/shard_map/ppermute | solution.py:143
  74.9 2.9 %collective-permute-start.18 = (bf16[512,256]{1,0:T(8,128)(2,1)S(1)}, bf16[512,256]{1,0:T(8,128)(2,1)S(1)}, u32[]{:S(2)}, u32[]{:S(2)}) collective-permute-start(bf16[512,256]{1,0:T(8,128)(2,1)S(1)} %convolution_convert_fusion.refs_0_), channel_id=1, source_target_pairs={{4,0},{5,1},{6,2},{7,3},{0,4},{1,5},{2,6},{3,7},{12,8},{13,9},{14,... | collective-permute-start | bytes 786440 | tf_op jit(solution)/shard_map/ppermute | solution.py:143
  78.1 14.8 %all_to_all.15 = f32[16,16,256]{2,1,0:T(8,128)} all-to-all(f32[16,16,256]{2,1,0:T(8,128)S(1)} %bitcast.14), channel_id=1, replica_groups=mesh['row'=16,'rep'=8] {'row'}, dimensions={0} | all-to-all | bytes 524288 | tf_op jit(solution)/shard_map/all_to_all | solution.py:225
  93.0 2.6 %collective-permute-done.20.refs_4_ = bf16[2048,256]{1,0:T(8,128)(2,1)S(1)} collective-permute-done((bf16[2048,256]{1,0:T(8,128)(2,1)S(1)}, bf16[2048,256]{1,0:T(8,128)(2,1)S(1)}, u32[]{:S(2)}, u32[]{:S(2)}) %collective-permute-start.20) | collective-permute-done | bytes 1048608 | tf_op jit(solution)/shard_map/ppermute | solution.py:147
  95.7 8.9 %shard_map.104 = (f32[1024,256]{1,0:T(8,128)S(1)}, bf16[1024,256]{1,0:T(8,128)(2,1)}, bf16[1024,256]{1,0:T(8,128)(2,1)S(1)}, bf16[1024,256]{1,0:T(8,128)(2,1)S(1...) custom-call(s32[1121]{0:T(1024)S(1)} %concatenate.28.table, ...), custom_call_target="tpu_custom_call" | custom-call | flops 3221225472 | bytes 12582912 | tf_op jit(solution)/shard_map/pallas_call | solution.py:95
  105.4 2.5 %collective-permute-start.28 = (bf16[512,256]{1,0:T(8,128)(2,1)S(1)}, bf16[512,256]{1,0:T(8,128)(2,1)S(1)}, u32[]{:S(2)}, u32[]{:S(2)}) collective-permute-start(bf16[512,256]{1,0:T(8,128)(2,1)S(1)} %get-tuple-element.78), channel_id=1, source_target_pairs={{32,0},{40,8},{48,16},{56,24},{64,32},{72,40},{80,48},{88,56},{96,... | collective-permute-start | bytes 786440 | tf_op jit(solution)/shard_map/ppermute | solution.py:143
  108.8 2.5 %collective-permute-start.23 = (bf16[1024,256]{1,0:T(8,128)(2,1)S(1)}, bf16[1024,256]{1,0:T(8,128)(2,1)}, u32[]{:S(2)}, u32[]{:S(2)}) collective-permute-start(bf16[1024,256]{1,0:T(8,128)(2,1)S(1)} %get-tuple-element.71), channel_id=1, source_target_pairs={{8,0},{16,8},{24,16},{0,24},{40,32},{48,40},{56,48},{32,56},{72,64... | collective-permute-start | bytes 1572872 | tf_op jit(solution)/shard_map/ppermute | solution.py:143
  111.3 2.5 %collective-permute-done.27 = bf16[512,256]{1,0:T(8,128)(2,1)S(1)} collective-permute-done((bf16[512,256]{1,0:T(8,128)(2,1)S(1)}, bf16[512,256]{1,0:T(8,128)(2,1)S(1)}, u32[]{:S(2)}, u32[]{:S(2)}) %collective-permute-start.27) | collective-permute-done | bytes 262176 | tf_op jit(solution)/shard_map/ppermute | solution.py:143
  117.3 3.4 %all-to-all-start.1 = ((f32[8,16,256]{2,1,0:T(8,128)}), f32[8,16,256]{2,1,0:T(8,128)S(1)}, u32[]{:S(2)}, u32[]{:S(2)}) async-start(f32[8,16,256]{2,1,0:T(8,128)} %broadcast_in_dim.132), calls=%async_computation.1 | async-start | bytes 262144 | tf_op jit(solution)/shard_map/all_to_all | solution.py:225
  120.8 3.2 %collective-permute-start.30 = (bf16[1024,256]{1,0:T(8,128)(2,1)}, bf16[1024,256]{1,0:T(8,128)(2,1)}, u32[]{:S(2)}, u32[]{:S(2)}) collective-permute-start(bf16[1024,256]{1,0:T(8,128)(2,1)} %pad_maximum_fusion.3), channel_id=1, source_target_pairs={{32,0},{40,8},{48,16},{56,24},{64,32},{72,40},{80,48},{88,56},{96,... | collective-permute-start | bytes 1572872 | tf_op jit(solution)/shard_map/ppermute | solution.py:143
  124.0 2.7 %all-to-all-done.1 = f32[8,16,256]{2,1,0:T(8,128)S(1)} async-done(((f32[8,16,256]{2,1,0:T(8,128)}), f32[8,16,256]{2,1,0:T(8,128)S(1)}, u32[]{:S(2)}, u32[]{:S(2)}) %all-to-all-start.1) | async-done | bytes 131104 | tf_op jit(solution)/shard_map/all_to_all | solution.py:225
  127.4 4.1 %all-to-all-start.2 = ((f32[16,16,256]{2,1,0:T(8,128)}), f32[16,16,256]{2,1,0:T(8,128)S(1)}, u32[]{:S(2)}, u32[]{:S(2)}) async-start(f32[16,16,256]{2,1,0:T(8,128)} %broadcast_in_dim.133), calls=%async_computation.2 | async-start | bytes 524288 | tf_op jit(solution)/shard_map/all_to_all | solution.py:225
  131.6 3.3 %collective-permute-done.21 = bf16[1024,256]{1,0:T(8,128)(2,1)} collective-permute-done((bf16[1024,256]{1,0:T(8,128)(2,1)}, bf16[1024,256]{1,0:T(8,128)(2,1)}, u32[]{:S(2)}, u32[]{:S(2)}) %collective-permute-start.21) | collective-permute-done | bytes 524320 | tf_op jit(solution)/shard_map/ppermute | solution.py:143
  137.5 3.2 %collective-permute-start.26 = (bf16[256,256]{1,0:T(8,128)(2,1)S(1)}, bf16[256,256]{1,0:T(8,128)(2,1)S(1)}, u32[]{:S(2)}, u32[]{:S(2)}) collective-permute-start(bf16[256,256]{1,0:T(8,128)(2,1)S(1)} %get-tuple-element.108), channel_id=1, source_target_pairs={{32,0},{40,8},{48,16},{56,24},{64,32},{72,40},{80,48},{88,56},{96,... | collective-permute-start | bytes 393224 | tf_op jit(solution)/shard_map/ppermute | solution.py:143
  142.1 2.9 %collective-permute-start.33 = (bf16[256,256]{1,0:T(8,128)(2,1)S(1)}, bf16[256,256]{1,0:T(8,128)(2,1)S(1)}, u32[]{:S(2)}, u32[]{:S(2)}) collective-permute-start(bf16[256,256]{1,0:T(8,128)(2,1)S(1)} %get-tuple-element.110), channel_id=1, source_target_pairs={{8,0},{16,8},{24,16},{0,24},{40,32},{48,40},{56,48},{32,56},{72,64... | collective-permute-start | bytes 393224 | tf_op jit(solution)/shard_map/ppermute | solution.py:143
  147.9 2.8 %collective-permute-done.33 = bf16[256,256]{1,0:T(8,128)(2,1)S(1)} collective-permute-done((bf16[256,256]{1,0:T(8,128)(2,1)S(1)}, bf16[256,256]{1,0:T(8,128)(2,1)S(1)}, u32[]{:S(2)}, u32[]{:S(2)}) %collective-permute-start.33) | collective-permute-done | bytes 131104 | tf_op jit(solution)/shard_map/ppermute | solution.py:143
  150.7 2.3 %collective-permute-done.32 = bf16[256,256]{1,0:T(8,128)(2,1)S(1)} collective-permute-done((bf16[256,256]{1,0:T(8,128)(2,1)S(1)}, bf16[256,256]{1,0:T(8,128)(2,1)S(1)}, u32[]{:S(2)}, u32[]{:S(2)}) %collective-permute-start.32) | collective-permute-done | bytes 131104 | tf_op jit(solution)/shard_map/ppermute | solution.py:143
  (108 shorter events, 49.2 us)
Async XLA Ops:
  1.7 12.0 %collective-permute-start.2 = (bf16[256,256]{1,0:T(8,128)(2,1)S(1)}, bf16[256,256]{1,0:T(8,128)(2,1)S(1)}, u32[]{:S(2)}, u32[]{:S(2)}) collective-permute-start(bf16[256,256]{1,0:T(8,128)(2,1)S(1)} %get-tuple-element.45), channel_id=1, source_target_pairs={{24,0},{0,8},{8,16},{16,24},{56,32},{32,40},{40,48},{48,56},{88,64... | collective-permute-start | bytes 393224 | tf_op jit(solution)/shard_map/ppermute | solution.py:143
  3.3 11.4 %collective-permute-start.1 = (bf16[256,256]{1,0:T(8,128)(2,1)S(1)}, bf16[256,256]{1,0:T(8,128)(2,1)S(1)}, u32[]{:S(2)}, u32[]{:S(2)}) collective-permute-start(bf16[256,256]{1,0:T(8,128)(2,1)S(1)} %get-tuple-element.45), channel_id=1, source_target_pairs={{16,0},{24,8},{0,16},{8,24},{48,32},{56,40},{32,48},{40,56},{80,64... | collective-permute-start | bytes 393224 | tf_op jit(solution)/shard_map/ppermute | solution.py:143
  7.5 12.2 %collective-permute-start.8 = (bf16[256,256]{1,0:T(8,128)(2,1)S(1)}, bf16[256,256]{1,0:T(8,128)(2,1)S(1)}, u32[]{:S(2)}, u32[]{:S(2)}) collective-permute-start(bf16[256,256]{1,0:T(8,128)(2,1)S(1)} %get-tuple-element.115), channel_id=1, source_target_pairs={{96,0},{104,8},{112,16},{120,24},{0,32},{8,40},{16,48},{24,56},{32... | collective-permute-start | bytes 393224 | tf_op jit(solution)/shard_map/ppermute | solution.py:143
  9.4 11.4 %collective-permute-start.7 = (bf16[256,256]{1,0:T(8,128)(2,1)S(1)}, bf16[256,256]{1,0:T(8,128)(2,1)S(1)}, u32[]{:S(2)}, u32[]{:S(2)}) collective-permute-start(bf16[256,256]{1,0:T(8,128)(2,1)S(1)} %get-tuple-element.115), channel_id=1, source_target_pairs={{64,0},{72,8},{80,16},{88,24},{96,32},{104,40},{112,48},{120,56},{... | collective-permute-start | bytes 393224 | tf_op jit(solution)/shard_map/ppermute | solution.py:143
  14.8 30.6 %collective-permute-start.5 = (bf16[1024,256]{1,0:T(8,128)(2,1)S(1)}, bf16[1024,256]{1,0:T(8,128)(2,1)S(1)}, u32[]{:S(2)}, u32[]{:S(2)}) collective-permute-start(bf16[1024,256]{1,0:T(8,128)(2,1)S(1)} %constant_dynamic-update-slice_fusion.refs_0_), channel_id=1, source_target_pairs={{96,0},{104,8},{112,16},{120,24},{0,32},{8,40},{16,48},{24,56},{32... | collective-permute-start | bytes 1572872 | tf_op jit(solution)/shard_map/ppermute | solution.py:143
  15.9 29.5 %collective-permute-start.4 = (bf16[1024,256]{1,0:T(8,128)(2,1)S(1)}, bf16[1024,256]{1,0:T(8,128)(2,1)S(1)}, u32[]{:S(2)}, u32[]{:S(2)}) collective-permute-start(bf16[1024,256]{1,0:T(8,128)(2,1)S(1)} %constant_dynamic-update-slice_fusion.refs_0_), channel_id=1, source_target_pairs={{64,0},{72,8},{80,16},{88,24},{96,32},{104,40},{112,48},{120,56},{... | collective-permute-start | bytes 1572872 | tf_op jit(solution)/shard_map/ppermute | solution.py:143
  19.7 25.7 %collective-permute-start.3 = (bf16[1024,256]{1,0:T(8,128)(2,1)S(1)}, bf16[1024,256]{1,0:T(8,128)(2,1)}, u32[]{:S(2)}, u32[]{:S(2)}) collective-permute-start(bf16[1024,256]{1,0:T(8,128)(2,1)S(1)} %constant_dynamic-update-slice_fusion.refs_0_), channel_id=1, source_target_pairs={{32,0},{40,8},{48,16},{56,24},{64,32},{72,40},{80,48},{88,56},{96,... | collective-permute-start | bytes 1572872 | tf_op jit(solution)/shard_map/ppermute | solution.py:143
  20.8 13.2 %collective-permute-start.11 = (bf16[1024,256]{1,0:T(8,128)(2,1)S(1)}, bf16[1024,256]{1,0:T(8,128)(2,1)S(1)}, u32[]{:S(2)}, u32[]{:S(2)}) collective-permute-start(bf16[1024,256]{1,0:T(8,128)(2,1)S(1)} %pad_maximum_fusion.1.refs_4_), channel_id=1, source_target_pairs={{24,0},{0,8},{8,16},{16,24},{56,32},{32,40},{40,48},{48,56},{88,64... | collective-permute-start | bytes 1572872 | tf_op jit(solution)/shard_map/ppermute | solution.py:143
  22.2 12.8 %collective-permute-start.9 = (bf16[1024,256]{1,0:T(8,128)(2,1)S(1)}, bf16[1024,256]{1,0:T(8,128)(2,1)S(1)}, u32[]{:S(2)}, u32[]{:S(2)}) collective-permute-start(bf16[1024,256]{1,0:T(8,128)(2,1)S(1)} %pad_maximum_fusion.1.refs_4_), channel_id=1, source_target_pairs={{8,0},{16,8},{24,16},{0,24},{40,32},{48,40},{56,48},{32,56},{72,64... | collective-permute-start | bytes 1572872 | tf_op jit(solution)/shard_map/ppermute | solution.py:143
  34.8 10.6 %collective-permute-start.12 = (bf16[512,256]{1,0:T(8,128)(2,1)}, bf16[512,256]{1,0:T(8,128)(2,1)S(1)}, u32[]{:S(2)}, u32[]{:S(2)}) collective-permute-start(bf16[512,256]{1,0:T(8,128)(2,1)} %slice.89), channel_id=1, source_target_pairs={{24,0},{0,8},{8,16},{16,24},{56,32},{32,40},{40,48},{48,56},{88,64... | collective-permute-start | bytes 786440 | tf_op jit(solution)/shard_map/ppermute | solution.py:143
  35.8 9.7 %collective-permute-start.10 = (bf16[512,256]{1,0:T(8,128)(2,1)}, bf16[512,256]{1,0:T(8,128)(2,1)}, u32[]{:S(2)}, u32[]{:S(2)}) collective-permute-start(bf16[512,256]{1,0:T(8,128)(2,1)} %slice.88), channel_id=1, source_target_pairs={{8,0},{16,8},{24,16},{0,24},{40,32},{48,40},{56,48},{32,56},{72,64... | collective-permute-start | bytes 786440 | tf_op jit(solution)/shard_map/ppermute | solution.py:143
  56.5 10.1 %collective-permute-start.14 = (bf16[512,256]{1,0:T(8,128)(2,1)S(1)}, bf16[512,256]{1,0:T(8,128)(2,1)S(1)}, u32[]{:S(2)}, u32[]{:S(2)}) collective-permute-start(bf16[512,256]{1,0:T(8,128)(2,1)S(1)} %get-tuple-element.104), channel_id=1, source_target_pairs={{6,0},{7,1},{0,2},{1,3},{2,4},{3,5},{4,6},{5,7},{14,8},{15,9},{8,1... | collective-permute-start | bytes 786440 | tf_op jit(solution)/shard_map/ppermute | solution.py:143
  57.6 13.5 %collective-permute-start.16 = (bf16[512,256]{1,0:T(8,128)(2,1)S(1)}, bf16[512,256]{1,0:T(8,128)(2,1)S(1)}, u32[]{:S(2)}, u32[]{:S(2)}) collective-permute-start(bf16[512,256]{1,0:T(8,128)(2,1)S(1)} %get-tuple-element.105), channel_id=1, source_target_pairs={{2,0},{3,1},{4,2},{5,3},{6,4},{7,5},{0,6},{1,7},{10,8},{11,9},{12,... | collective-permute-start | bytes 786440 | tf_op jit(solution)/shard_map/ppermute | solution.py:143
  59.8 12.3 %collective-permute-start.15 = (bf16[512,256]{1,0:T(8,128)(2,1)S(1)}, bf16[512,256]{1,0:T(8,128)(2,1)S(1)}, u32[]{:S(2)}, u32[]{:S(2)}) collective-permute-start(bf16[512,256]{1,0:T(8,128)(2,1)S(1)} %get-tuple-element.106), channel_id=1, source_target_pairs={{4,0},{5,1},{6,2},{7,3},{0,4},{1,5},{2,6},{3,7},{12,8},{13,9},{14,... | collective-permute-start | bytes 786440 | tf_op jit(solution)/shard_map/ppermute | solution.py:143
  73.6 19.2 %collective-permute-start.19 = (bf16[512,256]{1,0:T(8,128)(2,1)S(1)}, bf16[512,256]{1,0:T(8,128)(2,1)S(1)}, u32[]{:S(2)}, u32[]{:S(2)}) collective-permute-start(bf16[512,256]{1,0:T(8,128)(2,1)S(1)} %convolution_convert_fusion.refs_0_), channel_id=1, source_target_pairs={{6,0},{7,1},{0,2},{1,3},{2,4},{3,5},{4,6},{5,7},{14,8},{15,9},{8,1... | collective-permute-start | bytes 786440 | tf_op jit(solution)/shard_map/ppermute | solution.py:143
  74.9 18.0 %collective-permute-start.18 = (bf16[512,256]{1,0:T(8,128)(2,1)S(1)}, bf16[512,256]{1,0:T(8,128)(2,1)S(1)}, u32[]{:S(2)}, u32[]{:S(2)}) collective-permute-start(bf16[512,256]{1,0:T(8,128)(2,1)S(1)} %convolution_convert_fusion.refs_0_), channel_id=1, source_target_pairs={{4,0},{5,1},{6,2},{7,3},{0,4},{1,5},{2,6},{3,7},{12,8},{13,9},{14,... | collective-permute-start | bytes 786440 | tf_op jit(solution)/shard_map/ppermute | solution.py:143
  77.8 15.1 %collective-permute-start.17 = (bf16[512,256]{1,0:T(8,128)(2,1)S(1)}, bf16[512,256]{1,0:T(8,128)(2,1)S(1)}, u32[]{:S(2)}, u32[]{:S(2)}) collective-permute-start(bf16[512,256]{1,0:T(8,128)(2,1)S(1)} %convolution_convert_fusion.refs_0_), channel_id=1, source_target_pairs={{2,0},{3,1},{4,2},{5,3},{6,4},{7,5},{0,6},{1,7},{10,8},{11,9},{12,... | collective-permute-start | bytes 786440 | tf_op jit(solution)/shard_map/ppermute | solution.py:143
  107.9 27.0 %collective-permute-start.21 = (bf16[1024,256]{1,0:T(8,128)(2,1)}, bf16[1024,256]{1,0:T(8,128)(2,1)}, u32[]{:S(2)}, u32[]{:S(2)}) collective-permute-start(bf16[1024,256]{1,0:T(8,128)(2,1)} %get-tuple-element.69), channel_id=1, source_target_pairs={{24,0},{0,8},{8,16},{16,24},{56,32},{32,40},{40,48},{48,56},{88,64... | collective-permute-start | bytes 1572872 | tf_op jit(solution)/shard_map/ppermute | solution.py:143
  108.6 26.2 %collective-permute-start.22 = (bf16[1024,256]{1,0:T(8,128)(2,1)S(1)}, bf16[1024,256]{1,0:T(8,128)(2,1)}, u32[]{:S(2)}, u32[]{:S(2)}) collective-permute-start(bf16[1024,256]{1,0:T(8,128)(2,1)S(1)} %get-tuple-element.70), channel_id=1, source_target_pairs={{16,0},{24,8},{0,16},{8,24},{48,32},{56,40},{32,48},{40,56},{80,64... | collective-permute-start | bytes 1572872 | tf_op jit(solution)/shard_map/ppermute | solution.py:143
  108.8 27.0 %collective-permute-start.23 = (bf16[1024,256]{1,0:T(8,128)(2,1)S(1)}, bf16[1024,256]{1,0:T(8,128)(2,1)}, u32[]{:S(2)}, u32[]{:S(2)}) collective-permute-start(bf16[1024,256]{1,0:T(8,128)(2,1)S(1)} %get-tuple-element.71), channel_id=1, source_target_pairs={{8,0},{16,8},{24,16},{0,24},{40,32},{48,40},{56,48},{32,56},{72,64... | collective-permute-start | bytes 1572872 | tf_op jit(solution)/shard_map/ppermute | solution.py:143
  117.3 9.4 %all-to-all-start.1 = ((f32[8,16,256]{2,1,0:T(8,128)}), f32[8,16,256]{2,1,0:T(8,128)S(1)}, u32[]{:S(2)}, u32[]{:S(2)}) async-start(f32[8,16,256]{2,1,0:T(8,128)} %broadcast_in_dim.132), calls=%async_computation.1 | async-start | bytes 262144 | tf_op jit(solution)/shard_map/all_to_all | solution.py:225
  120.6 20.1 %collective-permute-start.29 = (bf16[1024,256]{1,0:T(8,128)(2,1)}, bf16[1024,256]{1,0:T(8,128)(2,1)}, u32[]{:S(2)}, u32[]{:S(2)}) collective-permute-start(bf16[1024,256]{1,0:T(8,128)(2,1)} %pad_maximum_fusion.2), channel_id=1, source_target_pairs={{96,0},{104,8},{112,16},{120,24},{0,32},{8,40},{16,48},{24,56},{32... | collective-permute-start | bytes 1572872 | tf_op jit(solution)/shard_map/ppermute | solution.py:143
  120.8 19.9 %collective-permute-start.30 = (bf16[1024,256]{1,0:T(8,128)(2,1)}, bf16[1024,256]{1,0:T(8,128)(2,1)}, u32[]{:S(2)}, u32[]{:S(2)}) collective-permute-start(bf16[1024,256]{1,0:T(8,128)(2,1)} %pad_maximum_fusion.3), channel_id=1, source_target_pairs={{32,0},{40,8},{48,16},{56,24},{64,32},{72,40},{80,48},{88,56},{96,... | collective-permute-start | bytes 1572872 | tf_op jit(solution)/shard_map/ppermute | solution.py:143
  127.4 20.4 %all-to-all-start.2 = ((f32[16,16,256]{2,1,0:T(8,128)}), f32[16,16,256]{2,1,0:T(8,128)S(1)}, u32[]{:S(2)}, u32[]{:S(2)}) async-start(f32[16,16,256]{2,1,0:T(8,128)} %broadcast_in_dim.133), calls=%async_computation.2 | async-start | bytes 524288 | tf_op jit(solution)/shard_map/all_to_all | solution.py:225
  (15 other events, 183.9 us)

commit v6 on v5

--- a/solution.py
+++ b/solution.py
@@ -115,7 +115,7 @@
     )(table, values, *pieces)
 
 
-def pair_lists(live, dst, src, n_dst, n_src):
+def pair_lists(live, n_dst, dst, src, n_src):
     slots = dst.shape[0]
     room = -(-((slots + n_dst) // 2) // UNROLL) * UNROLL
     index = jnp.arange(slots, dtype=jnp.int32)
@@ -191,9 +191,12 @@
     zx, xz = dz * RING + dx, dx * RING + dz
     gathered_at = (h * n_row + jnp.where(h == 0, zx, xz)) * per_half + q % per_half
     scattered_at = (h * n_row + jnp.where(h == 0, xz, zx)) * per_half + q % per_half
-    forward = pair_lists(live, row_at, gathered_at, group_blocks, line_blocks)
-    backward = pair_lists(live, scattered_at, row_at, line_blocks, group_blocks)
-    line, forward, backward = lax.optimization_barrier((line, forward, backward))
+    tables = jax.vmap(functools.partial(pair_lists, live, max(group_blocks, line_blocks)))(
+        jnp.stack([row_at, scattered_at]),
+        jnp.stack([gathered_at, row_at]),
+        jnp.array([line_blocks, group_blocks], jnp.int32),
+    )
+    line, forward, backward = lax.optimization_barrier((line, tables[0], tables[1]))
 
     def scatter(parts, ring):
         got = {s: ring(parts[s], shift=RING - s) for s in shifts}

time: 156 us -> 155 us (level); the launches traced: 156 us -> 152 us
  starting transfers between devices: 55.6 us -> 65.7 us
  Pallas kernels: 17 us -> 12.5 us
  other arithmetic: 13.9 us -> 9.81 us
  waiting for transfers between devices: 42.8 us -> 39.3 us
    ppermute x32, starting transfers between devices: 47.9 us -> 55.3 us  [from_ring(): return lax.ppermute(value, axis, pairs)]
    pallas_call x2, Pallas kernels: 17 us -> 12.5 us  [spmm(): pl.pallas_call(functools.partial(spmm_body, transposed, splits, len(piece...]
    ppermute x32, waiting for transfers between devices: 34.7 us -> 31.1 us  [from_ring(): return lax.ppermute(value, axis, pairs)]
    all_to_all x2, starting transfers between devices: 7.51 us -> 10.1 us  [trade(): return lax.all_to_all(value, axis, 0, 0, tiled=True)]
  transfers between devices with their start and end apart: 36 -> 36, of which waited for: 15 -> 19; matrix products, arithmetic and copies ran while one was open for 12% -> 8% of each run, Pallas kernels for 0% -> 0%
where the time goes in v6:
time: 155 us; the launch traced here: 152 us
  starting transfers between devices  65.7 us (42%)
  waiting for transfers between devices  39.3 us (25%)
  blocking collectives  16.1 us (10%)
  Pallas kernels  12.5 us (8%)
  other arithmetic  9.81 us (6%)
  local copies, waits for them, and re-layouts  5.69 us (4%)
  between operations  1.67 us (1%)
  matrix products  1.61 us (1%)
    ppermute x32, starting transfers between devices, from_ring(): return lax.ppermute(value, axis, pairs)  55.3 us
    ppermute x32, waiting for transfers between devices, from_ring(): return lax.ppermute(value, axis, pairs)  31.1 us
    all_to_all x1, blocking collectives, trade(): return lax.all_to_all(value, axis, 0, 0, tiled=True)  16.1 us
    pallas_call x2, Pallas kernels, spmm(): pl.pallas_call(functools.partial(spmm_body, transposed, splits, len(piece...  12.5 us
    all_to_all x2, starting transfers between devices, trade(): return lax.all_to_all(value, axis, 0, 0, tiled=True)  10.1 us
    ppermute x2, waiting for transfers between devices, other_core(): return lax.ppermute(value, 'rep', [(i, i ^ 1) for i in range(RING * CORES)])  5.29 us
  transfers between devices with their start and end apart: 36, of which 19 were waited for; matrix products, arithmetic and copies ran while one was open for 8% of the time, Pallas kernels for 0%

profile of v6, /device:TPU:0, one launch (start us, length us, event | category | flops | bytes accessed | tf_op | source)
XLA Modules:
  0.0 152.4 jit_solution(14792808781618191169)
XLA Ops:
  3.8 3.6 %collective-permute-start.7 = (bf16[256,256]{1,0:T(8,128)(2,1)S(1)}, bf16[256,256]{1,0:T(8,128)(2,1)S(1)}, u32[]{:S(2)}, u32[]{:S(2)}) collective-permute-start(bf16[256,256]{1,0:T(8,128)(2,1)S(1)} %get-tuple-element.108), channel_id=1, source_target_pairs={{64,0},{72,8},{80,16},{88,24},{96,32},{104,40},{112,48},{120,56},{... | collective-permute-start | bytes 393224 | tf_op jit(solution)/shard_map/ppermute | solution.py:143
  8.9 2.7 %collective-permute-start.1 = (bf16[256,256]{1,0:T(8,128)(2,1)S(1)}, bf16[256,256]{1,0:T(8,128)(2,1)S(1)}, u32[]{:S(2)}, u32[]{:S(2)}) collective-permute-start(bf16[256,256]{1,0:T(8,128)(2,1)S(1)} %get-tuple-element.45), channel_id=1, source_target_pairs={{16,0},{24,8},{0,16},{8,24},{48,32},{56,40},{32,48},{40,56},{80,64... | collective-permute-start | bytes 393224 | tf_op jit(solution)/shard_map/ppermute | solution.py:143
  17.3 2.5 %collective-permute-start.4 = (bf16[1024,256]{1,0:T(8,128)(2,1)S(1)}, bf16[1024,256]{1,0:T(8,128)(2,1)S(1)}, u32[]{:S(2)}, u32[]{:S(2)}) collective-permute-start(bf16[1024,256]{1,0:T(8,128)(2,1)S(1)} %constant_dynamic-update-slice_fusion.refs_0_), channel_id=1, source_target_pairs={{64,0},{72,8},{80,16},{88,24},{96,32},{104,40},{112,48},{120,56},{... | collective-permute-start | bytes 1572872 | tf_op jit(solution)/shard_map/ppermute | solution.py:143
  27.1 6.5 %collective-permute-done.11.refs_8_ = bf16[1024,256]{1,0:T(8,128)(2,1)S(1)} collective-permute-done((bf16[1024,256]{1,0:T(8,128)(2,1)S(1)}, bf16[1024,256]{1,0:T(8,128)(2,1)S(1)}, u32[]{:S(2)}, u32[]{:S(2)}) %collective-permute-start.11) | collective-permute-done | bytes 524320 | tf_op jit(solution)/shard_map/ppermute | solution.py:143
  35.1 3.2 %collective-permute-start.10 = (bf16[512,256]{1,0:T(8,128)(2,1)}, bf16[512,256]{1,0:T(8,128)(2,1)}, u32[]{:S(2)}, u32[]{:S(2)}) collective-permute-start(bf16[512,256]{1,0:T(8,128)(2,1)} %slice.92), channel_id=1, source_target_pairs={{8,0},{16,8},{24,16},{0,24},{40,32},{48,40},{56,48},{32,56},{72,64... | collective-permute-start | bytes 786440 | tf_op jit(solution)/shard_map/ppermute | solution.py:143
  42.6 5.8 %shard_map.112 = (f32[2048,256]{1,0:T(8,128)S(1)}, bf16[2048,256]{1,0:T(8,128)(2,1)S(1)}) custom-call(s32[1121]{0:T(1024)S(1)} %get-tuple-element.51.table, bf16[384,128,128]{2,1,0:T(8,128)(2,1)} %values.3, bf16[1024,256]{1,0:T(8,128)(2,1)S(1)} %constant_dynamic-update-slice_fusion.refs_0_, bf16[1024,256]{1,0:T(8,128)(2,1)} %collective-permute-done.3.refs_1_, ...), custom_call_target="tpu_custom_call" | custom-call | flops 3221225472 | bytes 12582912 | tf_op jit(solution)/shard_map/pallas_call | solution.py:95
  48.5 2.6 %collective-permute-done.13 = bf16[2048,256]{1,0:T(8,128)(2,1)S(1)} collective-permute-done((bf16[2048,256]{1,0:T(8,128)(2,1)S(1)}, bf16[2048,256]{1,0:T(8,128)(2,1)S(1)}, u32[]{:S(2)}, u32[]{:S(2)}) %collective-permute-start.13) | collective-permute-done | bytes 1048608 | tf_op jit(solution)/shard_map/ppermute | solution.py:147
  51.4 5.1 %collective-permute-start.14 = (bf16[512,256]{1,0:T(8,128)(2,1)S(1)}, bf16[512,256]{1,0:T(8,128)(2,1)S(1)}, u32[]{:S(2)}, u32[]{:S(2)}) collective-permute-start(bf16[512,256]{1,0:T(8,128)(2,1)S(1)} %get-tuple-element.97), channel_id=1, source_target_pairs={{6,0},{7,1},{0,2},{1,3},{2,4},{3,5},{4,6},{5,7},{14,8},{15,9},{8,1... | collective-permute-start | bytes 786440 | tf_op jit(solution)/shard_map/ppermute | solution.py:143
  58.6 4.5 %collective-permute-done.14 = bf16[512,256]{1,0:T(8,128)(2,1)S(1)} collective-permute-done((bf16[512,256]{1,0:T(8,128)(2,1)S(1)}, bf16[512,256]{1,0:T(8,128)(2,1)S(1)}, u32[]{:S(2)}, u32[]{:S(2)}) %collective-permute-start.14) | collective-permute-done | bytes 262176 | tf_op jit(solution)/shard_map/ppermute | solution.py:143
  63.1 2.5 %collective-permute-done.16 = bf16[512,256]{1,0:T(8,128)(2,1)S(1)} collective-permute-done((bf16[512,256]{1,0:T(8,128)(2,1)S(1)}, bf16[512,256]{1,0:T(8,128)(2,1)S(1)}, u32[]{:S(2)}, u32[]{:S(2)}) %collective-permute-start.16) | collective-permute-done | bytes 262176 | tf_op jit(solution)/shard_map/ppermute | solution.py:143
  65.7 2.7 %collective-permute-done.15 = bf16[512,256]{1,0:T(8,128)(2,1)S(1)} collective-permute-done((bf16[512,256]{1,0:T(8,128)(2,1)S(1)}, bf16[512,256]{1,0:T(8,128)(2,1)S(1)}, u32[]{:S(2)}, u32[]{:S(2)}) %collective-permute-start.15) | collective-permute-done | bytes 262176 | tf_op jit(solution)/shard_map/ppermute | solution.py:143
  72.1 3.8 %collective-permute-start.18 = (bf16[512,256]{1,0:T(8,128)(2,1)S(1)}, bf16[512,256]{1,0:T(8,128)(2,1)S(1)}, u32[]{:S(2)}, u32[]{:S(2)}) collective-permute-start(bf16[512,256]{1,0:T(8,128)(2,1)S(1)} %convolution_convert_fusion.refs_0_), channel_id=1, source_target_pairs={{4,0},{5,1},{6,2},{7,3},{0,4},{1,5},{2,6},{3,7},{12,8},{13,9},{14,... | collective-permute-start | bytes 786440 | tf_op jit(solution)/shard_map/ppermute | solution.py:143
  76.5 16.1 %all_to_all.15 = f32[16,16,256]{2,1,0:T(8,128)S(1)} all-to-all(f32[16,16,256]{2,1,0:T(8,128)S(1)} %bitcast.12), channel_id=1, replica_groups=mesh['row'=16,'rep'=8] {'row'}, dimensions={0} | all-to-all | bytes 524288 | tf_op jit(solution)/shard_map/all_to_all | solution.py:228
  92.9 2.6 %collective-permute-done.20.refs_4_ = bf16[2048,256]{1,0:T(8,128)(2,1)S(1)} collective-permute-done((bf16[2048,256]{1,0:T(8,128)(2,1)S(1)}, bf16[2048,256]{1,0:T(8,128)(2,1)S(1)}, u32[]{:S(2)}, u32[]{:S(2)}) %collective-permute-start.20) | collective-permute-done | bytes 1048608 | tf_op jit(solution)/shard_map/ppermute | solution.py:147
  95.5 6.7 %shard_map.113 = (f32[1024,256]{1,0:T(8,128)S(1)}, bf16[1024,256]{1,0:T(8,128)(2,1)}, bf16[1024,256]{1,0:T(8,128)(2,1)S(1)}, bf16[1024,256]{1,0:T(8,128)(2,1)S(1...) custom-call(s32[1121]{0:T(1024)S(1)} %get-tuple-element.63.table, ...), custom_call_target="tpu_custom_call" | custom-call | flops 3221225472 | bytes 12582912 | tf_op jit(solution)/shard_map/pallas_call | solution.py:95
  102.6 2.9 %collective-permute-start.28 = (bf16[512,256]{1,0:T(8,128)(2,1)S(1)}, bf16[512,256]{1,0:T(8,128)(2,1)S(1)}, u32[]{:S(2)}, u32[]{:S(2)}) collective-permute-start(bf16[512,256]{1,0:T(8,128)(2,1)S(1)} %get-tuple-element.78), channel_id=1, source_target_pairs={{32,0},{40,8},{48,16},{56,24},{64,32},{72,40},{80,48},{88,56},{96,... | collective-permute-start | bytes 786440 | tf_op jit(solution)/shard_map/ppermute | solution.py:143
  108.4 2.6 %collective-permute-start.23 = (bf16[1024,256]{1,0:T(8,128)(2,1)S(1)}, bf16[1024,256]{1,0:T(8,128)(2,1)}, u32[]{:S(2)}, u32[]{:S(2)}) collective-permute-start(bf16[1024,256]{1,0:T(8,128)(2,1)S(1)} %get-tuple-element.71), channel_id=1, source_target_pairs={{8,0},{16,8},{24,16},{0,24},{40,32},{48,40},{56,48},{32,56},{72,64... | collective-permute-start | bytes 1572872 | tf_op jit(solution)/shard_map/ppermute | solution.py:143
  114.3 5.0 %all-to-all-start.1 = ((f32[8,16,256]{2,1,0:T(8,128)}), f32[8,16,256]{2,1,0:T(8,128)S(1)}, u32[]{:S(2)}, u32[]{:S(2)}) async-start(f32[8,16,256]{2,1,0:T(8,128)} %broadcast_in_dim.88), calls=%async_computation.1 | async-start | bytes 262144 | tf_op jit(solution)/shard_map/all_to_all | solution.py:228
  122.5 2.9 %all-to-all-done.1 = f32[8,16,256]{2,1,0:T(8,128)S(1)} async-done(((f32[8,16,256]{2,1,0:T(8,128)}), f32[8,16,256]{2,1,0:T(8,128)S(1)}, u32[]{:S(2)}, u32[]{:S(2)}) %all-to-all-start.1) | async-done | bytes 131104 | tf_op jit(solution)/shard_map/all_to_all | solution.py:228
  126.2 5.1 %all-to-all-start.2 = ((f32[16,16,256]{2,1,0:T(8,128)}), f32[16,16,256]{2,1,0:T(8,128)S(1)}, u32[]{:S(2)}, u32[]{:S(2)}) async-start(f32[16,16,256]{2,1,0:T(8,128)} %broadcast_in_dim.89), calls=%async_computation.2 | async-start | bytes 524288 | tf_op jit(solution)/shard_map/all_to_all | solution.py:228
  134.9 3.0 %collective-permute-start.26 = (bf16[256,256]{1,0:T(8,128)(2,1)S(1)}, bf16[256,256]{1,0:T(8,128)(2,1)S(1)}, u32[]{:S(2)}, u32[]{:S(2)}) collective-permute-start(bf16[256,256]{1,0:T(8,128)(2,1)S(1)} %get-tuple-element.101), channel_id=1, source_target_pairs={{32,0},{40,8},{48,16},{56,24},{64,32},{72,40},{80,48},{88,56},{96,... | collective-permute-start | bytes 393224 | tf_op jit(solution)/shard_map/ppermute | solution.py:143
  139.8 2.7 %collective-permute-start.33 = (bf16[256,256]{1,0:T(8,128)(2,1)S(1)}, bf16[256,256]{1,0:T(8,128)(2,1)S(1)}, u32[]{:S(2)}, u32[]{:S(2)}) collective-permute-start(bf16[256,256]{1,0:T(8,128)(2,1)S(1)} %get-tuple-element.103), channel_id=1, source_target_pairs={{8,0},{16,8},{24,16},{0,24},{40,32},{48,40},{56,48},{32,56},{72,64... | collective-permute-start | bytes 393224 | tf_op jit(solution)/shard_map/ppermute | solution.py:143
  144.9 2.4 %collective-permute-done.33 = bf16[256,256]{1,0:T(8,128)(2,1)S(1)} collective-permute-done((bf16[256,256]{1,0:T(8,128)(2,1)S(1)}, bf16[256,256]{1,0:T(8,128)(2,1)S(1)}, u32[]{:S(2)}, u32[]{:S(2)}) %collective-permute-start.33) | collective-permute-done | bytes 131104 | tf_op jit(solution)/shard_map/ppermute | solution.py:143
  147.2 2.3 %collective-permute-done.32 = bf16[256,256]{1,0:T(8,128)(2,1)S(1)} collective-permute-done((bf16[256,256]{1,0:T(8,128)(2,1)S(1)}, bf16[256,256]{1,0:T(8,128)(2,1)S(1)}, u32[]{:S(2)}, u32[]{:S(2)}) %collective-permute-start.32) | collective-permute-done | bytes 131104 | tf_op jit(solution)/shard_map/ppermute | solution.py:143
  (117 shorter events, 50.9 us)
Async XLA Ops:
  1.7 18.0 %collective-permute-start.8 = (bf16[256,256]{1,0:T(8,128)(2,1)S(1)}, bf16[256,256]{1,0:T(8,128)(2,1)S(1)}, u32[]{:S(2)}, u32[]{:S(2)}) collective-permute-start(bf16[256,256]{1,0:T(8,128)(2,1)S(1)} %get-tuple-element.108), channel_id=1, source_target_pairs={{96,0},{104,8},{112,16},{120,24},{0,32},{8,40},{16,48},{24,56},{32... | collective-permute-start | bytes 393224 | tf_op jit(solution)/shard_map/ppermute | solution.py:143
  3.8 16.7 %collective-permute-start.7 = (bf16[256,256]{1,0:T(8,128)(2,1)S(1)}, bf16[256,256]{1,0:T(8,128)(2,1)S(1)}, u32[]{:S(2)}, u32[]{:S(2)}) collective-permute-start(bf16[256,256]{1,0:T(8,128)(2,1)S(1)} %get-tuple-element.108), channel_id=1, source_target_pairs={{64,0},{72,8},{80,16},{88,24},{96,32},{104,40},{112,48},{120,56},{... | collective-permute-start | bytes 393224 | tf_op jit(solution)/shard_map/ppermute | solution.py:143
  17.2 24.7 %collective-permute-start.5 = (bf16[1024,256]{1,0:T(8,128)(2,1)S(1)}, bf16[1024,256]{1,0:T(8,128)(2,1)S(1)}, u32[]{:S(2)}, u32[]{:S(2)}) collective-permute-start(bf16[1024,256]{1,0:T(8,128)(2,1)S(1)} %constant_dynamic-update-slice_fusion.refs_0_), channel_id=1, source_target_pairs={{96,0},{104,8},{112,16},{120,24},{0,32},{8,40},{16,48},{24,56},{32... | collective-permute-start | bytes 1572872 | tf_op jit(solution)/shard_map/ppermute | solution.py:143
  17.3 24.6 %collective-permute-start.4 = (bf16[1024,256]{1,0:T(8,128)(2,1)S(1)}, bf16[1024,256]{1,0:T(8,128)(2,1)S(1)}, u32[]{:S(2)}, u32[]{:S(2)}) collective-permute-start(bf16[1024,256]{1,0:T(8,128)(2,1)S(1)} %constant_dynamic-update-slice_fusion.refs_0_), channel_id=1, source_target_pairs={{64,0},{72,8},{80,16},{88,24},{96,32},{104,40},{112,48},{120,56},{... | collective-permute-start | bytes 1572872 | tf_op jit(solution)/shard_map/ppermute | solution.py:143
  19.7 22.8 %collective-permute-start.3 = (bf16[1024,256]{1,0:T(8,128)(2,1)S(1)}, bf16[1024,256]{1,0:T(8,128)(2,1)}, u32[]{:S(2)}, u32[]{:S(2)}) collective-permute-start(bf16[1024,256]{1,0:T(8,128)(2,1)S(1)} %constant_dynamic-update-slice_fusion.refs_0_), channel_id=1, source_target_pairs={{32,0},{40,8},{48,16},{56,24},{64,32},{72,40},{80,48},{88,56},{96,... | collective-permute-start | bytes 1572872 | tf_op jit(solution)/shard_map/ppermute | solution.py:143
  20.5 13.1 %collective-permute-start.11 = (bf16[1024,256]{1,0:T(8,128)(2,1)S(1)}, bf16[1024,256]{1,0:T(8,128)(2,1)S(1)}, u32[]{:S(2)}, u32[]{:S(2)}) collective-permute-start(bf16[1024,256]{1,0:T(8,128)(2,1)S(1)} %pad_maximum_fusion.1.refs_4_), channel_id=1, source_target_pairs={{24,0},{0,8},{8,16},{16,24},{56,32},{32,40},{40,48},{48,56},{88,64... | collective-permute-start | bytes 1572872 | tf_op jit(solution)/shard_map/ppermute | solution.py:143
  21.9 12.5 %collective-permute-start.9 = (bf16[1024,256]{1,0:T(8,128)(2,1)S(1)}, bf16[1024,256]{1,0:T(8,128)(2,1)S(1)}, u32[]{:S(2)}, u32[]{:S(2)}) collective-permute-start(bf16[1024,256]{1,0:T(8,128)(2,1)S(1)} %pad_maximum_fusion.1.refs_4_), channel_id=1, source_target_pairs={{8,0},{16,8},{24,16},{0,24},{40,32},{48,40},{56,48},{32,56},{72,64... | collective-permute-start | bytes 1572872 | tf_op jit(solution)/shard_map/ppermute | solution.py:143
  51.4 11.7 %collective-permute-start.14 = (bf16[512,256]{1,0:T(8,128)(2,1)S(1)}, bf16[512,256]{1,0:T(8,128)(2,1)S(1)}, u32[]{:S(2)}, u32[]{:S(2)}) collective-permute-start(bf16[512,256]{1,0:T(8,128)(2,1)S(1)} %get-tuple-element.97), channel_id=1, source_target_pairs={{6,0},{7,1},{0,2},{1,3},{2,4},{3,5},{4,6},{5,7},{14,8},{15,9},{8,1... | collective-permute-start | bytes 786440 | tf_op jit(solution)/shard_map/ppermute | solution.py:143
  56.5 9.2 %collective-permute-start.16 = (bf16[512,256]{1,0:T(8,128)(2,1)S(1)}, bf16[512,256]{1,0:T(8,128)(2,1)S(1)}, u32[]{:S(2)}, u32[]{:S(2)}) collective-permute-start(bf16[512,256]{1,0:T(8,128)(2,1)S(1)} %get-tuple-element.98), channel_id=1, source_target_pairs={{2,0},{3,1},{4,2},{5,3},{6,4},{7,5},{0,6},{1,7},{10,8},{11,9},{12,... | collective-permute-start | bytes 786440 | tf_op jit(solution)/shard_map/ppermute | solution.py:143
  56.5 11.9 %collective-permute-start.15 = (bf16[512,256]{1,0:T(8,128)(2,1)S(1)}, bf16[512,256]{1,0:T(8,128)(2,1)S(1)}, u32[]{:S(2)}, u32[]{:S(2)}) collective-permute-start(bf16[512,256]{1,0:T(8,128)(2,1)S(1)} %get-tuple-element.99), channel_id=1, source_target_pairs={{4,0},{5,1},{6,2},{7,3},{0,4},{1,5},{2,6},{3,7},{12,8},{13,9},{14,... | collective-permute-start | bytes 786440 | tf_op jit(solution)/shard_map/ppermute | solution.py:143
  70.0 22.6 %collective-permute-start.19 = (bf16[512,256]{1,0:T(8,128)(2,1)S(1)}, bf16[512,256]{1,0:T(8,128)(2,1)S(1)}, u32[]{:S(2)}, u32[]{:S(2)}) collective-permute-start(bf16[512,256]{1,0:T(8,128)(2,1)S(1)} %convolution_convert_fusion.refs_0_), channel_id=1, source_target_pairs={{6,0},{7,1},{0,2},{1,3},{2,4},{3,5},{4,6},{5,7},{14,8},{15,9},{8,1... | collective-permute-start | bytes 786440 | tf_op jit(solution)/shard_map/ppermute | solution.py:143
  72.1 20.4 %collective-permute-start.18 = (bf16[512,256]{1,0:T(8,128)(2,1)S(1)}, bf16[512,256]{1,0:T(8,128)(2,1)S(1)}, u32[]{:S(2)}, u32[]{:S(2)}) collective-permute-start(bf16[512,256]{1,0:T(8,128)(2,1)S(1)} %convolution_convert_fusion.refs_0_), channel_id=1, source_target_pairs={{4,0},{5,1},{6,2},{7,3},{0,4},{1,5},{2,6},{3,7},{12,8},{13,9},{14,... | collective-permute-start | bytes 786440 | tf_op jit(solution)/shard_map/ppermute | solution.py:143
  75.9 16.6 %collective-permute-start.17 = (bf16[512,256]{1,0:T(8,128)(2,1)S(1)}, bf16[512,256]{1,0:T(8,128)(2,1)S(1)}, u32[]{:S(2)}, u32[]{:S(2)}) collective-permute-start(bf16[512,256]{1,0:T(8,128)(2,1)S(1)} %convolution_convert_fusion.refs_0_), channel_id=1, source_target_pairs={{2,0},{3,1},{4,2},{5,3},{6,4},{7,5},{0,6},{1,7},{10,8},{11,9},{12,... | collective-permute-start | bytes 786440 | tf_op jit(solution)/shard_map/ppermute | solution.py:143
  102.2 9.5 %collective-permute-start.27 = (bf16[512,256]{1,0:T(8,128)(2,1)S(1)}, bf16[512,256]{1,0:T(8,128)(2,1)S(1)}, u32[]{:S(2)}, u32[]{:S(2)}) collective-permute-start(bf16[512,256]{1,0:T(8,128)(2,1)S(1)} %get-tuple-element.74), channel_id=1, source_target_pairs={{96,0},{104,8},{112,16},{120,24},{0,32},{8,40},{16,48},{24,56},{32... | collective-permute-start | bytes 786440 | tf_op jit(solution)/shard_map/ppermute | solution.py:143
  102.6 10.1 %collective-permute-start.28 = (bf16[512,256]{1,0:T(8,128)(2,1)S(1)}, bf16[512,256]{1,0:T(8,128)(2,1)S(1)}, u32[]{:S(2)}, u32[]{:S(2)}) collective-permute-start(bf16[512,256]{1,0:T(8,128)(2,1)S(1)} %get-tuple-element.78), channel_id=1, source_target_pairs={{32,0},{40,8},{48,16},{56,24},{64,32},{72,40},{80,48},{88,56},{96,... | collective-permute-start | bytes 786440 | tf_op jit(solution)/shard_map/ppermute | solution.py:143
  105.5 25.7 %collective-permute-start.21 = (bf16[1024,256]{1,0:T(8,128)(2,1)}, bf16[1024,256]{1,0:T(8,128)(2,1)}, u32[]{:S(2)}, u32[]{:S(2)}) collective-permute-start(bf16[1024,256]{1,0:T(8,128)(2,1)} %get-tuple-element.69), channel_id=1, source_target_pairs={{24,0},{0,8},{8,16},{16,24},{56,32},{32,40},{40,48},{48,56},{88,64... | collective-permute-start | bytes 1572872 | tf_op jit(solution)/shard_map/ppermute | solution.py:143
  107.5 24.2 %collective-permute-start.22 = (bf16[1024,256]{1,0:T(8,128)(2,1)S(1)}, bf16[1024,256]{1,0:T(8,128)(2,1)}, u32[]{:S(2)}, u32[]{:S(2)}) collective-permute-start(bf16[1024,256]{1,0:T(8,128)(2,1)S(1)} %get-tuple-element.70), channel_id=1, source_target_pairs={{16,0},{24,8},{0,16},{8,24},{48,32},{56,40},{32,48},{40,56},{80,64... | collective-permute-start | bytes 1572872 | tf_op jit(solution)/shard_map/ppermute | solution.py:143
  108.4 24.6 %collective-permute-start.23 = (bf16[1024,256]{1,0:T(8,128)(2,1)S(1)}, bf16[1024,256]{1,0:T(8,128)(2,1)}, u32[]{:S(2)}, u32[]{:S(2)}) collective-permute-start(bf16[1024,256]{1,0:T(8,128)(2,1)S(1)} %get-tuple-element.71), channel_id=1, source_target_pairs={{8,0},{16,8},{24,16},{0,24},{40,32},{48,40},{56,48},{32,56},{72,64... | collective-permute-start | bytes 1572872 | tf_op jit(solution)/shard_map/ppermute | solution.py:143
  114.3 11.1 %all-to-all-start.1 = ((f32[8,16,256]{2,1,0:T(8,128)}), f32[8,16,256]{2,1,0:T(8,128)S(1)}, u32[]{:S(2)}, u32[]{:S(2)}) async-start(f32[8,16,256]{2,1,0:T(8,128)} %broadcast_in_dim.88), calls=%async_computation.1 | async-start | bytes 262144 | tf_op jit(solution)/shard_map/all_to_all | solution.py:228
  119.3 19.1 %collective-permute-start.29 = (bf16[1024,256]{1,0:T(8,128)(2,1)}, bf16[1024,256]{1,0:T(8,128)(2,1)}, u32[]{:S(2)}, u32[]{:S(2)}) collective-permute-start(bf16[1024,256]{1,0:T(8,128)(2,1)} %pad_maximum_fusion.2), channel_id=1, source_target_pairs={{96,0},{104,8},{112,16},{120,24},{0,32},{8,40},{16,48},{24,56},{32... | collective-permute-start | bytes 1572872 | tf_op jit(solution)/shard_map/ppermute | solution.py:143
  120.4 18.0 %collective-permute-start.30 = (bf16[1024,256]{1,0:T(8,128)(2,1)}, bf16[1024,256]{1,0:T(8,128)(2,1)}, u32[]{:S(2)}, u32[]{:S(2)}) collective-permute-start(bf16[1024,256]{1,0:T(8,128)(2,1)} %pad_maximum_fusion.3), channel_id=1, source_target_pairs={{32,0},{40,8},{48,16},{56,24},{64,32},{72,40},{80,48},{88,56},{96,... | collective-permute-start | bytes 1572872 | tf_op jit(solution)/shard_map/ppermute | solution.py:143
  126.2 18.7 %all-to-all-start.2 = ((f32[16,16,256]{2,1,0:T(8,128)}), f32[16,16,256]{2,1,0:T(8,128)S(1)}, u32[]{:S(2)}, u32[]{:S(2)}) async-start(f32[16,16,256]{2,1,0:T(8,128)} %broadcast_in_dim.89), calls=%async_computation.2 | async-start | bytes 524288 | tf_op jit(solution)/shard_map/all_to_all | solution.py:228
  134.6 10.1 %collective-permute-start.24 = (bf16[256,256]{1,0:T(8,128)(2,1)S(1)}, bf16[256,256]{1,0:T(8,128)(2,1)S(1)}, u32[]{:S(2)}, u32[]{:S(2)}) collective-permute-start(bf16[256,256]{1,0:T(8,128)(2,1)S(1)} %get-tuple-element.100), channel_id=1, source_target_pairs={{96,0},{104,8},{112,16},{120,24},{0,32},{8,40},{16,48},{24,56},{32... | collective-permute-start | bytes 393224 | tf_op jit(solution)/shard_map/ppermute | solution.py:143
  134.9 9.9 %collective-permute-start.26 = (bf16[256,256]{1,0:T(8,128)(2,1)S(1)}, bf16[256,256]{1,0:T(8,128)(2,1)S(1)}, u32[]{:S(2)}, u32[]{:S(2)}) collective-permute-start(bf16[256,256]{1,0:T(8,128)(2,1)S(1)} %get-tuple-element.101), channel_id=1, source_target_pairs={{32,0},{40,8},{48,16},{56,24},{64,32},{72,40},{80,48},{88,56},{96,... | collective-permute-start | bytes 393224 | tf_op jit(solution)/shard_map/ppermute | solution.py:143
  (19 other events, 263.3 us)
